TPU v7x, 128 devices: a whole 4x4x4 slice. The times are simulated.
128 devices in a mesh: pb: 4 (over x), pa: 32 (over z, y, core).
Axes of the slice: x: 4, y: 4, z: 4, core: 2. Of those that a mesh axis runs over, the one named last changes fastest.
Arguments:
- queries: bfloat16 [512, 32, 128], P('pb'), may hold values from -30 to 30
- passages: bfloat16 [256, 180, 128], P('pa'), may hold values from -1.8 to 1.8
- pair_mask: int32 [64, 32], P('pb', 'pa'), may hold values from 0 to 1, as said below
- positive: int32 [512], P('pb'), may hold values from 0 to 255, as said below
Outputs:
- loss: float32 [512], P(('pb', 'pa'))
- grad_queries: float32 [512, 32, 128], P(('pb', 'pa'))
- grad_passages: float32 [256, 180, 128], P('pa')
Inputs may be any that keep to these rules, and one draw needn't show every extreme that they name: `pair_mask`: every query block is paired with the block of each of its queries' positives. The positive of a query lies in a passage block paired with the query's block.
All inputs are finite; a program needn't handle non-finite values.
Results may differ from a plain program's by a relative error of at most 0.0029.
Values may be sent and summed in bfloat16 or wider, within the bound.
No kernel may reach another device: no remote copies, remote signals or barrier semaphores. Data moves between devices by JAX's collectives and lax.ppermute only.
A program may use at most 128 MiB of HBM per device.

v0:
```python
import jax
import jax.numpy as jnp
from jax import lax
from jax.sharding import PartitionSpec as P

very_low = -1e30
contrast_temp = 0.05


def merged(part, axis, combine):
    gathered = jax.tree.map(lambda a: lax.all_gather(a, axis), part)

    def take(source):
        return jax.tree.map(lambda a: lax.dynamic_index_in_dim(a, source, 0, False), gathered)

    return lax.fori_loop(
        1, lax.axis_size(axis), lambda source, state: combine(state, take(source)), take(0)
    )


def block_sim(query_block, passage_block):
    return lax.dot_general(
        query_block, passage_block, (((1,), (1,)), ((), ())), preferred_element_type=jnp.float32
    )


def token_stats(similar, query_count, q_tokens, item_count, p_tokens):
    shaped = similar.reshape(query_count, q_tokens, item_count, p_tokens)
    row_top = jnp.max(shaped, axis=3, keepdims=True)
    scaled = jnp.exp(shaped - row_top)
    tok_total = jnp.sum(scaled, axis=3, keepdims=True)
    return (row_top, scaled, tok_total)


def combine_totals(first, second):
    top_a, total_a, pos_a = first
    top_b, total_b, pos_b = second
    joint = jnp.maximum(top_a, top_b)
    return (
        joint,
        total_a * jnp.exp(top_a - joint) + total_b * jnp.exp(top_b - joint),
        pos_a + pos_b,
    )


def on_device(queries, passages, pair_mask, positive):
    query_rows, q_tokens, feature = queries.shape
    item_count, p_tokens = (passages.shape[0], passages.shape[1])
    block_count = query_rows // item_count
    query_flat = queries.reshape(query_rows * q_tokens, feature)
    passage_flat = passages.reshape(item_count * p_tokens, feature)
    my_column = pair_mask[:, 0]
    my_index = lax.axis_index("pa")
    stacked = passage_flat[None]
    side_blocks = jnp.reshape(my_index, (1,))
    task_order = jnp.argsort(1 - my_column, stable=True)
    first_task = jnp.int32(0)
    finish = jnp.sum(my_column)
    side_count = stacked.shape[0]

    def decode(task):
        task_slot = task_order[task]
        which_side = task_slot // block_count
        kblock = task_slot % block_count
        query_block = lax.dynamic_slice_in_dim(
            query_flat, kblock * item_count * q_tokens, item_count * q_tokens, 0
        )
        passage_block = lax.dynamic_index_in_dim(stacked, which_side, 0, keepdims=False)
        return (which_side, kblock, query_block, passage_block)

    def forward(task, scores):
        which_side, kblock, query_block, passage_block = decode(task)
        row_top, scaled, tok_total = token_stats(
            block_sim(query_block, passage_block), item_count, q_tokens, item_count, p_tokens
        )
        score_block = jnp.mean(row_top[..., 0] + jnp.log(tok_total[..., 0]), axis=1)
        return lax.dynamic_update_slice(
            scores, score_block[None], (which_side, kblock * item_count, jnp.int32(0))
        )

    scores = jnp.full((side_count, query_rows, item_count), very_low, jnp.float32)
    scores = lax.fori_loop(first_task, finish, forward, scores)
    active = scores > very_low / 2
    logits = jnp.where(active, scores / contrast_temp, very_low)
    local_top = jnp.max(logits, axis=(0, 2))
    local_total = jnp.sum(
        jnp.where(active, jnp.exp(logits - local_top[None, :, None]), 0.0), axis=(0, 2)
    )
    pos_block = positive // item_count
    pos_item = positive % item_count
    onehot = (
        (side_blocks[:, None, None] == pos_block[None, :, None])
        & (jnp.arange(item_count, dtype=jnp.int32)[None, None, :] == pos_item[None, :, None])
        & active
    )
    local_pos = jnp.sum(jnp.where(onehot, logits, 0.0), axis=(0, 2))
    glob_top, glob_total, glob_pos = merged(
        (local_top, local_total, local_pos), "pa", combine_totals
    )
    own_rows = query_rows // lax.axis_size("pa")
    loss_all = glob_top + jnp.log(glob_total) - glob_pos
    loss_rows = lax.dynamic_slice_in_dim(loss_all, my_index * own_rows, own_rows, 0)
    probs = jnp.where(
        active, jnp.exp(logits - glob_top[None, :, None]) / glob_total[None, :, None], 0.0
    )
    coef = (probs - onehot.astype(jnp.float32)) / (contrast_temp * q_tokens)

    def backward(task, carry):
        grad_q, grad_p = carry
        which_side, kblock, query_block, passage_block = decode(task)
        row_top, scaled, tok_total = token_stats(
            block_sim(query_block, passage_block), item_count, q_tokens, item_count, p_tokens
        )
        coef_block = lax.dynamic_slice(
            coef, (which_side, kblock * item_count, jnp.int32(0)), (1, item_count, item_count)
        )[0]
        dsim = (coef_block[:, None, :, None] * (scaled / tok_total)).astype(jnp.bfloat16)
        dsim = dsim.reshape(item_count * q_tokens, item_count * p_tokens)
        q_start = kblock * item_count * q_tokens
        q_part = lax.dynamic_slice_in_dim(grad_q, q_start, item_count * q_tokens, 0)
        q_part = q_part + jnp.dot(dsim, passage_block, preferred_element_type=jnp.float32)
        grad_q = lax.dynamic_update_slice_in_dim(grad_q, q_part, q_start, 0)
        p_part = lax.dot_general(
            dsim, query_block, (((0,), (0,)), ((), ())), preferred_element_type=jnp.float32
        )
        grad_p = grad_p.at[which_side].add(p_part)
        return (grad_q, grad_p)

    grad_q = jnp.zeros((query_rows * q_tokens, feature), jnp.float32)
    grad_p = jnp.zeros((side_count, item_count * p_tokens, feature), jnp.float32)
    grad_q, grad_p = lax.fori_loop(first_task, finish, backward, (grad_q, grad_p))
    my_grad_p = grad_p[0]
    passage_grad = lax.psum(my_grad_p, "pb").reshape(item_count, p_tokens, feature)
    grad_terms = grad_q.reshape(query_rows, q_tokens * feature)
    query_grad = lax.psum_scatter(grad_terms, "pa", scatter_dimension=0, tiled=True).reshape(
        own_rows, q_tokens, feature
    )
    return (loss_rows, query_grad, passage_grad)


def solution(mesh):
    placed = (P("pb", None, None), P("pa", None, None), P("pb", "pa"), P("pb"))
    return jax.shard_map(
        on_device,
        mesh=mesh,
        in_specs=placed,
        out_specs=(P(("pb", "pa")), P(("pb", "pa"), None, None), P("pa", None, None)),
        check_vma=False,
    )
```

profile of v0, /device:TPU:0, one launch (start us, length us, event | category | flops | bytes accessed | tf_op | source)
XLA Modules:
  0.0 560.9 jit_solution(5425854097856273700)
XLA Ops:
  12.3 74.0 %while.46 = (s32[]{:T(128)}, f32[1,128,8]{2,1,0:T(8,128)S(1)}, s32[]{:T(128)}, s32[16]{0:T(128)S(1)}, bf16[4096,128]{1,0:T(8,128)(2,1)}, /*index=5*/bf16[1,1440,...) while((s32[]{:T(128)}, f32[1,128,8]{2,1,0:T(8,128)S(1)}, ...), condition=%wide.region_6.7_spmd, body=%wide.region_2.6_spmd.sunk | while | flops 95477784 | bytes 4301452 | solution.py:82
  86.7 38.7 %all-gather.4 = f32[32,1,128]{2,1,0:T(1,128)S(1)} all-gather(f32[1,1,128]{2,1,0:T(1,128)S(1)} %bitcast.115), channel_id=3, replica_groups=mesh['pb'=4,'pa'=32] {'pa'}, dimensions={0}, use_global_device_ids=true | all-gather | bytes 16896 | tf_op jit(solution)/shard_map/all_gather | solution.py:11
  125.4 19.0 %all-gather.5 = f32[32,1,128]{2,1,0:T(1,128)S(1)} all-gather(f32[1,1,128]{2,1,0:T(1,128)S(1)} %bitcast.114), channel_id=4, replica_groups=mesh['pb'=4,'pa'=32] {'pa'}, dimensions={0}, use_global_device_ids=true | all-gather | bytes 16896 | tf_op jit(solution)/shard_map/all_gather | solution.py:11
  144.4 20.9 %all-gather.3 = f32[32,1,128]{2,1,0:T(1,128)S(1)} all-gather(f32[1,1,128]{2,1,0:T(1,128)S(1)} %bitcast.113), channel_id=2, replica_groups=mesh['pb'=4,'pa'=32] {'pa'}, dimensions={0}, use_global_device_ids=true | all-gather | bytes 16896 | tf_op jit(solution)/shard_map/all_gather | solution.py:11
  168.4 186.3 %while.48 = (s32[]{:T(128)}, f32[4096,128]{1,0:T(8,128)}, f32[1,1440,128]{2,1,0:T(8,128)S(1)}, s32[]{:T(128)}, s32[16]{0:T(128)S(1)}, /*index=5*/f32[1,128,8]{2,...) while((s32[]{:T(128)}, f32[4096,128]{1,0:T(8,128)}, ...), condition=%wide.region_16.17_spmd, body=%wide.region_12.16_spmd.sunk | while | flops 284995968 | bytes 8635698 | solution.py:131
  173.9 2.5 multiply_convert_fusion.2
  176.4 1.9 copy.20
  180.8 1.9 fusion.55
  188.2 2.5 multiply_convert_fusion.2
  190.7 1.9 copy.20
  195.1 1.9 fusion.55
  202.5 2.5 multiply_convert_fusion.2
  205.0 1.9 copy.20
  209.4 1.9 fusion.55
  216.8 2.5 multiply_convert_fusion.2
  219.2 1.9 copy.20
  223.6 1.9 fusion.55
  231.1 2.5 multiply_convert_fusion.2
  233.5 1.9 copy.20
  237.9 1.9 fusion.55
  245.3 2.5 multiply_convert_fusion.2
  247.8 1.9 copy.20
  252.2 1.9 fusion.55
  259.6 2.5 multiply_convert_fusion.2
  262.1 1.9 copy.20
  266.5 1.9 fusion.55
  273.9 2.5 multiply_convert_fusion.2
  276.4 1.9 copy.20
  280.8 1.9 fusion.55
  288.2 2.5 multiply_convert_fusion.2
  290.6 1.9 copy.20
  295.0 1.9 fusion.55
  302.5 2.5 multiply_convert_fusion.2
  304.9 1.9 copy.20
  309.3 1.9 fusion.55
  316.7 2.5 multiply_convert_fusion.2
  319.2 1.9 copy.20
  323.6 1.9 fusion.55
  331.0 2.5 multiply_convert_fusion.2
  333.5 1.9 copy.20
  337.9 1.9 fusion.55
  345.3 2.5 multiply_convert_fusion.2
  347.8 1.9 copy.20
  352.2 1.9 fusion.55
  356.6 1.5 reshape.172
  360.6 80.2 %all-reduce.4.cloned.1.call-done = f32[8,180,128]{2,1,0:T(8,128)} async-done(((f32[8,180,128]{2,1,0:T(8,128)}), f32[8,180,128]{2,1,0:T(8,128)}) %all-reduce.4.cloned.1.call-update) | async-done | bytes 737296 | tf_op jit(solution)/shard_map/psum | solution.py:133
  440.8 2.1 copy.13
  442.9 109.6 %all-reduce.6.cloned.1.call-done = f32[128,4096]{1,0:T(8,128)} async-done(((f32[128,4096]{1,0:T(8,128)}), f32[128,4096]{1,0:T(8,128)}) %all-reduce.6.cloned.1.call-update) | async-done | bytes 2097168
  (244 shorter events, 113.4 us)
Async XLA Ops:
  7.2 433.6 %all-reduce.4.cloned.1.call-start = ((), (), s32[]{:S(2)}) async-start(), calls=%async_computation | async-start | bytes 1507328 | tf_op jit(solution)/shard_map/psum | solution.py:133
  354.8 1.9 copy-start
  355.7 196.7 %all-reduce.6.cloned.1.call-start = ((), (), s32[]{:S(2)}) async-start(), calls=%async_computation.1 | async-start | bytes 4194304
  358.1 0.7 copy-start.1
Sparse Core Ops, SparseCore 0:
  355.9 84.8 all-reduce.3
  444.0 108.3 all-reduce.5
where the time goes:
time: 566 us; the launch traced here: 561 us
  waiting for transfers between devices  190 us (34%)
  local copies, waits for them, and re-layouts  93.6 us (17%)
  loops' own time  80.9 us (14%)
  matrix products  78.7 us (14%)
  blocking collectives  78.6 us (14%)
  other arithmetic  24.3 us (4%)
  between operations  14.8 us (3%)
    unnamed x3, waiting for transfers between devices  110 us
    psum x1, waiting for transfers between devices, on_device(): lax.psum(my_grad_p, 'pb').reshape(item_count, p_tokens, feature)  80.2 us
    all_gather x3, blocking collectives, merged(): gathered = jax.tree.map(lambda a: lax.all_gather(a, axis), part)  78.6 us
    another operation x1, loops' own time, on_device(): lax.fori_loop(first_task, finish, backward, (grad_q, grad_p))  43.5 us
    another operation x1, loops' own time, on_device(): scores = lax.fori_loop(first_task, finish, forward, scores)  36.8 us
    div x13, matrix products, backward(): scaled / tok_total  32.1 us
    dot_general x13, matrix products, backward(): jnp.dot(dsim, passage_block, preferred_element_type=jnp.float32)  25.1 us
    convert_element_type x13, local copies, waits for them, and re-layouts, backward(): (coef_block[:, None, :, None] * (scaled / tok_total)).astype(jnp.bfloat16)  24.1 us
  transfers between devices with their start and end apart: 2, of which 2 were waited for; matrix products, arithmetic and copies ran while one was open for 1% of the time, Pallas kernels for 0%

commit v1 on v0

v1 whole, which is shorter than its diff:
```python
import jax
import jax.numpy as jnp
from jax import lax
from jax.experimental import pallas as pl
from jax.experimental.pallas import tpu as pltpu
from jax.sharding import PartitionSpec as P

very_low = -1e30
contrast_temp = 0.05
f32, bf16 = jnp.float32, jnp.bfloat16
VMEM = pl.BlockSpec(memory_space=pltpu.VMEM)
SMEM = pl.BlockSpec(memory_space=pltpu.SMEM)
B, LQ, LP, D = 8, 32, 180, 128
LPP = 192
MAIN = 176
QT = B * LQ


def iota(shape, dim):
    return lax.broadcasted_iota(jnp.int32, shape, dim)


def exact_dot(a, b):
    return jnp.dot(a, b, precision=lax.Precision.HIGHEST, preferred_element_type=f32)


def expand(row, blocks):
    count = blocks * B
    own = iota((blocks, count), 1) // B == iota((blocks, count), 0)
    pick = (iota((count, QT), 0) % B == iota((count, QT), 1) // LQ).astype(f32)
    return exact_dot(jnp.where(own, row, 0.0), pick)


def squeeze(wide, blocks):
    count = blocks * B
    pick = (iota((QT, count), 0) == LQ * (iota((QT, count), 1) % B)).astype(f32)
    own = iota((blocks, count), 1) // B == iota((blocks, count), 0)
    return jnp.sum(jnp.where(own, exact_dot(wide, pick), 0.0), axis=0, keepdims=True)


def pad_passages(p_ref, pad_ref):
    for p in range(B):
        padded = jnp.concatenate([p_ref[p].astype(f32), jnp.zeros((LPP - LP, D), f32)], axis=0)
        pad_ref[p] = padded.astype(bf16)


def passage_sim(pad_ref, p, qk):
    sim = lax.dot_general(pad_ref[p], qk, (((1,), (1,)), ((), ())), preferred_element_type=f32)
    tail = jnp.where(iota((LPP - MAIN, QT), 0) < LP - MAIN, sim[MAIN:], very_low)
    return sim[:MAIN], tail


def is_positive(pos_ref, active, blocks):
    pos = expand(pos_ref[...].astype(f32), blocks).astype(jnp.int32)
    item = iota((blocks, B, QT), 1) + lax.axis_index("pa") * B
    return (pos[:, None, :] == item) & active


def scores_kernel(mask_s, mask_v, pos_ref, q_ref, p_ref, send_ref, logit_ref, top_ref, tot_ref, pad_ref):
    blocks = mask_s.shape[0]
    pad_passages(p_ref, pad_ref)
    top_ref[...] = jnp.zeros_like(top_ref)
    tot_ref[...] = jnp.ones_like(tot_ref)

    @pl.loop(0, blocks)
    def _(k):
        @pl.when(mask_s[k, 0] > 0)
        def _():
            qk = q_ref[pl.ds(pl.multiple_of(k * QT, QT), QT), :]
            for p in range(B):
                main, tail = passage_sim(pad_ref, p, qk)
                top = jnp.maximum(
                    jnp.max(main, axis=0, keepdims=True), jnp.max(tail, axis=0, keepdims=True)
                )
                top_ref[k, p : p + 1] = top
                tot_ref[k, p : p + 1] = jnp.sum(
                    jnp.exp(main - top), axis=0, keepdims=True
                ) + jnp.sum(jnp.exp(tail - top), axis=0, keepdims=True)

    active = mask_v[...].reshape(blocks, 1, 1) > 0
    token_lse = (top_ref[...] + jnp.log(tot_ref[...])).reshape(blocks * B, QT)
    same = (iota((QT, QT), 0) // LQ == iota((QT, QT), 1) // LQ).astype(f32)
    score = (exact_dot(token_lse, same) / LQ).reshape(blocks, B, QT)
    logit = jnp.where(active, score / contrast_temp, very_low)
    logit_ref[...] = logit
    local_top = jnp.max(logit, axis=1, keepdims=True)
    local_total = jnp.sum(jnp.where(active, jnp.exp(logit - local_top), 0.0), axis=1)
    local_pos = jnp.sum(jnp.where(is_positive(pos_ref, active, blocks), logit, 0.0), axis=1)
    rows = [squeeze(x, blocks) for x in (local_top[:, 0, :], local_total, local_pos)]
    rows.append(jnp.zeros((5, blocks * B), f32))
    send_ref[...] = jnp.broadcast_to(jnp.concatenate(rows, axis=0)[None], send_ref.shape)


def grads_kernel(
    mask_s, mask_v, pos_ref, q_ref, p_ref, stat_ref, logit_ref, top_ref, tot_ref,
    loss_ref, gq_ref, own_ref, send1_ref, send2_ref, send3_ref,
    pad_ref, turn_ref, weight_ref, gp_ref,
):
    blocks = mask_s.shape[0]
    pad_passages(p_ref, pad_ref)
    for p in range(B):
        turn_ref[p] = pad_ref[p].astype(f32).T.astype(bf16)
    tops = stat_ref[:, 0, :]
    glob_top = jnp.max(tops, axis=0, keepdims=True)
    glob_total = jnp.sum(stat_ref[:, 1, :] * jnp.exp(tops - glob_top), axis=0, keepdims=True)
    glob_pos = jnp.sum(stat_ref[:, 2, :], axis=0, keepdims=True)
    loss_ref[...] = glob_top + jnp.log(glob_total) - glob_pos
    active = mask_v[...].reshape(blocks, 1, 1) > 0
    wide_top = expand(glob_top, blocks)[:, None, :]
    wide_total = expand(glob_total, blocks)[:, None, :]
    prob = jnp.where(active, jnp.exp(logit_ref[...] - wide_top) / wide_total, 0.0)
    onehot = is_positive(pos_ref, active, blocks).astype(f32)
    weight_ref[...] = (prob - onehot) / (contrast_temp * LQ) / tot_ref[...]
    gp_ref[...] = jnp.zeros_like(gp_ref)

    @pl.loop(0, blocks)
    def _(k):
        @pl.when(mask_s[k, 0] > 0)
        def _():
            qk = q_ref[pl.ds(pl.multiple_of(k * QT, QT), QT), :]
            turned = jnp.zeros((D, QT), f32)
            for p in range(B):
                main, tail = passage_sim(pad_ref, p, qk)
                top = top_ref[k, p : p + 1]
                weight = weight_ref[k, p : p + 1]
                dsim = jnp.concatenate(
                    [
                        (jnp.exp(main - top) * weight).astype(bf16),
                        (jnp.exp(tail - top) * weight).astype(bf16),
                    ],
                    axis=0,
                )
                gp_ref[p] += jnp.dot(dsim, qk, preferred_element_type=f32)
                turned += jnp.dot(turn_ref[p], dsim, preferred_element_type=f32)
            part = turned.T.astype(bf16)
            gq_ref[2 * k] = part[: QT // 2]
            gq_ref[2 * k + 1] = part[QT // 2 :]

        @pl.when(mask_s[k, 0] <= 0)
        def _():
            gq_ref[2 * k] = jnp.zeros((QT // 2, D), bf16)
            gq_ref[2 * k + 1] = jnp.zeros((QT // 2, D), bf16)

    mine = lax.axis_index("pb")
    for t in range(2):
        own_ref[t] = gp_ref[2 * mine + t]
        for s, send in ((1, send1_ref), (2, send2_ref), (3, send3_ref)):
            send[t] = gp_ref[2 * lax.rem(mine + s, 4) + t].astype(bf16)


def sum_kernel(own_ref, a_ref, b_ref, c_ref, out_ref):
    total = own_ref[...] + a_ref[...].astype(f32) + b_ref[...].astype(f32) + c_ref[...].astype(f32)
    out_ref[...] = total.astype(bf16)


def place_kernel(own_ref, a_ref, b_ref, c_ref, out_ref):
    mine = lax.axis_index("pb")
    for s, ref in ((0, own_ref), (1, a_ref), (2, b_ref), (3, c_ref)):
        owner = lax.rem(mine + 4 - s, 4)
        for t in range(2):
            out_ref[2 * owner + t] = ref[t].astype(f32)[:LP]


def rows_kernel(in_ref, out_ref):
    total = in_ref[0].astype(f32)
    for i in range(1, in_ref.shape[0]):
        total += in_ref[i].astype(f32)
    out_ref[...] = total


def call(kernel, out, n_in, smem_first=False, scratch=(), vmem=48 << 20):
    return pl.pallas_call(
        kernel,
        out_shape=out,
        in_specs=[SMEM if smem_first and i == 0 else VMEM for i in range(n_in)],
        out_specs=jax.tree.map(lambda _: VMEM, out),
        scratch_shapes=list(scratch),
        compiler_params=pltpu.CompilerParams(vmem_limit_bytes=vmem),
    )


def turn(x, s):
    return lax.ppermute(x, "pb", [(i, (i + s) % 4) for i in range(4)])


def on_device(queries, passages, pair_mask, positive):
    rows = queries.shape[0]
    blocks = rows // B
    peers = lax.axis_size("pa")
    shape = jax.ShapeDtypeStruct
    flat = queries.reshape(rows * LQ, D)
    pos = positive.reshape(1, rows)
    wide = shape((blocks, B, QT), f32)
    pad = pltpu.VMEM((B, LPP, D), bf16)
    send, logit, top, tot = call(
        scores_kernel, (shape((peers, 8, rows), f32), wide, wide, wide), 5, True, [pad]
    )(pair_mask, pair_mask, pos, flat, passages)
    stats = lax.all_to_all(send, "pa", 0, 0, tiled=True)
    piece = shape((2, LPP, D), bf16)
    loss, gq, own, send1, send2, send3 = call(
        grads_kernel,
        (shape((1, rows), f32), shape((peers, 4 * LQ, D), bf16), shape((2, LPP, D), f32), piece, piece, piece),
        9,
        True,
        [pad, pltpu.VMEM((B, D, LPP), bf16), pltpu.VMEM((blocks, B, QT), f32), pltpu.VMEM((B, LPP, D), f32)],
    )(pair_mask, pair_mask, pos, flat, passages, stats, logit, top, tot)
    got = [turn(x, s) for x, s in ((send1, 1), (send2, 2), (send3, 3))]
    gq_terms = lax.all_to_all(gq, "pa", 0, 0, tiled=True)
    mine = call(sum_kernel, piece, 4)(own, *got)
    others = [turn(mine, s) for s in (1, 2, 3)]
    grad_p = call(place_kernel, shape((B, LP, D), f32), 4)(mine, *others)
    grad_q = call(rows_kernel, shape((4 * LQ, D), f32), 1)(gq_terms).reshape(4, LQ, D)
    loss_rows = lax.dynamic_slice_in_dim(loss[0], lax.axis_index("pa") * 4, 4, 0)
    return loss_rows, grad_q, grad_p


def solution(mesh):
    placed = (P("pb", None, None), P("pa", None, None), P("pb", "pa"), P("pb"))
    return jax.shard_map(
        on_device,
        mesh=mesh,
        in_specs=placed,
        out_specs=(P(("pb", "pa")), P(("pb", "pa"), None, None), P("pa", None, None)),
        check_vma=False,
    )
```

time: 566 us -> 83.9 us (0.15)
  waiting for transfers between devices: 190 us -> 8.58 us
  local copies, waits for them, and re-layouts: 93.6 us -> 5.22 us
  loops' own time: 80.9 us -> 0 us
  matrix products: 78.7 us -> 0 us
  blocking collectives: 78.6 us -> 23.5 us
  starting transfers between devices: 0.08 us -> 36.1 us
  other arithmetic: 24.3 us -> 0 us
  between operations: 14.8 us -> 0.68 us
  Pallas kernels: 0 us -> 9.48 us
    unnamed x3 -> x0, waiting for transfers between devices: 110 us -> none
    another operation x3 -> x0, loops' own time: 80.9 us -> none  [the longest x1 43.5 us: on_device(): lax.fori_loop(first_task, finish, backward, (grad_q, grad_p))]
    psum x1 -> x0, waiting for transfers between devices: 80.2 us -> none  [on_device(): lax.psum(my_grad_p, 'pb').reshape(item_count, p_tokens, feature)]
    all_gather x3 -> x0, blocking collectives: 78.6 us -> none  [merged(): gathered = jax.tree.map(lambda a: lax.all_gather(a, axis), part)]
    dot_general x39 -> x0, matrix products: 46.7 us -> none  [the longest x13 25.1 us: backward(): jnp.dot(dsim, passage_block, preferred_element_type=jnp.float32)]
    dynamic_slice x56 -> x1, local copies, waits for them, and re-layouts: 38.9 us -> 0.58 us  [on_device(): lax.dynamic_slice_in_dim(loss[0], lax.axis_index('pa') * 4, 4, 0)]
    div x13 -> x0, matrix products: 32.1 us -> none  [backward(): scaled / tok_total]
    all_to_all x0 -> x1, starting transfers between devices: none -> 25.7 us  [on_device(): gq_terms = lax.all_to_all(gq, 'pa', 0, 0, tiled=True)]
  transfers between devices with their start and end apart: 2 -> 7, of which waited for: 2 -> 6; matrix products, arithmetic and copies ran while one was open for 1% -> 2% of each run, Pallas kernels for 0% -> 0%
where the time goes in v1:
time: 83.9 us; the launch traced here: 83.5 us
  starting transfers between devices  36.1 us (43%)
  blocking collectives  23.5 us (28%)
  Pallas kernels  9.48 us (11%)
  waiting for transfers between devices  8.58 us (10%)
  local copies, waits for them, and re-layouts  5.22 us (6%)
    all_to_all x1, starting transfers between devices, on_device(): gq_terms = lax.all_to_all(gq, 'pa', 0, 0, tiled=True)  25.7 us
    all_to_all x1, blocking collectives, on_device(): stats = lax.all_to_all(send, 'pa', 0, 0, tiled=True)  23.5 us
    ppermute x6, starting transfers between devices, turn(): return lax.ppermute(x, 'pb', [(i, (i + s) % 4) for i in range(4)])  10.3 us
    ppermute x6, waiting for transfers between devices, turn(): return lax.ppermute(x, 'pb', [(i, (i + s) % 4) for i in range(4)])  8.57 us
    pallas_call x1, Pallas kernels, on_device(): call(grads_kernel, (shape((1, rows), f32), shape((peers, 4 * LQ, D), bf16...  5.71 us
    unnamed x7, local copies, waits for them, and re-layouts  4.64 us
    pallas_call x1, Pallas kernels, on_device(): call(scores_kernel, (shape((peers, 8, rows), f32), wide, wide, wide), 5,...  2.88 us
  transfers between devices with their start and end apart: 7, of which 6 were waited for; matrix products, arithmetic and copies ran while one was open for 2% of the time, Pallas kernels for 0%

profile of v1, /device:TPU:0, one launch (start us, length us, event | category | flops | bytes accessed | tf_op | source)
XLA Modules:
  0.0 83.5 jit_solution(1076153118170660698)
XLA Ops:
  0.6 0.7 copy.10.mask_s.mask_v
  1.4 1.0 %copy.12.p_ref = bf16[8,180,128]{2,1,0:T(8,128)(2,1)S(1)} copy(bf16[8,180,128]{2,0,1:T(8,128)(2,1)} %param.5) | data formatting | bytes 737280 | tf_op args[1]
  2.4 0.0 copy-start.1
  2.4 0.6 copy-done.1
  3.1 0.0 copy-start
  3.1 1.2 %copy-done = bf16[128,32,128]{2,1,0:T(8,128)(2,1)S(1)} copy-done((bf16[128,32,128]{2,1,0:T(8,128)(2,1)S(1)}, bf16[128,32,128]{2,1,0:T(8,128)(2,1)}, u32[]{:S(2)}) %copy-start) | copy-done | bytes 1048600
  4.3 2.9 %shard_map.67 = (f32[32,8,128]{2,1,0:T(8,128)S(1)}, f32[16,8,256]{2,1,0:T(8,128)S(1)}, f32[16,8,256]{2,1,0:T(8,128)S(1)}, f32[16,8,256]{2,1,0:T(8,128)S(1)}) custom-call(s32[16,1]{1,0:T(8,128)S(1)} %copy.10.mask_s.mask_v, s32[16,1]{1,0:T(8,128)S(1)} %copy.10.mask_s.mask_v, s32[1,128]{1,0:T(1,128)S(1)} %bitcast.7, bf16[4096,128]{1,0:T(8,128)(2,1)S(1)} %bitcast.5, ...), custom_call_target="tpu_custom_call" | custom-call | tf_op jit(solution)/shard_map/pallas_call | solution.py:195
  7.2 23.5 %all_to_all.10.stat_ref = f32[32,8,128]{2,1,0:T(8,128)S(1)} all-to-all(f32[32,8,128]{2,1,0:T(8,128)S(1)} %get-tuple-element.13), channel_id=1, replica_groups=mesh['pb'=4,'pa'=32] {'pa'}, dimensions={0} | all-to-all | bytes 262144 | tf_op jit(solution)/shard_map/all_to_all | solution.py:198
  30.6 5.7 %shard_map.68 = (f32[1,128]{1,0:T(1,128)S(1)}, bf16[32,128,128]{2,1,0:T(8,128)(2,1)}, f32[2,192,128]{2,1,0:T(8,128)S(1)}, bf16[2,192,128]{2,1,0:T(8,128)(2,1)S(1...) custom-call(s32[16,1]{1,0:T(8,128)S(1)} %copy.10.mask_s.mask_v, s32[16,1]{1,0:T(8,128)S(1)} %copy.10.mask_s.mask_v, ...), custom_call_target="tpu_custom_call" | custom-call | tf_op jit(solution)/shard_map/pallas_call | solution.py:200
  36.3 25.7 %all-to-all-start.1 = ((bf16[32,128,128]{2,1,0:T(8,128)(2,1)}), bf16[32,128,128]{2,1,0:T(8,128)(2,1)S(1)}, u32[]{:S(2)}, u32[]{:S(2)}) async-start(bf16[32,128,128]{2,1,0:T(8,128)(2,1)} %get-tuple-element.18), calls=%async_computation.1 | async-start | bytes 2097152 | tf_op jit(solution)/shard_map/all_to_all | solution.py:208
  62.1 1.6 %collective-permute-start = (bf16[2,192,128]{2,1,0:T(8,128)(2,1)S(1)}, bf16[2,192,128]{2,1,0:T(8,128)(2,1)S(1)}, u32[]{:S(2)}, u32[]{:S(2)}) collective-permute-start(bf16[2,192,128]{2,1,0:T(8,128)(2,1)S(1)} %get-tuple-element.20), channel_id=1, source_target_pairs={{0,32},{32,64},{64,96},{96,0},{1,33},{33,65},{65,97},{97,1},{2,34}... | collective-permute-start | bytes 294920 | tf_op jit(solution)/shard_map/ppermute | solution.py:183
  63.6 2.0 %collective-permute-start.1 = (bf16[2,192,128]{2,1,0:T(8,128)(2,1)S(1)}, bf16[2,192,128]{2,1,0:T(8,128)(2,1)S(1)}, u32[]{:S(2)}, u32[]{:S(2)}) collective-permute-start(bf16[2,192,128]{2,1,0:T(8,128)(2,1)S(1)} %get-tuple-element.21), channel_id=1, source_target_pairs={{0,64},{32,96},{64,0},{96,32},{1,65},{33,97},{65,1},{97,33},{2,66}... | collective-permute-start | bytes 294920 | tf_op jit(solution)/shard_map/ppermute | solution.py:183
  65.6 2.2 %collective-permute-start.2 = (bf16[2,192,128]{2,1,0:T(8,128)(2,1)S(1)}, bf16[2,192,128]{2,1,0:T(8,128)(2,1)S(1)}, u32[]{:S(2)}, u32[]{:S(2)}) collective-permute-start(bf16[2,192,128]{2,1,0:T(8,128)(2,1)S(1)} %get-tuple-element.22), channel_id=1, source_target_pairs={{0,96},{32,0},{64,32},{96,64},{1,97},{33,1},{65,33},{97,65},{2,98}... | collective-permute-start | bytes 294920 | tf_op jit(solution)/shard_map/ppermute | solution.py:183
  67.8 0.9 %collective-permute-done.a_ref = bf16[2,192,128]{2,1,0:T(8,128)(2,1)S(1)} collective-permute-done((bf16[2,192,128]{2,1,0:T(8,128)(2,1)S(1)}, bf16[2,192,128]{2,1,0:T(8,128)(2,1)S(1)}, u32[]{:S(2)}, u32[]{:S(2)}) %collective-permute-start) | collective-permute-done | bytes 98336 | tf_op jit(solution)/shard_map/ppermute | solution.py:183
  68.7 1.9 %collective-permute-done.1.b_ref = bf16[2,192,128]{2,1,0:T(8,128)(2,1)S(1)} collective-permute-done((bf16[2,192,128]{2,1,0:T(8,128)(2,1)S(1)}, bf16[2,192,128]{2,1,0:T(8,128)(2,1)S(1)}, u32[]{:S(2)}, u32[]{:S(2)}) %collective-permute-start.1) | collective-permute-done | bytes 98336 | tf_op jit(solution)/shard_map/ppermute | solution.py:183
  70.7 0.4 collective-permute-done.2.c_ref
  71.1 3.1 %collective-permute-start.5 = (bf16[2,192,128]{2,1,0:T(8,128)(2,1)S(1)}, bf16[2,192,128]{2,1,0:T(8,128)(2,1)S(1)}, u32[]{:S(2)}, u32[]{:S(2)}) collective-permute-start(bf16[2,192,128]{2,1,0:T(8,128)(2,1)S(1)} %shard_map.70.own_ref), channel_id=1, source_target_pairs={{0,96},{32,0},{64,32},{96,64},{1,97},{33,1},{65,33},{97,65},{2,98}... | collective-permute-start | bytes 294920 | tf_op jit(solution)/shard_map/ppermute | solution.py:183
  74.2 0.8 collective-permute-start.4
  74.9 0.7 collective-permute-start.3
  75.6 0.6 dynamic-slice_bitcast_fusion
  76.2 1.7 %collective-permute-done.5.c_ref = bf16[2,192,128]{2,1,0:T(8,128)(2,1)S(1)} collective-permute-done((bf16[2,192,128]{2,1,0:T(8,128)(2,1)S(1)}, bf16[2,192,128]{2,1,0:T(8,128)(2,1)S(1)}, u32[]{:S(2)}, u32[]{:S(2)}) %collective-permute-start.5) | collective-permute-done | bytes 98336 | tf_op jit(solution)/shard_map/ppermute | solution.py:183
  77.9 2.7 %collective-permute-done.4.b_ref = bf16[2,192,128]{2,1,0:T(8,128)(2,1)S(1)} collective-permute-done((bf16[2,192,128]{2,1,0:T(8,128)(2,1)S(1)}, bf16[2,192,128]{2,1,0:T(8,128)(2,1)S(1)}, u32[]{:S(2)}, u32[]{:S(2)}) %collective-permute-start.4) | collective-permute-done | bytes 98336 | tf_op jit(solution)/shard_map/ppermute | solution.py:183
  80.7 0.9 %collective-permute-done.3.a_ref = bf16[2,192,128]{2,1,0:T(8,128)(2,1)S(1)} collective-permute-done((bf16[2,192,128]{2,1,0:T(8,128)(2,1)S(1)}, bf16[2,192,128]{2,1,0:T(8,128)(2,1)S(1)}, u32[]{:S(2)}, u32[]{:S(2)}) %collective-permute-start.3) | collective-permute-done | bytes 98336 | tf_op jit(solution)/shard_map/ppermute | solution.py:183
  81.6 0.1 shard_map.71
  81.7 1.0 %copy.13 = f32[8,180,128]{2,0,1:T(8,128)} copy(f32[8,180,128]{2,1,0:T(8,128)S(1)} %shard_map.71) | data formatting | bytes 1474560
  82.7 0.0 all-to-all-done.1.in_ref
  82.7 0.8 shard_map.69
  (1 shorter events, 0.0 us)
Async XLA Ops:
  2.4 0.7 copy-start.1
  3.1 1.2 %copy-start = (bf16[128,32,128]{2,1,0:T(8,128)(2,1)S(1)}, bf16[128,32,128]{2,1,0:T(8,128)(2,1)}, u32[]{:S(2)}) copy-start(bf16[128,32,128]{2,1,0:T(8,128)(2,1)} %param.4) | copy-start | bytes 3145732
  36.3 46.3 %all-to-all-start.1 = ((bf16[32,128,128]{2,1,0:T(8,128)(2,1)}), bf16[32,128,128]{2,1,0:T(8,128)(2,1)S(1)}, u32[]{:S(2)}, u32[]{:S(2)}) async-start(bf16[32,128,128]{2,1,0:T(8,128)(2,1)} %get-tuple-element.18), calls=%async_computation.1 | async-start | bytes 2097152 | tf_op jit(solution)/shard_map/all_to_all | solution.py:208
  62.1 6.7 %collective-permute-start = (bf16[2,192,128]{2,1,0:T(8,128)(2,1)S(1)}, bf16[2,192,128]{2,1,0:T(8,128)(2,1)S(1)}, u32[]{:S(2)}, u32[]{:S(2)}) collective-permute-start(bf16[2,192,128]{2,1,0:T(8,128)(2,1)S(1)} %get-tuple-element.20), channel_id=1, source_target_pairs={{0,32},{32,64},{64,96},{96,0},{1,33},{33,65},{65,97},{97,1},{2,34}... | collective-permute-start | bytes 294920 | tf_op jit(solution)/shard_map/ppermute | solution.py:183
  63.6 7.0 %collective-permute-start.1 = (bf16[2,192,128]{2,1,0:T(8,128)(2,1)S(1)}, bf16[2,192,128]{2,1,0:T(8,128)(2,1)S(1)}, u32[]{:S(2)}, u32[]{:S(2)}) collective-permute-start(bf16[2,192,128]{2,1,0:T(8,128)(2,1)S(1)} %get-tuple-element.21), channel_id=1, source_target_pairs={{0,64},{32,96},{64,0},{96,32},{1,65},{33,97},{65,1},{97,33},{2,66}... | collective-permute-start | bytes 294920 | tf_op jit(solution)/shard_map/ppermute | solution.py:183
  65.6 5.4 %collective-permute-start.2 = (bf16[2,192,128]{2,1,0:T(8,128)(2,1)S(1)}, bf16[2,192,128]{2,1,0:T(8,128)(2,1)S(1)}, u32[]{:S(2)}, u32[]{:S(2)}) collective-permute-start(bf16[2,192,128]{2,1,0:T(8,128)(2,1)S(1)} %get-tuple-element.22), channel_id=1, source_target_pairs={{0,96},{32,0},{64,32},{96,64},{1,97},{33,1},{65,33},{97,65},{2,98}... | collective-permute-start | bytes 294920 | tf_op jit(solution)/shard_map/ppermute | solution.py:183
  71.1 6.9 %collective-permute-start.5 = (bf16[2,192,128]{2,1,0:T(8,128)(2,1)S(1)}, bf16[2,192,128]{2,1,0:T(8,128)(2,1)S(1)}, u32[]{:S(2)}, u32[]{:S(2)}) collective-permute-start(bf16[2,192,128]{2,1,0:T(8,128)(2,1)S(1)} %shard_map.70.own_ref), channel_id=1, source_target_pairs={{0,96},{32,0},{64,32},{96,64},{1,97},{33,1},{65,33},{97,65},{2,98}... | collective-permute-start | bytes 294920 | tf_op jit(solution)/shard_map/ppermute | solution.py:183
  74.2 6.5 %collective-permute-start.4 = (bf16[2,192,128]{2,1,0:T(8,128)(2,1)S(1)}, bf16[2,192,128]{2,1,0:T(8,128)(2,1)S(1)}, u32[]{:S(2)}, u32[]{:S(2)}) collective-permute-start(bf16[2,192,128]{2,1,0:T(8,128)(2,1)S(1)} %shard_map.70.own_ref), channel_id=1, source_target_pairs={{0,64},{32,96},{64,0},{96,32},{1,65},{33,97},{65,1},{97,33},{2,66}... | collective-permute-start | bytes 294920 | tf_op jit(solution)/shard_map/ppermute | solution.py:183
  74.9 6.7 %collective-permute-start.3 = (bf16[2,192,128]{2,1,0:T(8,128)(2,1)S(1)}, bf16[2,192,128]{2,1,0:T(8,128)(2,1)S(1)}, u32[]{:S(2)}, u32[]{:S(2)}) collective-permute-start(bf16[2,192,128]{2,1,0:T(8,128)(2,1)S(1)} %shard_map.70.own_ref), channel_id=1, source_target_pairs={{0,32},{32,64},{64,96},{96,0},{1,33},{33,65},{65,97},{97,1},{2,34}... | collective-permute-start | bytes 294920 | tf_op jit(solution)/shard_map/ppermute | solution.py:183

commit v2 on v1

v2 whole, which is shorter than its diff:
```python
import jax
import jax.numpy as jnp
from jax import lax
from jax.experimental import pallas as pl
from jax.experimental.pallas import tpu as pltpu
from jax.sharding import PartitionSpec as P

very_low = -1e30
contrast_temp = 0.05
f32, bf16 = jnp.float32, jnp.bfloat16
VMEM = pl.BlockSpec(memory_space=pltpu.VMEM)
SMEM = pl.BlockSpec(memory_space=pltpu.SMEM)
B, LQ, LP, D = 8, 32, 180, 128
QT = B * LQ
PT = B * LP
turned_dims = (((1,), (1,)), ((), ()))


def iota(shape, dim):
    return lax.broadcasted_iota(jnp.int32, shape, dim)


def exact_dot(a, b):
    return jnp.dot(a, b, precision=lax.Precision.HIGHEST, preferred_element_type=f32)


def expand(row, blocks):
    count = blocks * B
    own = iota((blocks, count), 1) // B == iota((blocks, count), 0)
    pick = (iota((count, QT), 0) % B == iota((count, QT), 1) // LQ).astype(f32)
    return exact_dot(jnp.where(own, row, 0.0), pick)


def squeeze(wide, blocks):
    count = blocks * B
    pick = (iota((QT, count), 0) == LQ * (iota((QT, count), 1) % B)).astype(f32)
    own = iota((blocks, count), 1) // B == iota((blocks, count), 0)
    return jnp.sum(jnp.where(own, exact_dot(wide, pick), 0.0), axis=0, keepdims=True)


def list_tasks(mask_s, order):
    blocks = mask_s.shape[0]
    count = jnp.int32(0)
    for wanted in (True, False):
        for k in range(blocks):
            here = (mask_s[k] > 0) == wanted

            @pl.when(here)
            def _(k=k, count=count):
                order[count] = k

            count = count + here.astype(jnp.int32)
        if wanted:
            active = count
    return active


def active_blocks(mask_s):
    blocks = mask_s.shape[0]
    return jnp.stack([jnp.full((B, QT), mask_s[k], jnp.int32) for k in range(blocks)]) > 0


def pair_queries(q_ref, first, second):
    return jnp.concatenate(
        [q_ref[pl.ds(pl.multiple_of(k * QT, QT), QT), :] for k in (first, second)], axis=0
    )


def is_positive(pos_ref, active, blocks):
    pos = expand(pos_ref[...].astype(f32), blocks).astype(jnp.int32)
    item = iota((blocks, B, QT), 1) + lax.axis_index("pa") * B
    return (pos[:, None, :] == item) & active


def scores_kernel(mask_s, pos_ref, q_ref, p_ref, send_ref, logit_ref, top_ref, tot_ref, order, sim_ref):
    blocks = mask_s.shape[0]
    count = list_tasks(mask_s, order)
    top_ref[...] = jnp.zeros_like(top_ref)
    tot_ref[...] = jnp.ones_like(tot_ref)

    @pl.loop(0, (count + 1) // 2)
    def _(step):
        pair = (order[2 * step], order[2 * step + 1])
        qk = pair_queries(q_ref, *pair)
        sim_ref[...] = lax.dot_general(p_ref[...], qk, turned_dims, preferred_element_type=f32)
        for half, k in enumerate(pair):
            part = sim_ref[:, half * QT : (half + 1) * QT].reshape(LP, B, QT)
            top = jnp.max(part, axis=0)
            top_ref[k] = top
            tot_ref[k] = jnp.sum(jnp.exp(part - top[None]), axis=0)

    active = active_blocks(mask_s)
    token_lse = (top_ref[...] + jnp.log(tot_ref[...])).reshape(blocks * B, QT)
    same = (iota((QT, QT), 0) // LQ == iota((QT, QT), 1) // LQ).astype(f32)
    score = (exact_dot(token_lse, same) / LQ).reshape(blocks, B, QT)
    logit = jnp.where(active, score / contrast_temp, very_low)
    logit_ref[...] = logit
    local_top = jnp.max(logit, axis=1, keepdims=True)
    local_total = jnp.sum(jnp.where(active, jnp.exp(logit - local_top), 0.0), axis=1)
    local_pos = jnp.sum(jnp.where(is_positive(pos_ref, active, blocks), logit, 0.0), axis=1)
    rows = [squeeze(x, blocks) for x in (local_top[:, 0, :], local_total, local_pos)]
    rows.append(jnp.zeros((5, blocks * B), f32))
    send_ref[...] = jnp.broadcast_to(jnp.concatenate(rows, axis=0)[None], send_ref.shape)


def grads_kernel(
    mask_s, pos_ref, q_ref, p_ref, stat_ref, logit_ref, top_ref, tot_ref,
    loss_ref, gq_ref, own_ref, send1_ref, send2_ref, send3_ref,
    order, turn_ref, weight_ref, gp_ref, sim_ref, dsim_ref,
):
    blocks = mask_s.shape[0]
    count = list_tasks(mask_s, order)
    turn_ref[...] = p_ref[...].astype(f32).T.astype(bf16)
    tops = stat_ref[:, 0, :]
    glob_top = jnp.max(tops, axis=0, keepdims=True)
    glob_total = jnp.sum(stat_ref[:, 1, :] * jnp.exp(tops - glob_top), axis=0, keepdims=True)
    glob_pos = jnp.sum(stat_ref[:, 2, :], axis=0, keepdims=True)
    loss_ref[...] = glob_top + jnp.log(glob_total) - glob_pos
    active = active_blocks(mask_s)
    wide_top = expand(glob_top, blocks)[:, None, :]
    wide_total = expand(glob_total, blocks)[:, None, :]
    prob = jnp.where(active, jnp.exp(logit_ref[...] - wide_top) / wide_total, 0.0)
    onehot = is_positive(pos_ref, active, blocks).astype(f32)
    weight_ref[...] = (prob - onehot) / (contrast_temp * LQ) / tot_ref[...]
    gp_ref[...] = jnp.zeros_like(gp_ref)
    gq_ref[...] = jnp.zeros_like(gq_ref)

    @pl.loop(0, (count + 1) // 2)
    def _(step):
        pair = (order[2 * step], order[2 * step + 1])
        qk = pair_queries(q_ref, *pair)
        sim_ref[...] = lax.dot_general(p_ref[...], qk, turned_dims, preferred_element_type=f32)
        for half, k in enumerate(pair):
            here = slice(half * QT, (half + 1) * QT)
            part = sim_ref[:, here].reshape(LP, B, QT)
            dsim = jnp.exp(part - top_ref[k][None]) * weight_ref[k][None]
            dsim_ref[:, here] = dsim.astype(bf16).reshape(PT, QT)
        gp_ref[...] += jnp.dot(dsim_ref[...], qk, preferred_element_type=f32)
        turned = jnp.dot(turn_ref[...], dsim_ref[...], preferred_element_type=f32).astype(bf16)
        for half, k in enumerate(pair):
            for j in range(2):
                start = half * QT + j * D
                gq_ref[2 * k + j] = turned[:, start : start + D]

    mine = lax.axis_index("pb")
    piece = PT // 4

    def rows_of(owner):
        return gp_ref[pl.ds(pl.multiple_of(owner * piece, B), piece), :]

    own_ref[...] = rows_of(mine)
    for s, send in ((1, send1_ref), (2, send2_ref), (3, send3_ref)):
        send[...] = rows_of(lax.rem(mine + s, 4)).astype(bf16)


def sum_kernel(own_ref, a_ref, b_ref, c_ref, out_ref):
    total = own_ref[...] + a_ref[...].astype(f32) + b_ref[...].astype(f32) + c_ref[...].astype(f32)
    out_ref[...] = total.astype(bf16)


def place_kernel(own_ref, a_ref, b_ref, c_ref, out_ref):
    mine = lax.axis_index("pb")
    piece = PT // 4
    for s, ref in ((0, own_ref), (1, a_ref), (2, b_ref), (3, c_ref)):
        owner = lax.rem(mine + 4 - s, 4)
        out_ref[pl.ds(pl.multiple_of(owner * piece, B), piece), :] = ref[...].astype(f32)


def rows_kernel(in_ref, out_ref):
    total = in_ref[0].astype(f32)
    for i in range(1, in_ref.shape[0]):
        total += in_ref[i].astype(f32)
    out_ref[...] = total.T


def call(kernel, out, n_in, scalars=0, scratch=(), vmem=48 << 20, flops=0, nbytes=0):
    return pl.pallas_call(
        kernel,
        out_shape=out,
        in_specs=[SMEM if i < scalars else VMEM for i in range(n_in)],
        out_specs=jax.tree.map(lambda _: VMEM, out),
        scratch_shapes=list(scratch),
        compiler_params=pltpu.CompilerParams(vmem_limit_bytes=vmem),
        cost_estimate=pl.CostEstimate(flops=flops, bytes_accessed=nbytes, transcendentals=0),
    )


def turn(x, s):
    return lax.ppermute(x, "pb", [(i, (i + s) % 4) for i in range(4)])


def on_device(queries, passages, pair_mask, positive):
    rows = queries.shape[0]
    blocks = rows // B
    peers = lax.axis_size("pa")
    shape = jax.ShapeDtypeStruct
    flat_q = queries.reshape(rows * LQ, D)
    flat_p = jnp.swapaxes(passages, 0, 1).reshape(PT, D)
    mask = pair_mask.reshape(blocks)
    pos = positive.reshape(1, rows)
    wide = shape((blocks, B, QT), f32)
    order = pltpu.SMEM((blocks,), jnp.int32)
    sim = pltpu.VMEM((PT, 2 * QT), f32)
    send, logit, top, tot = call(
        scores_kernel,
        (shape((peers, 8, rows), f32), wide, wide, wide),
        4,
        1,
        [order, sim],
        flops=5_000_000_000,
        nbytes=3_000_000,
    )(mask, pos, flat_q, flat_p)
    stats = lax.all_to_all(send, "pa", 0, 0, tiled=True)
    piece = shape((PT // 4, D), bf16)
    loss, gq, own, send1, send2, send3 = call(
        grads_kernel,
        (shape((1, rows), f32), shape((peers, D, 4 * LQ), bf16), shape((PT // 4, D), f32), piece, piece, piece),
        8,
        1,
        [
            order,
            pltpu.VMEM((D, PT), bf16),
            pltpu.VMEM((blocks, B, QT), f32),
            pltpu.VMEM((PT, D), f32),
            sim,
            pltpu.VMEM((PT, 2 * QT), bf16),
        ],
        flops=10_000_000_000,
        nbytes=5_000_000,
    )(mask, pos, flat_q, flat_p, stats, logit, top, tot)
    got = [turn(x, s) for x, s in ((send1, 1), (send2, 2), (send3, 3))]
    gq_terms = lax.all_to_all(gq, "pa", 0, 0, tiled=True)
    mine = call(sum_kernel, piece, 4, nbytes=1_000_000)(own, *got)
    others = [turn(mine, s) for s in (1, 2, 3)]
    flat = call(place_kernel, shape((PT, D), f32), 4, nbytes=1_000_000)(mine, *others)
    grad_p = jnp.swapaxes(flat.reshape(LP, B, D), 0, 1)
    grad_q = call(rows_kernel, shape((4 * LQ, D), f32), 1, nbytes=1_000_000)(gq_terms)
    loss_rows = lax.dynamic_slice_in_dim(loss[0], lax.axis_index("pa") * 4, 4, 0)
    return loss_rows, grad_q.reshape(4, LQ, D), grad_p


def solution(mesh):
    placed = (P("pb", None, None), P("pa", None, None), P("pb", "pa"), P("pb"))
    return jax.shard_map(
        on_device,
        mesh=mesh,
        in_specs=placed,
        out_specs=(P(("pb", "pa")), P(("pb", "pa"), None, None), P("pa", None, None)),
        check_vma=False,
    )
```

time: 83.9 us -> 64.5 us (0.77)
  starting transfers between devices: 36.1 us -> 22.3 us
  Pallas kernels: 9.48 us -> 7.53 us
  local copies, waits for them, and re-layouts: 5.22 us -> 3.45 us
  blocking collectives: 23.5 us -> 22.2 us
    all_to_all x1, starting transfers between devices: 25.7 us -> 10.9 us  [on_device(): gq_terms = lax.all_to_all(gq, 'pa', 0, 0, tiled=True)]
    pallas_call x5, Pallas kernels: 9.48 us -> 7.53 us  [the longest x1 3.23 us: on_device(): call(grads_kernel, (shape((1, rows), f32), shape((peers, D, 4 * LQ), bf16...]
    unnamed x7 -> x8, local copies, waits for them, and re-layouts: 4.64 us -> 2.87 us
    all_to_all x1, blocking collectives: 23.5 us -> 22.2 us  [on_device(): stats = lax.all_to_all(send, 'pa', 0, 0, tiled=True)]
    ppermute x6, starting transfers between devices: 10.3 us -> 11.4 us  [turn(): return lax.ppermute(x, 'pb', [(i, (i + s) % 4) for i in range(4)])]
  transfers between devices with their start and end apart: 7 -> 7, of which waited for: 6 -> 5; matrix products, arithmetic and copies ran while one was open for 2% -> 1% of each run, Pallas kernels for 0% -> 2%
where the time goes in v2:
time: 64.5 us; the launch traced here: 64.3 us
  starting transfers between devices  22.3 us (35%)
  blocking collectives  22.2 us (34%)
  waiting for transfers between devices  8.18 us (13%)
  Pallas kernels  7.53 us (12%)
  local copies, waits for them, and re-layouts  3.45 us (5%)
  between operations  0.68 us (1%)
    all_to_all x1, blocking collectives, on_device(): stats = lax.all_to_all(send, 'pa', 0, 0, tiled=True)  22.2 us
    ppermute x6, starting transfers between devices, turn(): return lax.ppermute(x, 'pb', [(i, (i + s) % 4) for i in range(4)])  11.4 us
    all_to_all x1, starting transfers between devices, on_device(): gq_terms = lax.all_to_all(gq, 'pa', 0, 0, tiled=True)  10.9 us
    ppermute x6, waiting for transfers between devices, turn(): return lax.ppermute(x, 'pb', [(i, (i + s) % 4) for i in range(4)])  8.18 us
    pallas_call x1, Pallas kernels, on_device(): call(grads_kernel, (shape((1, rows), f32), shape((peers, D, 4 * LQ), bf16...  3.23 us
    unnamed x8, local copies, waits for them, and re-layouts  2.87 us
    pallas_call x1, Pallas kernels, on_device(): call(scores_kernel, (shape((peers, 8, rows), f32), wide, wide, wide), 4,...  2.48 us
  transfers between devices with their start and end apart: 7, of which 5 were waited for; matrix products, arithmetic and copies ran while one was open for 1% of the time, Pallas kernels for 2%

profile of v2, /device:TPU:0, one launch (start us, length us, event | category | flops | bytes accessed | tf_op | source)
XLA Modules:
  0.0 64.3 jit_solution(9622465095302684225)
XLA Ops:
  0.6 0.0 copy-start.2
  0.6 0.0 copy-start.3
  0.7 0.6 copy-done.2
  1.3 0.0 copy-done.3
  1.3 0.0 copy-start
  1.3 1.2 %copy-done = bf16[128,32,128]{2,1,0:T(8,128)(2,1)S(1)} copy-done((bf16[128,32,128]{2,1,0:T(8,128)(2,1)S(1)}, bf16[128,32,128]{2,1,0:T(8,128)(2,1)}, u32[]{:S(2)}) %copy-start) | copy-done | bytes 1048600
  2.5 0.0 copy-start.1
  2.5 1.0 %copy-done.1 = bf16[8,180,128]{2,0,1:T(8,128)(2,1)S(1)} copy-done((bf16[8,180,128]{2,0,1:T(8,128)(2,1)S(1)}, bf16[8,180,128]{2,0,1:T(8,128)(2,1)}, u32[]{:S(2)}) %copy-start.1) | copy-done | bytes 368664
  3.5 2.5 %shard_map.67 = (f32[32,8,128]{2,1,0:T(8,128)S(1)}, f32[16,8,256]{2,1,0:T(8,128)S(1)}, f32[16,8,256]{2,1,0:T(8,128)S(1)}, f32[16,8,256]{2,1,0:T(8,128)S(1)}) custom-call(s32[16]{0:T(128)S(1)} %bitcast.16, s32[1,128]{1,0:T(1,128)S(1)} %bitcast.18, bf16[4096,128]{1,0:T(8,128)(2,1)S(1)} %bitcast.12, bf16[1440,128]{1,0:T(8,128)(2,1)S(1)} %bitcast.14), custom_call_target="tpu_custom_call" | custom-call | flops 5000000000 | bytes 3000000 | tf_op jit(solution)/shard_map/pallas_call | solution.py:204
  6.0 22.2 %all_to_all.10.stat_ref = f32[32,8,128]{2,1,0:T(8,128)S(1)} all-to-all(f32[32,8,128]{2,1,0:T(8,128)S(1)} %get-tuple-element.13), channel_id=1, replica_groups=mesh['pb'=4,'pa'=32] {'pa'}, dimensions={0} | all-to-all | bytes 262144 | tf_op jit(solution)/shard_map/all_to_all | solution.py:213
  28.2 3.2 %shard_map.68 = (f32[1,128]{1,0:T(1,128)S(1)}, bf16[32,128,128]{2,1,0:T(8,128)(2,1)}, f32[360,128]{1,0:T(8,128)S(1)}, bf16[360,128]{1,0:T(8,128)(2,1)S(1)}, bf16...) custom-call(s32[16]{0:T(128)S(1)} %bitcast.17, s32[1,128]{1,0:T(1,128)S(1)} %bitcast.19, ...), custom_call_target="tpu_custom_call" | custom-call | flops 10000000000 | bytes 5000000 | tf_op jit(solution)/shard_map/pallas_call | solution.py:215
  31.4 10.9 %all-to-all-start.1 = ((bf16[32,128,128]{2,1,0:T(8,128)(2,1)}), bf16[32,128,128]{2,1,0:T(8,128)(2,1)S(1)}, u32[]{:S(2)}, u32[]{:S(2)}) async-start(bf16[32,128,128]{2,1,0:T(8,128)(2,1)} %get-tuple-element.18), calls=%async_computation.1 | async-start | bytes 2097152 | tf_op jit(solution)/shard_map/all_to_all | solution.py:232
  42.3 3.1 %collective-permute-start = (bf16[360,128]{1,0:T(8,128)(2,1)S(1)}, bf16[360,128]{1,0:T(8,128)(2,1)S(1)}, u32[]{:S(2)}, u32[]{:S(2)}) collective-permute-start(bf16[360,128]{1,0:T(8,128)(2,1)S(1)} %get-tuple-element.20), channel_id=1, source_target_pairs={{0,32},{32,64},{64,96},{96,0},{1,33},{33,65},{65,97},{97,1},{2,34}... | collective-permute-start | bytes 276488 | tf_op jit(solution)/shard_map/ppermute | solution.py:189
  45.4 2.7 %collective-permute-start.1 = (bf16[360,128]{1,0:T(8,128)(2,1)S(1)}, bf16[360,128]{1,0:T(8,128)(2,1)S(1)}, u32[]{:S(2)}, u32[]{:S(2)}) collective-permute-start(bf16[360,128]{1,0:T(8,128)(2,1)S(1)} %get-tuple-element.21), channel_id=1, source_target_pairs={{0,64},{32,96},{64,0},{96,32},{1,65},{33,97},{65,1},{97,33},{2,66}... | collective-permute-start | bytes 276488 | tf_op jit(solution)/shard_map/ppermute | solution.py:189
  48.1 1.4 %collective-permute-start.2 = (bf16[360,128]{1,0:T(8,128)(2,1)S(1)}, bf16[360,128]{1,0:T(8,128)(2,1)S(1)}, u32[]{:S(2)}, u32[]{:S(2)}) collective-permute-start(bf16[360,128]{1,0:T(8,128)(2,1)S(1)} %get-tuple-element.22), channel_id=1, source_target_pairs={{0,96},{32,0},{64,32},{96,64},{1,97},{33,1},{65,33},{97,65},{2,98}... | collective-permute-start | bytes 276488 | tf_op jit(solution)/shard_map/ppermute | solution.py:189
  49.5 0.5 collective-permute-done.a_ref
  50.0 3.2 %collective-permute-done.1.b_ref = bf16[360,128]{1,0:T(8,128)(2,1)S(1)} collective-permute-done((bf16[360,128]{1,0:T(8,128)(2,1)S(1)}, bf16[360,128]{1,0:T(8,128)(2,1)S(1)}, u32[]{:S(2)}, u32[]{:S(2)}) %collective-permute-start.1) | collective-permute-done | bytes 92192 | tf_op jit(solution)/shard_map/ppermute | solution.py:189
  53.2 0.0 collective-permute-done.2.c_ref
  53.2 2.2 %collective-permute-start.5 = (bf16[360,128]{1,0:T(8,128)(2,1)S(1)}, bf16[360,128]{1,0:T(8,128)(2,1)S(1)}, u32[]{:S(2)}, u32[]{:S(2)}) collective-permute-start(bf16[360,128]{1,0:T(8,128)(2,1)S(1)} %shard_map.70.own_ref), channel_id=1, source_target_pairs={{0,96},{32,0},{64,32},{96,64},{1,97},{33,1},{65,33},{97,65},{2,98}... | collective-permute-start | bytes 276488 | tf_op jit(solution)/shard_map/ppermute | solution.py:189
  55.5 1.1 %collective-permute-start.4 = (bf16[360,128]{1,0:T(8,128)(2,1)S(1)}, bf16[360,128]{1,0:T(8,128)(2,1)S(1)}, u32[]{:S(2)}, u32[]{:S(2)}) collective-permute-start(bf16[360,128]{1,0:T(8,128)(2,1)S(1)} %shard_map.70.own_ref), channel_id=1, source_target_pairs={{0,64},{32,96},{64,0},{96,32},{1,65},{33,97},{65,1},{97,33},{2,66}... | collective-permute-start | bytes 276488 | tf_op jit(solution)/shard_map/ppermute | solution.py:189
  56.6 0.8 %collective-permute-start.3 = (bf16[360,128]{1,0:T(8,128)(2,1)S(1)}, bf16[360,128]{1,0:T(8,128)(2,1)S(1)}, u32[]{:S(2)}, u32[]{:S(2)}) collective-permute-start(bf16[360,128]{1,0:T(8,128)(2,1)S(1)} %shard_map.70.own_ref), channel_id=1, source_target_pairs={{0,32},{32,64},{64,96},{96,0},{1,33},{33,65},{65,97},{97,1},{2,34}... | collective-permute-start | bytes 276488 | tf_op jit(solution)/shard_map/ppermute | solution.py:189
  57.4 0.6 dynamic-slice_bitcast_fusion
  58.0 1.4 %collective-permute-done.5.c_ref = bf16[360,128]{1,0:T(8,128)(2,1)S(1)} collective-permute-done((bf16[360,128]{1,0:T(8,128)(2,1)S(1)}, bf16[360,128]{1,0:T(8,128)(2,1)S(1)}, u32[]{:S(2)}, u32[]{:S(2)}) %collective-permute-start.5) | collective-permute-done | bytes 92192 | tf_op jit(solution)/shard_map/ppermute | solution.py:189
  59.3 2.2 %collective-permute-done.4.b_ref = bf16[360,128]{1,0:T(8,128)(2,1)S(1)} collective-permute-done((bf16[360,128]{1,0:T(8,128)(2,1)S(1)}, bf16[360,128]{1,0:T(8,128)(2,1)S(1)}, u32[]{:S(2)}, u32[]{:S(2)}) %collective-permute-start.4) | collective-permute-done | bytes 92192 | tf_op jit(solution)/shard_map/ppermute | solution.py:189
  61.5 1.0 %collective-permute-done.3.a_ref = bf16[360,128]{1,0:T(8,128)(2,1)S(1)} collective-permute-done((bf16[360,128]{1,0:T(8,128)(2,1)S(1)}, bf16[360,128]{1,0:T(8,128)(2,1)S(1)}, u32[]{:S(2)}, u32[]{:S(2)}) %collective-permute-start.3) | collective-permute-done | bytes 92192 | tf_op jit(solution)/shard_map/ppermute | solution.py:189
  62.5 0.9 %shard_map.71 = f32[1440,128]{1,0:T(8,128)} custom-call(bf16[360,128]{1,0:T(8,128)(2,1)S(1)} %shard_map.70.own_ref, bf16[360,128]{1,0:T(8,128)(2,1)S(1)} %collective-permute-done.3.a_ref, bf16[360,128]{1,0:T(8,128)(2,1)S(1)} %collective-permute-done.4.b_ref, bf16[360,128]{1,0:T(8,128)(2,1)S(1)} %collective-permute-done.5.c_ref), custom_call_target="tpu_custom_call" | custom-call | bytes 1000000 | tf_op jit(solution)/shard_map/pallas_call | solution.py:235
  63.4 0.0 all-to-all-done.1.in_ref
  63.4 0.8 %shard_map.69 = f32[128,128]{1,0:T(8,128)} custom-call(bf16[32,128,128]{2,1,0:T(8,128)(2,1)S(1)} %all-to-all-done.1.in_ref), custom_call_target="tpu_custom_call" | custom-call | bytes 1000000 | tf_op jit(solution)/shard_map/pallas_call | solution.py:237
  (1 shorter events, 0.0 us)
Async XLA Ops:
  0.6 0.7 %copy-start.2 = (s32[16,1]{0,1:T(1,128)S(1)}, s32[16,1]{0,1:T(1,128)}, u32[]{:S(2)}) copy-start(s32[16,1]{0,1:T(1,128)} %param.6) | copy-start | bytes 196
  0.6 0.7 %copy-start.3 = (s32[128]{0:T(128)S(1)}, s32[128]{0:T(128)}, u32[]{:S(2)}) copy-start(s32[128]{0:T(128)} %param.7) | copy-start | bytes 1540
  1.3 1.2 %copy-start = (bf16[128,32,128]{2,1,0:T(8,128)(2,1)S(1)}, bf16[128,32,128]{2,1,0:T(8,128)(2,1)}, u32[]{:S(2)}) copy-start(bf16[128,32,128]{2,1,0:T(8,128)(2,1)} %param.4) | copy-start | bytes 3145732
  2.5 1.0 %copy-start.1 = (bf16[8,180,128]{2,0,1:T(8,128)(2,1)S(1)}, bf16[8,180,128]{2,0,1:T(8,128)(2,1)}, u32[]{:S(2)}) copy-start(bf16[8,180,128]{2,0,1:T(8,128)(2,1)} %param.5) | copy-start | bytes 1105924
  31.4 32.0 %all-to-all-start.1 = ((bf16[32,128,128]{2,1,0:T(8,128)(2,1)}), bf16[32,128,128]{2,1,0:T(8,128)(2,1)S(1)}, u32[]{:S(2)}, u32[]{:S(2)}) async-start(bf16[32,128,128]{2,1,0:T(8,128)(2,1)} %get-tuple-element.18), calls=%async_computation.1 | async-start | bytes 2097152 | tf_op jit(solution)/shard_map/all_to_all | solution.py:232
  42.3 7.7 %collective-permute-start = (bf16[360,128]{1,0:T(8,128)(2,1)S(1)}, bf16[360,128]{1,0:T(8,128)(2,1)S(1)}, u32[]{:S(2)}, u32[]{:S(2)}) collective-permute-start(bf16[360,128]{1,0:T(8,128)(2,1)S(1)} %get-tuple-element.20), channel_id=1, source_target_pairs={{0,32},{32,64},{64,96},{96,0},{1,33},{33,65},{65,97},{97,1},{2,34}... | collective-permute-start | bytes 276488 | tf_op jit(solution)/shard_map/ppermute | solution.py:189
  45.4 7.8 %collective-permute-start.1 = (bf16[360,128]{1,0:T(8,128)(2,1)S(1)}, bf16[360,128]{1,0:T(8,128)(2,1)S(1)}, u32[]{:S(2)}, u32[]{:S(2)}) collective-permute-start(bf16[360,128]{1,0:T(8,128)(2,1)S(1)} %get-tuple-element.21), channel_id=1, source_target_pairs={{0,64},{32,96},{64,0},{96,32},{1,65},{33,97},{65,1},{97,33},{2,66}... | collective-permute-start | bytes 276488 | tf_op jit(solution)/shard_map/ppermute | solution.py:189
  48.1 5.1 %collective-permute-start.2 = (bf16[360,128]{1,0:T(8,128)(2,1)S(1)}, bf16[360,128]{1,0:T(8,128)(2,1)S(1)}, u32[]{:S(2)}, u32[]{:S(2)}) collective-permute-start(bf16[360,128]{1,0:T(8,128)(2,1)S(1)} %get-tuple-element.22), channel_id=1, source_target_pairs={{0,96},{32,0},{64,32},{96,64},{1,97},{33,1},{65,33},{97,65},{2,98}... | collective-permute-start | bytes 276488 | tf_op jit(solution)/shard_map/ppermute | solution.py:189
  53.2 6.1 %collective-permute-start.5 = (bf16[360,128]{1,0:T(8,128)(2,1)S(1)}, bf16[360,128]{1,0:T(8,128)(2,1)S(1)}, u32[]{:S(2)}, u32[]{:S(2)}) collective-permute-start(bf16[360,128]{1,0:T(8,128)(2,1)S(1)} %shard_map.70.own_ref), channel_id=1, source_target_pairs={{0,96},{32,0},{64,32},{96,64},{1,97},{33,1},{65,33},{97,65},{2,98}... | collective-permute-start | bytes 276488 | tf_op jit(solution)/shard_map/ppermute | solution.py:189
  55.5 6.1 %collective-permute-start.4 = (bf16[360,128]{1,0:T(8,128)(2,1)S(1)}, bf16[360,128]{1,0:T(8,128)(2,1)S(1)}, u32[]{:S(2)}, u32[]{:S(2)}) collective-permute-start(bf16[360,128]{1,0:T(8,128)(2,1)S(1)} %shard_map.70.own_ref), channel_id=1, source_target_pairs={{0,64},{32,96},{64,0},{96,32},{1,65},{33,97},{65,1},{97,33},{2,66}... | collective-permute-start | bytes 276488 | tf_op jit(solution)/shard_map/ppermute | solution.py:189
  56.6 5.9 %collective-permute-start.3 = (bf16[360,128]{1,0:T(8,128)(2,1)S(1)}, bf16[360,128]{1,0:T(8,128)(2,1)S(1)}, u32[]{:S(2)}, u32[]{:S(2)}) collective-permute-start(bf16[360,128]{1,0:T(8,128)(2,1)S(1)} %shard_map.70.own_ref), channel_id=1, source_target_pairs={{0,32},{32,64},{64,96},{96,0},{1,33},{33,65},{65,97},{97,1},{2,34}... | collective-permute-start | bytes 276488 | tf_op jit(solution)/shard_map/ppermute | solution.py:189

commit v3 on v2

v3 whole, which is shorter than its diff:
```python
import jax
import jax.numpy as jnp
from jax import lax
from jax.experimental import pallas as pl
from jax.experimental.pallas import tpu as pltpu
from jax.sharding import PartitionSpec as P

very_low = -1e30
contrast_temp = 0.05
safe_low, safe_high = 1e-12, 1e12
kept_pairs = 5
f32, bf16 = jnp.float32, jnp.bfloat16
VMEM = pl.BlockSpec(memory_space=pltpu.VMEM)
SMEM = pl.BlockSpec(memory_space=pltpu.SMEM)
ANY = pl.BlockSpec(memory_space=pl.ANY)
B, LQ, LP, D = 8, 32, 180, 128
QT = B * LQ
PT = B * LP
turned_dims = (((1,), (1,)), ((), ()))


def iota(shape, dim):
    return lax.broadcasted_iota(jnp.int32, shape, dim)


def exact_dot(a, b):
    return jnp.dot(a, b, precision=lax.Precision.HIGHEST, preferred_element_type=f32)


def expand(row, blocks):
    count = blocks * B
    own = iota((blocks, count), 1) // B == iota((blocks, count), 0)
    pick = (iota((count, QT), 0) % B == iota((count, QT), 1) // LQ).astype(f32)
    return exact_dot(jnp.where(own, row, 0.0), pick)


def squeeze(wides, blocks):
    count = blocks * B
    pick = (iota((QT, count), 0) == LQ * (iota((QT, count), 1) % B)).astype(f32)
    own = iota((blocks, count), 1) // B == iota((blocks, count), 0)
    picked = exact_dot(jnp.concatenate(wides, axis=0), pick).reshape(len(wides), blocks, count)
    return [jnp.sum(jnp.where(own, x, 0.0), axis=0, keepdims=True) for x in picked]


def list_tasks(mask_s, order):
    blocks = mask_s.shape[0]
    count = jnp.int32(0)
    for wanted in (True, False):
        for k in range(blocks):
            here = (mask_s[k] > 0) == wanted

            @pl.when(here)
            def _(k=k, count=count):
                order[count] = k

            count = count + here.astype(jnp.int32)
        if wanted:
            active = count
    return active


def active_blocks(mask_s):
    blocks = mask_s.shape[0]
    return jnp.stack([jnp.full((B, QT), mask_s[k], jnp.int32) for k in range(blocks)]) > 0


def is_positive(pos_ref, active, blocks):
    pos = expand(pos_ref[...].astype(f32), blocks).astype(jnp.int32)
    item = iota((blocks, B, QT), 1) + lax.axis_index("pa") * B
    return (pos[:, None, :] == item) & active


def block_rows(q_ref, k):
    return q_ref[pl.ds(pl.multiple_of(k * QT, QT), QT), :]


def fetch_all(pairs, sems):
    fetches = [pltpu.make_async_copy(src, dst, sems.at[i]) for i, (src, dst) in enumerate(pairs)]
    for fetch in fetches:
        fetch.start()
    return [fetch.wait for fetch in fetches]


def task_sim(p_ref, q_ref, k):
    return lax.dot_general(p_ref[...], block_rows(q_ref, k), turned_dims, preferred_element_type=f32)


def scores_kernel(
    mask_hbm, pos_hbm, q_hbm, p_hbm,
    send_ref, logit_ref, onehot_ref, top_ref, tot_ref, kept_hbm,
    mask_s, pos_ref, q_ref, p_ref, order, sim_ref, kept_ref, sems, kept_sems,
):
    blocks = mask_s.shape[0]
    pairs = ((mask_hbm, mask_s), (pos_hbm, pos_ref), (p_hbm, p_ref), (q_hbm, q_ref))
    mask_wait, pos_wait, p_wait, q_wait = fetch_all(pairs, sems)
    top_ref[...] = jnp.zeros_like(top_ref)
    tot_ref[...] = jnp.ones_like(tot_ref)
    mask_wait()
    count = list_tasks(mask_s, order)
    steps = (count + 1) // 2
    kept_steps = jnp.minimum(steps, kept_pairs)
    active = active_blocks(mask_s)
    pos_wait()
    positive = is_positive(pos_ref, active, blocks)
    onehot_ref[...] = positive.astype(f32)
    p_wait()
    q_wait()

    def keep(task):
        return pltpu.make_async_copy(kept_ref.at[task], kept_hbm.at[task], kept_sems.at[task])

    def no_shift(task):
        k = order[task]
        scaled = jnp.exp(task_sim(p_ref, q_ref, k))
        tot_ref[k] = jnp.sum(scaled.reshape(LP, B, QT), axis=0)
        return scaled

    @pl.loop(0, kept_steps)
    def _(step):
        for half in range(2):
            kept_ref[2 * step + half] = no_shift(2 * step + half)
        for half in range(2):
            keep(2 * step + half).start()

    @pl.loop(kept_steps, steps)
    def _(step):
        for half in range(2):
            no_shift(2 * step + half)

    safe = (jnp.min(tot_ref[...]) > safe_low) & (jnp.max(tot_ref[...]) < safe_high)

    @pl.when(jnp.logical_not(safe))
    def _():
        @pl.loop(0, 2 * kept_steps)
        def _(task):
            keep(task).wait()

        @pl.loop(0, 2 * steps)
        def _(task):
            k = order[task]
            sim_ref[...] = task_sim(p_ref, q_ref, k)
            sim = sim_ref[...].reshape(LP, B, QT)
            top = jnp.max(sim, axis=0)
            scaled = jnp.exp(sim - top[None])
            top_ref[k] = top
            tot_ref[k] = jnp.sum(scaled, axis=0)

            @pl.when(task < 2 * kept_steps)
            def _():
                kept_ref[task] = scaled.reshape(PT, QT)
                keep(task).start()

    token_lse = (top_ref[...] + jnp.log(tot_ref[...])).reshape(blocks * B, QT)
    same = (iota((QT, QT), 0) // LQ == iota((QT, QT), 1) // LQ).astype(f32)
    score = (exact_dot(token_lse, same) / LQ).reshape(blocks, B, QT)
    logit = jnp.where(active, score / contrast_temp, very_low)
    logit_ref[...] = logit
    local_top = jnp.max(logit, axis=1, keepdims=True)
    local_total = jnp.sum(jnp.where(active, jnp.exp(logit - local_top), 0.0), axis=1)
    local_pos = jnp.sum(jnp.where(positive, logit, 0.0), axis=1)
    rows = squeeze((local_top[:, 0, :], local_total, local_pos), blocks)
    rows.append(jnp.zeros((5, blocks * B), f32))
    send_ref[...] = jnp.broadcast_to(jnp.concatenate(rows, axis=0)[None], send_ref.shape)

    @pl.loop(0, 2 * kept_steps)
    def _(task):
        keep(task).wait()


def grads_kernel(
    mask_hbm, stat_ref, logit_hbm, onehot_hbm, top_hbm, tot_hbm, q_hbm, p_hbm, turn_hbm, kept_hbm,
    loss_ref, gq_ref, own_ref, send1_ref, send2_ref, send3_ref,
    mask_s, logit_ref, onehot_ref, top_ref, tot_ref, q_ref, p_ref, turn_ref, kept_ref,
    order, weight_ref, gp_ref, sim_ref, dsim_ref, sems, kept_sems,
):
    blocks = mask_s.shape[0]
    ins = (mask_hbm, logit_hbm, onehot_hbm, top_hbm, tot_hbm, q_hbm, p_hbm, turn_hbm)
    refs = (mask_s, logit_ref, onehot_ref, top_ref, tot_ref, q_ref, p_ref, turn_ref)
    waits = fetch_all(zip(ins, refs), sems)

    def kept(task):
        return pltpu.make_async_copy(kept_hbm.at[task], kept_ref.at[task], kept_sems.at[task])

    waits[0]()
    count = list_tasks(mask_s, order)
    steps = (count + 1) // 2
    kept_steps = jnp.minimum(steps, kept_pairs)
    gp_ref[...] = jnp.zeros_like(gp_ref)
    tops = stat_ref[:, 0, :]
    glob_top = jnp.max(tops, axis=0, keepdims=True)
    glob_total = jnp.sum(stat_ref[:, 1, :] * jnp.exp(tops - glob_top), axis=0, keepdims=True)
    glob_pos = jnp.sum(stat_ref[:, 2, :], axis=0, keepdims=True)
    loss_ref[...] = glob_top + jnp.log(glob_total) - glob_pos
    wide_top = expand(glob_top, blocks)[:, None, :]
    wide_total = expand(glob_total, blocks)[:, None, :]
    for wait in waits[1:]:
        wait()

    @pl.loop(0, 2 * kept_steps)
    def _(task):
        kept(task).start()

    active = logit_ref[...] > very_low / 2
    prob = jnp.where(active, jnp.exp(logit_ref[...] - wide_top) / wide_total, 0.0)
    weight_ref[...] = (prob - onehot_ref[...]) / (contrast_temp * LQ) / tot_ref[...]

    def grads(step, scaled_of):
        pair = (order[2 * step], order[2 * step + 1])
        for half, k in enumerate(pair):
            scaled = scaled_of(half, k).reshape(LP, B, QT)
            dsim = (scaled * weight_ref[k][None]).astype(bf16)
            dsim_ref[:, half * QT : (half + 1) * QT] = dsim.reshape(PT, QT)
        qk = jnp.concatenate([block_rows(q_ref, k) for k in pair], axis=0)
        gp_ref[...] += jnp.dot(dsim_ref[...], qk, preferred_element_type=f32)
        turned = jnp.dot(turn_ref[...], dsim_ref[...], preferred_element_type=f32).astype(bf16)
        for half, k in enumerate(pair):
            for j in range(2):
                start = half * QT + j * D
                gq_ref[2 * k + j] = turned[:, start : start + D]

    @pl.loop(kept_steps, steps)
    def _(step):
        both = jnp.concatenate([block_rows(q_ref, order[2 * step + half]) for half in range(2)], axis=0)
        sim_ref[...] = lax.dot_general(p_ref[...], both, turned_dims, preferred_element_type=f32)

        def again(half, k):
            sim = sim_ref[:, half * QT : (half + 1) * QT].reshape(LP, B, QT)
            return jnp.exp(sim - top_ref[k][None])

        grads(step, again)

    @pl.loop(0, kept_steps)
    def _(step):
        kept(2 * step).wait()
        kept(2 * step + 1).wait()
        grads(step, lambda half, k: kept_ref[2 * step + half])

    @pl.loop(2 * steps, blocks)
    def _(task):
        k = order[task]
        for j in range(2):
            gq_ref[2 * k + j] = jnp.zeros((D, 4 * LQ), bf16)

    mine = lax.axis_index("pb")
    piece = PT // 4

    def rows_of(owner):
        return gp_ref[pl.ds(pl.multiple_of(owner * piece, B), piece), :]

    own_ref[...] = rows_of(mine)
    for s, send in ((1, send1_ref), (2, send2_ref), (3, send3_ref)):
        send[...] = rows_of(lax.rem(mine + s, 4)).astype(bf16)


def turn_kernel(p_ref, out_ref):
    out_ref[...] = p_ref[...].astype(f32).T.astype(bf16)


def sum_kernel(own_ref, a_ref, b_ref, c_ref, out_ref):
    total = own_ref[...] + a_ref[...].astype(f32) + b_ref[...].astype(f32) + c_ref[...].astype(f32)
    out_ref[...] = total.astype(bf16)


def last_kernel(own_ref, a_ref, b_ref, c_ref, terms_ref, gp_ref, gq_ref):
    mine = lax.axis_index("pb")
    piece = PT // 4
    for s, ref in ((0, own_ref), (1, a_ref), (2, b_ref), (3, c_ref)):
        owner = lax.rem(mine + 4 - s, 4)
        gp_ref[pl.ds(pl.multiple_of(owner * piece, B), piece), :] = ref[...].astype(f32)
    total = terms_ref[0].astype(f32)
    for i in range(1, terms_ref.shape[0]):
        total += terms_ref[i].astype(f32)
    gq_ref[...] = total.T


def in_hbm(x):
    return pltpu.with_memory_space_constraint(x, pltpu.HBM)


def call(kernel, out, specs, scratch=(), outs=None, vmem=40 << 20, flops=0, nbytes=0):
    return pl.pallas_call(
        kernel,
        out_shape=out,
        in_specs=list(specs),
        out_specs=outs or jax.tree.map(lambda _: VMEM, out),
        scratch_shapes=list(scratch),
        compiler_params=pltpu.CompilerParams(vmem_limit_bytes=vmem),
        cost_estimate=pl.CostEstimate(flops=flops, bytes_accessed=nbytes, transcendentals=0),
    )


def turn(x, s):
    return lax.ppermute(x, "pb", [(i, (i + s) % 4) for i in range(4)])


def on_device(queries, passages, pair_mask, positive):
    rows = queries.shape[0]
    blocks = rows // B
    peers = lax.axis_size("pa")
    shape = jax.ShapeDtypeStruct
    flat_q = queries.reshape(rows * LQ, D)
    flat_p = jnp.swapaxes(passages, 0, 1).reshape(PT, D)
    mask = pair_mask.reshape(blocks)
    pos = positive.reshape(1, rows)
    wide = shape((blocks, B, QT), f32)
    ints = pltpu.SMEM((blocks,), jnp.int32)
    vmem = pltpu.VMEM
    wide_ref, q_ref, p_ref = vmem((blocks, B, QT), f32), vmem((rows * LQ, D), bf16), vmem((PT, D), bf16)
    kept_ref = vmem((2 * kept_pairs, PT, QT), f32)
    kept_sems = pltpu.SemaphoreType.DMA((2 * kept_pairs,))
    mask, pos, flat_q, flat_p = (in_hbm(x) for x in (mask, pos, flat_q, flat_p))
    wide = pltpu.HBM((blocks, B, QT), f32)
    send, logit, onehot, top, tot, kept = call(
        scores_kernel,
        (shape((peers, 8, rows), f32), wide, wide, wide, wide, pltpu.HBM(kept_ref.shape, f32)),
        (ANY,) * 4,
        [
            ints,
            vmem((1, rows), jnp.int32),
            q_ref,
            p_ref,
            ints,
            vmem((PT, QT), f32),
            kept_ref,
            pltpu.SemaphoreType.DMA((4,)),
            kept_sems,
        ],
        outs=(VMEM,) * 5 + (ANY,),
        flops=2_000_000_000,
        nbytes=3_000_000,
    )(mask, pos, flat_q, flat_p)
    stats = lax.all_to_all(send, "pa", 0, 0, tiled=True)
    flat_p_after, _ = lax.optimization_barrier((flat_p, tot))
    turned_p = call(turn_kernel, pltpu.HBM((D, PT), bf16), (VMEM,), nbytes=1_000_000)(flat_p_after)
    piece = shape((PT // 4, D), bf16)
    ins = (logit, onehot, top, tot, flat_q, flat_p, turned_p, kept)
    loss, gq, own, send1, send2, send3 = call(
        grads_kernel,
        (shape((1, rows), f32), shape((peers, D, 4 * LQ), bf16), shape((PT // 4, D), f32), piece, piece, piece),
        (ANY, VMEM) + (ANY,) * 8,
        [
            ints,
            wide_ref,
            wide_ref,
            wide_ref,
            wide_ref,
            q_ref,
            p_ref,
            vmem((D, PT), bf16),
            kept_ref,
            ints,
            wide_ref,
            vmem((PT, D), f32),
            vmem((PT, 2 * QT), f32),
            vmem((PT, 2 * QT), bf16),
            pltpu.SemaphoreType.DMA((8,)),
            kept_sems,
        ],
        flops=5_000_000_000,
        nbytes=5_000_000,
    )(mask, stats, *(in_hbm(x) for x in ins))
    got = [turn(x, s) for x, s in ((send1, 1), (send2, 2), (send3, 3))]
    gq_terms = lax.all_to_all(gq, "pa", 0, 0, tiled=True)
    mine = call(sum_kernel, piece, (VMEM,) * 4, nbytes=1_000_000)(own, *got)
    others = [turn(mine, s) for s in (1, 2, 3)]
    flat, grad_q = call(
        last_kernel, (shape((PT, D), f32), shape((4 * LQ, D), f32)), (VMEM,) * 5, nbytes=2_000_000
    )(mine, *others, gq_terms)
    grad_p = jnp.swapaxes(flat.reshape(LP, B, D), 0, 1)
    loss_rows = lax.dynamic_slice_in_dim(loss[0], lax.axis_index("pa") * 4, 4, 0)
    return loss_rows, grad_q.reshape(4, LQ, D), grad_p


def solution(mesh):
    placed = (P("pb", None, None), P("pa", None, None), P("pb", "pa"), P("pb"))
    return jax.shard_map(
        on_device,
        mesh=mesh,
        in_specs=placed,
        out_specs=(P(("pb", "pa")), P(("pb", "pa"), None, None), P("pa", None, None)),
        check_vma=False,
    )
```

time: 64.5 us -> 68.7 us (1.065)
  the two profiles are of different devices: /device:TPU:0 before, /device:TPU:1 now
where the time goes in v3:
time: 68.7 us; the launch traced here: 68.3 us
  starting transfers between devices  32.3 us (47%)
  Pallas kernels  19.1 us (28%)
  waiting for transfers between devices  15.6 us (23%)
  between operations  0.69 us (1%)
    all_to_all x1, starting transfers between devices, on_device(): stats = lax.all_to_all(send, 'pa', 0, 0, tiled=True)  18.7 us
    pallas_call x1, Pallas kernels, on_device(): call(scores_kernel, (shape((peers, 8, rows), f32), wide, wide, wide, wide...  9.58 us
    ppermute x6, waiting for transfers between devices, turn(): return lax.ppermute(x, 'pb', [(i, (i + s) % 4) for i in range(4)])  8.88 us
    all_to_all x1, starting transfers between devices, on_device(): gq_terms = lax.all_to_all(gq, 'pa', 0, 0, tiled=True)  6.94 us
    ppermute x6, starting transfers between devices, turn(): return lax.ppermute(x, 'pb', [(i, (i + s) % 4) for i in range(4)])  6.62 us
    pallas_call x1, Pallas kernels, on_device(): call(grads_kernel, (shape((1, rows), f32), shape((peers, D, 4 * LQ), bf16...  6.5 us
    all_to_all x1, waiting for transfers between devices, on_device(): stats = lax.all_to_all(send, 'pa', 0, 0, tiled=True)  5.69 us
    pallas_call x1, Pallas kernels, on_device(): call(turn_kernel, pltpu.HBM((D, PT), bf16), (VMEM,), nbytes=1000000)  1.94 us
  transfers between devices with their start and end apart: 8, of which 7 were waited for; matrix products, arithmetic and copies ran while one was open for 1% of the time, Pallas kernels for 3%

profile of v3, /device:TPU:1, one launch (start us, length us, event | category | flops | bytes accessed | tf_op | source)
XLA Modules:
  0.0 68.3 jit_solution(16923734720535852535)
XLA Ops:
  0.6 9.6 %shard_map.67 = (f32[32,8,128]{2,1,0:T(8,128)}, f32[16,8,256]{2,1,0:T(8,128)}, f32[16,8,256]{2,1,0:T(8,128)}, f32[16,8,256]{2,1,0:T(8,128)}, f32[16,8,256]{2,1,0:T(8,128)}, /*index=5*/f32[10,1440,256]{2,1,0:T(8,128)}) custom-call(s32[16]{0:T(128)} %bitcast.20, s32[1,128]{1,0:T(1,128)} %bitcast.19, bf16[4096,128]{1,0:T(8,128)(2,1)} %bitcast.15, ...), custom_call_target="tpu_custom_call" | custom-call | flops 2000000000 | bytes 3000000 | tf_op jit(solution)/shard_map/pallas_call | solution.py:313
  10.2 18.7 %all-to-all-start = ((f32[32,8,128]{2,1,0:T(8,128)}), f32[32,8,128]{2,1,0:T(8,128)S(1)}, u32[]{:S(2)}, u32[]{:S(2)}) async-start(f32[32,8,128]{2,1,0:T(8,128)} %get-tuple-element.18), calls=%async_computation | async-start | bytes 262144 | tf_op jit(solution)/shard_map/all_to_all | solution.py:332
  28.9 1.9 %shard_map.68.turn_hbm = bf16[128,1440]{1,0:T(8,128)(2,1)} custom-call(bf16[1440,128]{1,0:T(8,128)(2,1)} %bitcast.13), custom_call_target="tpu_custom_call" | custom-call | bytes 1000000 | tf_op jit(solution)/shard_map/pallas_call | solution.py:334
  30.9 5.7 %all-to-all-done.stat_ref = f32[32,8,128]{2,1,0:T(8,128)S(1)} async-done(((f32[32,8,128]{2,1,0:T(8,128)}), f32[32,8,128]{2,1,0:T(8,128)S(1)}, u32[]{:S(2)}, u32[]{:S(2)}) %all-to-all-start) | async-done | bytes 131104 | tf_op jit(solution)/shard_map/all_to_all | solution.py:332
  36.6 6.5 %shard_map.69 = (f32[1,128]{1,0:T(1,128)S(1)}, bf16[32,128,128]{2,1,0:T(8,128)(2,1)}, f32[360,128]{1,0:T(8,128)S(1)}, bf16[360,128]{1,0:T(8,128)(2,1)S(1)}, bf16...) custom-call(s32[16]{0:T(128)} %bitcast.21, f32[32,8,128]{2,1,0:T(8,128)S(1)} %all-to-all-done.stat_ref, ...), custom_call_target="tpu_custom_call" | custom-call | flops 5000000000 | bytes 5000000 | tf_op jit(solution)/shard_map/pallas_call | solution.py:337
  43.1 6.9 %all-to-all-start.1 = ((bf16[32,128,128]{2,1,0:T(8,128)(2,1)}), bf16[32,128,128]{2,1,0:T(8,128)(2,1)S(1)}, u32[]{:S(2)}, u32[]{:S(2)}) async-start(bf16[32,128,128]{2,1,0:T(8,128)(2,1)} %get-tuple-element.30), calls=%async_computation.1 | async-start | bytes 2097152 | tf_op jit(solution)/shard_map/all_to_all | solution.py:363
  50.0 0.1 collective-permute-start
  50.1 0.1 collective-permute-start.1
  50.2 2.6 %collective-permute-start.2 = (bf16[360,128]{1,0:T(8,128)(2,1)S(1)}, bf16[360,128]{1,0:T(8,128)(2,1)S(1)}, u32[]{:S(2)}, u32[]{:S(2)}) collective-permute-start(bf16[360,128]{1,0:T(8,128)(2,1)S(1)} %get-tuple-element.29), channel_id=1, source_target_pairs={{0,96},{32,0},{64,32},{96,64},{1,97},{33,1},{65,33},{97,65},{2,98}... | collective-permute-start | bytes 276488 | tf_op jit(solution)/shard_map/ppermute | solution.py:293
  52.8 4.7 %collective-permute-done.a_ref = bf16[360,128]{1,0:T(8,128)(2,1)S(1)} collective-permute-done((bf16[360,128]{1,0:T(8,128)(2,1)S(1)}, bf16[360,128]{1,0:T(8,128)(2,1)S(1)}, u32[]{:S(2)}, u32[]{:S(2)}) %collective-permute-start) | collective-permute-done | bytes 92192 | tf_op jit(solution)/shard_map/ppermute | solution.py:293
  57.5 0.0 collective-permute-done.1.b_ref
  57.5 0.1 collective-permute-done.2.c_ref
  57.7 0.3 collective-permute-start.3
  58.0 3.5 %collective-permute-start.4 = (bf16[360,128]{1,0:T(8,128)(2,1)S(1)}, bf16[360,128]{1,0:T(8,128)(2,1)S(1)}, u32[]{:S(2)}, u32[]{:S(2)}) collective-permute-start(bf16[360,128]{1,0:T(8,128)(2,1)S(1)} %shard_map.70.own_ref), channel_id=1, source_target_pairs={{0,64},{32,96},{64,0},{96,32},{1,65},{33,97},{65,1},{97,33},{2,66}... | collective-permute-start | bytes 276488 | tf_op jit(solution)/shard_map/ppermute | solution.py:293
  61.6 0.0 collective-permute-start.5
  61.6 0.6 dynamic-slice_bitcast_fusion
  62.1 0.5 collective-permute-done.3.a_ref
  62.7 2.5 %collective-permute-done.4.b_ref = bf16[360,128]{1,0:T(8,128)(2,1)S(1)} collective-permute-done((bf16[360,128]{1,0:T(8,128)(2,1)S(1)}, bf16[360,128]{1,0:T(8,128)(2,1)S(1)}, u32[]{:S(2)}, u32[]{:S(2)}) %collective-permute-start.4) | collective-permute-done | bytes 92192 | tf_op jit(solution)/shard_map/ppermute | solution.py:293
  65.2 1.0 %collective-permute-done.5.c_ref = bf16[360,128]{1,0:T(8,128)(2,1)S(1)} collective-permute-done((bf16[360,128]{1,0:T(8,128)(2,1)S(1)}, bf16[360,128]{1,0:T(8,128)(2,1)S(1)}, u32[]{:S(2)}, u32[]{:S(2)}) %collective-permute-start.5) | collective-permute-done | bytes 92192 | tf_op jit(solution)/shard_map/ppermute | solution.py:293
  66.2 1.0 %all-to-all-done.1.terms_ref = bf16[32,128,128]{2,1,0:T(8,128)(2,1)S(1)} async-done(((bf16[32,128,128]{2,1,0:T(8,128)(2,1)}), bf16[32,128,128]{2,1,0:T(8,128)(2,1)S(1)}, u32[]{:S(2)}, u32[]{:S(2)}) %all-to-all-start.1) | async-done | bytes 1048608 | tf_op jit(solution)/shard_map/all_to_all | solution.py:363
  67.2 1.1 %shard_map.71 = (f32[1440,128]{1,0:T(8,128)}, f32[128,128]{1,0:T(8,128)}) custom-call(bf16[360,128]{1,0:T(8,128)(2,1)S(1)} %shard_map.70.own_ref, bf16[360,128]{1,0:T(8,128)(2,1)S(1)} %collective-permute-done.3.a_ref, bf16[360,128]{1,0:T(8,128)(2,1)S(1)} %collective-permute-done.4.b_ref, bf16[360,128]{1,0:T(8,128)(2,1)S(1)} %collective-permute-done.5.c_ref, ...), custom_call_target="tpu_custom_call" | custom-call | bytes 2000000 | tf_op jit(solution)/shard_map/pallas_call | solution.py:366
  (1 shorter events, 0.0 us)
Async XLA Ops:
  10.2 26.4 %all-to-all-start = ((f32[32,8,128]{2,1,0:T(8,128)}), f32[32,8,128]{2,1,0:T(8,128)S(1)}, u32[]{:S(2)}, u32[]{:S(2)}) async-start(f32[32,8,128]{2,1,0:T(8,128)} %get-tuple-element.18), calls=%async_computation | async-start | bytes 262144 | tf_op jit(solution)/shard_map/all_to_all | solution.py:332
  43.1 24.1 %all-to-all-start.1 = ((bf16[32,128,128]{2,1,0:T(8,128)(2,1)}), bf16[32,128,128]{2,1,0:T(8,128)(2,1)S(1)}, u32[]{:S(2)}, u32[]{:S(2)}) async-start(bf16[32,128,128]{2,1,0:T(8,128)(2,1)} %get-tuple-element.30), calls=%async_computation.1 | async-start | bytes 2097152 | tf_op jit(solution)/shard_map/all_to_all | solution.py:363
  50.0 7.5 %collective-permute-start = (bf16[360,128]{1,0:T(8,128)(2,1)S(1)}, bf16[360,128]{1,0:T(8,128)(2,1)S(1)}, u32[]{:S(2)}, u32[]{:S(2)}) collective-permute-start(bf16[360,128]{1,0:T(8,128)(2,1)S(1)} %get-tuple-element.27), channel_id=1, source_target_pairs={{0,32},{32,64},{64,96},{96,0},{1,33},{33,65},{65,97},{97,1},{2,34}... | collective-permute-start | bytes 276488 | tf_op jit(solution)/shard_map/ppermute | solution.py:293
  50.1 7.4 %collective-permute-start.1 = (bf16[360,128]{1,0:T(8,128)(2,1)S(1)}, bf16[360,128]{1,0:T(8,128)(2,1)S(1)}, u32[]{:S(2)}, u32[]{:S(2)}) collective-permute-start(bf16[360,128]{1,0:T(8,128)(2,1)S(1)} %get-tuple-element.28), channel_id=1, source_target_pairs={{0,64},{32,96},{64,0},{96,32},{1,65},{33,97},{65,1},{97,33},{2,66}... | collective-permute-start | bytes 276488 | tf_op jit(solution)/shard_map/ppermute | solution.py:293
  50.2 7.4 %collective-permute-start.2 = (bf16[360,128]{1,0:T(8,128)(2,1)S(1)}, bf16[360,128]{1,0:T(8,128)(2,1)S(1)}, u32[]{:S(2)}, u32[]{:S(2)}) collective-permute-start(bf16[360,128]{1,0:T(8,128)(2,1)S(1)} %get-tuple-element.29), channel_id=1, source_target_pairs={{0,96},{32,0},{64,32},{96,64},{1,97},{33,1},{65,33},{97,65},{2,98}... | collective-permute-start | bytes 276488 | tf_op jit(solution)/shard_map/ppermute | solution.py:293
  57.7 5.0 %collective-permute-start.3 = (bf16[360,128]{1,0:T(8,128)(2,1)S(1)}, bf16[360,128]{1,0:T(8,128)(2,1)S(1)}, u32[]{:S(2)}, u32[]{:S(2)}) collective-permute-start(bf16[360,128]{1,0:T(8,128)(2,1)S(1)} %shard_map.70.own_ref), channel_id=1, source_target_pairs={{0,32},{32,64},{64,96},{96,0},{1,33},{33,65},{65,97},{97,1},{2,34}... | collective-permute-start | bytes 276488 | tf_op jit(solution)/shard_map/ppermute | solution.py:293
  58.0 7.2 %collective-permute-start.4 = (bf16[360,128]{1,0:T(8,128)(2,1)S(1)}, bf16[360,128]{1,0:T(8,128)(2,1)S(1)}, u32[]{:S(2)}, u32[]{:S(2)}) collective-permute-start(bf16[360,128]{1,0:T(8,128)(2,1)S(1)} %shard_map.70.own_ref), channel_id=1, source_target_pairs={{0,64},{32,96},{64,0},{96,32},{1,65},{33,97},{65,1},{97,33},{2,66}... | collective-permute-start | bytes 276488 | tf_op jit(solution)/shard_map/ppermute | solution.py:293
  61.6 4.6 %collective-permute-start.5 = (bf16[360,128]{1,0:T(8,128)(2,1)S(1)}, bf16[360,128]{1,0:T(8,128)(2,1)S(1)}, u32[]{:S(2)}, u32[]{:S(2)}) collective-permute-start(bf16[360,128]{1,0:T(8,128)(2,1)S(1)} %shard_map.70.own_ref), channel_id=1, source_target_pairs={{0,96},{32,0},{64,32},{96,64},{1,97},{33,1},{65,33},{97,65},{2,98}... | collective-permute-start | bytes 276488 | tf_op jit(solution)/shard_map/ppermute | solution.py:293

commit v4 on v2

v4 whole, which is shorter than its diff:
```python
import jax
import jax.numpy as jnp
from jax import lax
from jax.experimental import pallas as pl
from jax.experimental.pallas import tpu as pltpu
from jax.sharding import PartitionSpec as P

very_low = -1e30
contrast_temp = 0.05
safe_low, safe_high = 1e-12, 1e12
f32, bf16 = jnp.float32, jnp.bfloat16
VMEM = pl.BlockSpec(memory_space=pltpu.VMEM)
ANY = pl.BlockSpec(memory_space=pl.ANY)
B, LQ, LP, D = 8, 32, 180, 128
QT = B * LQ
PT = B * LP
GROUP = 4
turned_dims = (((1,), (1,)), ((), ()))


def iota(shape, dim):
    return lax.broadcasted_iota(jnp.int32, shape, dim)


def exact_dot(a, b):
    return jnp.dot(a, b, precision=lax.Precision.HIGHEST, preferred_element_type=f32)


def own_lanes(blocks):
    return iota((blocks, B, blocks * B), 2) // B == iota((blocks, B, blocks * B), 0)


def pack_means(wide):
    blocks = wide.shape[0]
    count = blocks * B
    pick = (iota((QT, count), 0) // LQ == iota((QT, count), 1) % B).astype(f32)
    sums = exact_dot(wide.reshape(count, QT), pick).reshape(blocks, B, count)
    return jnp.sum(jnp.where(own_lanes(blocks), sums, 0.0), axis=0) / LQ


def unpack(packed):
    count = packed.shape[1]
    blocks = count // B
    pick = (iota((count, QT), 0) % B == iota((count, QT), 1) // LQ).astype(f32)
    spread = jnp.where(own_lanes(blocks), packed[None], 0.0).reshape(count, count)
    return exact_dot(spread, pick).reshape(blocks, B, QT)


def list_tasks(mask_s, order):
    blocks = mask_s.shape[0]
    count = jnp.int32(0)
    for wanted in (True, False):
        for k in range(blocks):
            here = (mask_s[k] > 0) == wanted

            @pl.when(here)
            def _(k=k, count=count):
                order[count] = k

            count = count + here.astype(jnp.int32)
        if wanted:
            active = count
    return active


def block_rows(q_ref, k):
    return q_ref[pl.ds(pl.multiple_of(k * QT, QT), QT), :]


def fetch_all(pairs, sems):
    fetches = [pltpu.make_async_copy(src, dst, sems.at[i]) for i, (src, dst) in enumerate(pairs)]
    for fetch in fetches:
        fetch.start()
    return [fetch.wait for fetch in fetches]


def task_sim(p_ref, q_ref, k):
    return lax.dot_general(p_ref[...], block_rows(q_ref, k), turned_dims, preferred_element_type=f32)


def scores_kernel(mask_hbm, pos_hbm, q_hbm, p_hbm, send_ref, logit_ref, tot_ref, q_ref, p_ref, *rest):
    blocks = tot_ref.shape[0]
    groups = blocks // GROUP
    scaled_refs, (mask_s, pos_ref, order, top_ref, sim_ref, sems) = rest[:groups], rest[groups:]
    pairs = ((mask_hbm, mask_s), (pos_hbm, pos_ref), (p_hbm, p_ref), (q_hbm, q_ref))
    mask_wait, pos_wait, p_wait, q_wait = fetch_all(pairs, sems)
    top_ref[...] = jnp.zeros_like(top_ref)
    tot_ref[...] = jnp.ones_like(tot_ref)
    mask_wait()
    count = list_tasks(mask_s, order)
    pos_wait()
    p_wait()
    q_wait()
    for group, scaled_ref in enumerate(scaled_refs):

        @pl.when(count > group * GROUP)
        def _(group=group, scaled_ref=scaled_ref):
            for i in range(GROUP):
                k = order[group * GROUP + i]
                scaled = jnp.exp(task_sim(p_ref, q_ref, k))
                scaled_ref[i] = scaled
                tot_ref[k] = jnp.sum(scaled.reshape(LP, B, QT), axis=0)

    safe = (jnp.min(tot_ref[...]) > safe_low) & (jnp.max(tot_ref[...]) < safe_high)

    @pl.when(jnp.logical_not(safe))
    def _():
        for group, scaled_ref in enumerate(scaled_refs):

            @pl.when(count > group * GROUP)
            def _(group=group, scaled_ref=scaled_ref):
                @pl.loop(0, GROUP)
                def _(i):
                    k = order[group * GROUP + i]
                    sim_ref[...] = task_sim(p_ref, q_ref, k)
                    sim = sim_ref[...].reshape(LP, B, QT)
                    top = jnp.max(sim, axis=0)
                    scaled = jnp.exp(sim - top[None])
                    top_ref[k] = top
                    tot_ref[k] = jnp.sum(scaled, axis=0)
                    scaled_ref[i] = scaled.reshape(PT, QT)

    lane_block = iota((B, blocks * B), 1) // B
    active = jnp.zeros((B, blocks * B), jnp.int32)
    for k in range(blocks):
        active = jnp.where(lane_block == k, mask_s[k], active)
    active = active > 0
    score = pack_means(top_ref[...] + jnp.log(tot_ref[...]))
    logit = jnp.where(active, score / contrast_temp, very_low)
    logit_ref[...] = logit
    positive = (pos_ref[...] == iota(logit.shape, 0) + lax.axis_index("pa") * B) & active
    local_top = jnp.max(logit, axis=0, keepdims=True)
    scaled = jnp.where(active, jnp.exp(logit - local_top), 0.0)
    local_total = jnp.sum(scaled, axis=0, keepdims=True)
    local_pos = jnp.sum(jnp.where(positive, logit, 0.0), axis=0, keepdims=True)
    row = iota(logit.shape, 0)
    send = jnp.where(row == 0, local_top, jnp.where(row == 1, local_total, local_pos))
    send_ref[...] = jnp.where(row < 3, send, 0.0)


def merged(*stats):
    row = iota(stats[0].shape, 0)
    top = stats[0][:1]
    for x in stats[1:]:
        top = jnp.maximum(top, x[:1])
    total = sum(x * jnp.where(row == 1, jnp.exp(x[:1] - top), 1.0) for x in stats)
    return jnp.where(row == 0, top, total)


def grads_kernel(
    mask_hbm, pos_ref, stat0_ref, stat1_ref, stat2_ref, stat3_ref, logit_ref, tot_ref, q_ref, turn_ref, *rest
):
    blocks = tot_ref.shape[0]
    groups = blocks // GROUP
    scaled_refs, rest = rest[:groups], rest[groups:]
    loss_ref, gq_ref, own_ref, send1_ref, send2_ref, send3_ref, *rest = rest
    mask_s, order, weight_ref, gp_ref, dsim_ref, sem = rest
    fetch = pltpu.make_async_copy(mask_hbm, mask_s, sem)
    fetch.start()
    stat = merged(stat0_ref[...], stat1_ref[...], stat2_ref[...], stat3_ref[...])
    glob_top, glob_total, glob_pos = stat[:1], stat[1:2], stat[2:3]
    loss_ref[...] = glob_top + jnp.log(glob_total) - glob_pos
    logit = logit_ref[...]
    active = logit > very_low / 2
    positive = (pos_ref[...] == iota(logit.shape, 0) + lax.axis_index("pa") * B) & active
    prob = jnp.where(active, jnp.exp(logit - glob_top) / glob_total, 0.0)
    coef = (prob - positive.astype(f32)) / (contrast_temp * LQ)
    weight_ref[...] = unpack(coef) / tot_ref[...]
    gp_ref[...] = jnp.zeros_like(gp_ref)
    fetch.wait()
    count = list_tasks(mask_s, order)
    for group, scaled_ref in enumerate(scaled_refs):

        @pl.when(count > group * GROUP)
        def _(group=group, scaled_ref=scaled_ref):
            tasks = [order[group * GROUP + i] for i in range(GROUP)]
            for i, k in enumerate(tasks):
                dsim = (scaled_ref[i].reshape(LP, B, QT) * weight_ref[k][None]).astype(bf16)
                dsim_ref[:, i * QT : (i + 1) * QT] = dsim.reshape(PT, QT)
            queries = jnp.concatenate([block_rows(q_ref, k) for k in tasks], axis=0)
            gp_ref[...] += jnp.dot(dsim_ref[...], queries, preferred_element_type=f32)
            turned = jnp.dot(turn_ref[...], dsim_ref[...], preferred_element_type=f32).astype(bf16)
            for i, k in enumerate(tasks):
                for j in range(2):
                    start = i * QT + j * D
                    gq_ref[2 * k + j] = turned[:, start : start + D]

        @pl.when(count <= group * GROUP)
        def _(group=group):
            for i in range(GROUP):
                for j in range(2):
                    gq_ref[2 * order[group * GROUP + i] + j] = jnp.zeros((D, 4 * LQ), bf16)

    mine = lax.axis_index("pb")
    piece = PT // 4

    def rows_of(owner):
        return gp_ref[pl.ds(pl.multiple_of(owner * piece, B), piece), :]

    own_ref[...] = rows_of(mine)
    for s, send in ((1, send1_ref), (2, send2_ref), (3, send3_ref)):
        send[...] = rows_of(lax.rem(mine + s, 4)).astype(bf16)


def turn_kernel(p_ref, out_ref):
    out_ref[...] = p_ref[...].astype(f32).T.astype(bf16)


def sum_kernel(own_ref, a_ref, b_ref, c_ref, out_ref):
    total = own_ref[...] + a_ref[...].astype(f32) + b_ref[...].astype(f32) + c_ref[...].astype(f32)
    out_ref[...] = total.astype(bf16)


def last_kernel(loss_ref, own_ref, a_ref, b_ref, c_ref, terms_ref, gp_ref, gq_ref, rows_ref):
    mine = lax.axis_index("pb")
    piece = PT // 4
    for s, ref in ((0, own_ref), (1, a_ref), (2, b_ref), (3, c_ref)):
        owner = lax.rem(mine + 4 - s, 4)
        gp_ref[pl.ds(pl.multiple_of(owner * piece, B), piece), :] = ref[...].astype(f32)
    total = terms_ref[0].astype(f32)
    for i in range(1, terms_ref.shape[0]):
        total += terms_ref[i].astype(f32)
    gq_ref[...] = total.T
    count, own = loss_ref.shape[1], rows_ref.shape[1]
    pick = iota((count, own), 0) == iota((count, own), 1) + own * lax.axis_index("pa")
    rows_ref[...] = exact_dot(loss_ref[...], pick.astype(f32))


def in_hbm(x):
    return pltpu.with_memory_space_constraint(x, pltpu.HBM)


def call(kernel, out, specs, scratch=(), vmem=16 << 20, flops=0, nbytes=0):
    return pl.pallas_call(
        kernel,
        out_shape=out,
        in_specs=list(specs),
        out_specs=jax.tree.map(lambda _: VMEM, out),
        scratch_shapes=list(scratch),
        compiler_params=pltpu.CompilerParams(vmem_limit_bytes=vmem),
        cost_estimate=pl.CostEstimate(flops=flops, bytes_accessed=nbytes, transcendentals=0),
    )


def turn(x, s):
    return lax.ppermute(x, "pb", [(i, (i + s) % 4) for i in range(4)])


def turn_digit(x, s, unit):
    def to(i):
        return i + unit * ((i // unit + s) % 4 - i // unit % 4)

    return lax.ppermute(x, "pa", [(i, to(i)) for i in range(lax.axis_size("pa"))])


def on_device(queries, passages, pair_mask, positive):
    rows = queries.shape[0]
    blocks = rows // B
    groups = blocks // GROUP
    peers = lax.axis_size("pa")
    own_rows = rows // peers
    shape = jax.ShapeDtypeStruct
    flat_q = queries.reshape(rows * LQ, D)
    flat_p = jnp.swapaxes(passages, 0, 1).reshape(PT, D)
    mask = pair_mask.reshape(blocks)
    pos = positive.reshape(1, rows)
    ints = pltpu.SMEM((blocks,), jnp.int32)
    mask, flat_q, flat_p = (in_hbm(x) for x in (mask, flat_q, flat_p))
    wide = shape((blocks, B, QT), f32)
    packed = shape((B, rows), f32)
    send, logit, tot, near_q, near_p, *scaled = call(
        scores_kernel,
        (
            packed,
            packed,
            wide,
            shape((rows * LQ, D), bf16),
            shape((PT, D), bf16),
            *(shape((GROUP, PT, QT), f32),) * groups,
        ),
        (ANY,) * 4,
        [
            ints,
            pltpu.VMEM((1, rows), jnp.int32),
            ints,
            pltpu.VMEM((blocks, B, QT), f32),
            pltpu.VMEM((PT, QT), f32),
            pltpu.SemaphoreType.DMA((4,)),
        ],
        flops=2_000_000_000,
        nbytes=3_000_000,
    )(mask, in_hbm(pos), flat_q, flat_p)
    stat = merged(send, lax.ppermute(send, "pa", [(i, i ^ 1) for i in range(peers)]))
    stat = merged(stat, *(turn_digit(stat, s, 2) for s in (1, 2, 3)))
    stats = (stat, *(turn_digit(stat, s, 8) for s in (3, 2, 1)))
    turned_p = call(turn_kernel, shape((D, PT), bf16), (VMEM,), nbytes=100_000)(near_p)
    piece = shape((PT // 4, D), bf16)
    loss, gq, own, send1, send2, send3 = call(
        grads_kernel,
        (shape((1, rows), f32), shape((peers, D, own_rows * LQ), bf16), shape((PT // 4, D), f32), piece, piece, piece),
        (ANY,) + (VMEM,) * (9 + groups),
        [
            ints,
            ints,
            pltpu.VMEM((blocks, B, QT), f32),
            pltpu.VMEM((PT, D), f32),
            pltpu.VMEM((PT, GROUP * QT), bf16),
            pltpu.SemaphoreType.DMA,
        ],
        flops=5_000_000_000,
        nbytes=5_000_000,
    )(mask, pos, *stats, logit, tot, near_q, turned_p, *scaled)
    sends = {1: send1, 2: send2, 3: send3}
    got = [turn(sends[s], s) for s in (1, 2, 3)]
    gq_terms = lax.all_to_all(gq, "pa", 0, 0, tiled=True)
    mine = call(sum_kernel, piece, (VMEM,) * 4, nbytes=1_000_000)(own, *got)
    others = [turn(mine, s) for s in (1, 2, 3)]
    flat, grad_q, loss_rows = call(
        last_kernel,
        (shape((PT, D), f32), shape((own_rows * LQ, D), f32), shape((1, own_rows), f32)),
        (VMEM,) * 6,
        nbytes=2_000_000,
    )(loss, mine, *others, gq_terms)
    grad_p = jnp.swapaxes(flat.reshape(LP, B, D), 0, 1)
    return loss_rows.reshape(own_rows), grad_q.reshape(own_rows, LQ, D), grad_p


def solution(mesh):
    placed = (P("pb", None, None), P("pa", None, None), P("pb", "pa"), P("pb"))
    return jax.shard_map(
        on_device,
        mesh=mesh,
        in_specs=placed,
        out_specs=(P(("pb", "pa")), P(("pb", "pa"), None, None), P("pa", None, None)),
        check_vma=False,
    )
```

time: 64.5 us -> 66.7 us (1.034)
  blocking collectives: 22.2 us -> 0 us
  Pallas kernels: 7.53 us -> 20.7 us
  waiting for transfers between devices: 8.18 us -> 19.7 us
  local copies, waits for them, and re-layouts: 3.45 us -> 0.01 us
  starting transfers between devices: 22.3 us -> 25.2 us
    all_to_all x1 -> x0, blocking collectives: 22.2 us -> none  [on_device(): stats = lax.all_to_all(send, 'pa', 0, 0, tiled=True)]
    ppermute x0 -> x7, starting transfers between devices: none -> 13.9 us  [the longest x6 13.8 us: turn_digit(): lax.ppermute(x, 'pa', [(i, to(i)) for i in range(lax.axis_size('pa'))])]
    pallas_call x5, Pallas kernels: 7.53 us -> 20.7 us  [the longest x1 13.1 us: on_device(): call(scores_kernel, (packed, packed, wide, shape((rows * LQ, D), bf16), s...]
    ppermute x0 -> x7, waiting for transfers between devices: none -> 8.02 us  [the longest x6 6.88 us: turn_digit(): lax.ppermute(x, 'pa', [(i, to(i)) for i in range(lax.axis_size('pa'))])]
    all_to_all x1, starting transfers between devices: 10.9 us -> 4.69 us  [on_device(): gq_terms = lax.all_to_all(gq, 'pa', 0, 0, tiled=True)]
    ppermute x6, starting transfers between devices: 11.4 us -> 6.65 us  [turn(): return lax.ppermute(x, 'pb', [(i, (i + s) % 4) for i in range(4)])]
    ppermute x6, waiting for transfers between devices: 8.18 us -> 11.7 us  [turn(): return lax.ppermute(x, 'pb', [(i, (i + s) % 4) for i in range(4)])]
    unnamed x8 -> x2, local copies, waits for them, and re-layouts: 2.87 us -> 0.01 us
  transfers between devices with their start and end apart: 7 -> 14, of which waited for: 5 -> 10; matrix products, arithmetic and copies ran while one was open for 1% -> 0% of each run, Pallas kernels for 2% -> 0%
where the time goes in v4:
time: 66.7 us; the launch traced here: 66.5 us
  starting transfers between devices  25.2 us (38%)
  Pallas kernels  20.7 us (31%)
  waiting for transfers between devices  19.7 us (30%)
  between operations  0.73 us (1%)
    ppermute x6, starting transfers between devices, turn_digit(): lax.ppermute(x, 'pa', [(i, to(i)) for i in range(lax.axis_size('pa'))])  13.8 us
    pallas_call x1, Pallas kernels, on_device(): call(scores_kernel, (packed, packed, wide, shape((rows * LQ, D), bf16), s...  13.1 us
    ppermute x6, waiting for transfers between devices, turn(): return lax.ppermute(x, 'pb', [(i, (i + s) % 4) for i in range(4)])  11.7 us
    ppermute x6, waiting for transfers between devices, turn_digit(): lax.ppermute(x, 'pa', [(i, to(i)) for i in range(lax.axis_size('pa'))])  6.88 us
    ppermute x6, starting transfers between devices, turn(): return lax.ppermute(x, 'pb', [(i, (i + s) % 4) for i in range(4)])  6.65 us
    pallas_call x1, Pallas kernels, on_device(): call(grads_kernel, (shape((1, rows), f32), shape((peers, D, own_rows * LQ...  6.3 us
    all_to_all x1, starting transfers between devices, on_device(): gq_terms = lax.all_to_all(gq, 'pa', 0, 0, tiled=True)  4.69 us
  transfers between devices with their start and end apart: 14, of which 10 were waited for; matrix products, arithmetic and copies ran while one was open for 0% of the time, Pallas kernels for 0%

profile of v4, /device:TPU:0, one launch (start us, length us, event | category | flops | bytes accessed | tf_op | source)
XLA Modules:
  0.0 66.5 jit_solution(15566957617334170619)
XLA Ops:
  0.6 0.0 copy-start
  0.6 13.1 %shard_map.67 = (f32[8,128]{1,0:T(8,128)S(1)}, f32[8,128]{1,0:T(8,128)S(1)}, f32[16,8,256]{2,1,0:T(8,128)S(1)}, bf16[4096,128]{1,0:T(8,128)(2,1)S(1)}, bf16[1440...) custom-call(s32[16]{0:T(128)} %bitcast.29, ...), custom_call_target="tpu_custom_call" | custom-call | flops 2000000000 | bytes 3000000 | tf_op jit(solution)/shard_map/pallas_call | solution.py:271
  13.7 0.1 collective-permute-start
  13.8 1.1 %collective-permute-done = f32[8,128]{1,0:T(8,128)S(1)} collective-permute-done((f32[8,128]{1,0:T(8,128)S(1)}, f32[8,128]{1,0:T(8,128)S(1)}, u32[]{:S(2)}, u32[]{:S(2)}) %collective-permute-start) | collective-permute-done | bytes 4128 | tf_op jit(solution)/shard_map/ppermute | solution.py:293
  15.0 0.1 add_select_fusion.1
  15.0 0.0 collective-permute-start.3
  15.1 7.1 %collective-permute-start.2 = (f32[8,128]{1,0:T(8,128)S(1)}, f32[8,128]{1,0:T(8,128)S(1)}, u32[]{:S(2)}, u32[]{:S(2)}) collective-permute-start(f32[8,128]{1,0:T(8,128)S(1)} %add_select_fusion.1), channel_id=1, source_target_pairs={{0,4},{1,5},{2,6},{3,7},{4,0},{5,1},{6,2},{7,3},{8,12},{9,13},{10,... | collective-permute-start | bytes 12296 | tf_op jit(solution)/shard_map/ppermute | solution.py:253
  22.1 1.3 %collective-permute-start.1 = (f32[8,128]{1,0:T(8,128)S(1)}, f32[8,128]{1,0:T(8,128)S(1)}, u32[]{:S(2)}, u32[]{:S(2)}) collective-permute-start(f32[8,128]{1,0:T(8,128)S(1)} %add_select_fusion.1), channel_id=1, source_target_pairs={{0,2},{1,3},{2,4},{3,5},{4,6},{5,7},{6,0},{7,1},{8,10},{9,11},{10,... | collective-permute-start | bytes 12296 | tf_op jit(solution)/shard_map/ppermute | solution.py:253
  23.5 0.0 collective-permute-done.3
  23.5 0.3 collective-permute-done.2
  23.7 3.2 %collective-permute-done.1 = f32[8,128]{1,0:T(8,128)S(1)} collective-permute-done((f32[8,128]{1,0:T(8,128)S(1)}, f32[8,128]{1,0:T(8,128)S(1)}, u32[]{:S(2)}, u32[]{:S(2)}) %collective-permute-start.1) | collective-permute-done | bytes 4128 | tf_op jit(solution)/shard_map/ppermute | solution.py:253
  27.0 0.1 add_select_fusion.stat0_ref
  27.1 2.3 %collective-permute-start.6 = (f32[8,128]{1,0:T(8,128)S(1)}, f32[8,128]{1,0:T(8,128)S(1)}, u32[]{:S(2)}, u32[]{:S(2)}) collective-permute-start(f32[8,128]{1,0:T(8,128)S(1)} %add_select_fusion.stat0_ref), channel_id=1, source_target_pairs={{0,8},{1,9},{2,10},{3,11},{4,12},{5,13},{6,14},{7,15},{8,16},{9,17... | collective-permute-start | bytes 12296 | tf_op jit(solution)/shard_map/ppermute | solution.py:253
  29.3 3.1 %collective-permute-start.5 = (f32[8,128]{1,0:T(8,128)S(1)}, f32[8,128]{1,0:T(8,128)S(1)}, u32[]{:S(2)}, u32[]{:S(2)}) collective-permute-start(f32[8,128]{1,0:T(8,128)S(1)} %add_select_fusion.stat0_ref), channel_id=1, source_target_pairs={{0,16},{1,17},{2,18},{3,19},{4,20},{5,21},{6,22},{7,23},{8,24},{9,... | collective-permute-start | bytes 12296 | tf_op jit(solution)/shard_map/ppermute | solution.py:253
  32.4 0.0 collective-permute-start.4
  32.4 0.2 shard_map.68.turn_ref
  32.6 0.0 collective-permute-done.6.stat3_ref
  32.6 1.8 %collective-permute-done.5.stat2_ref = f32[8,128]{1,0:T(8,128)S(1)} collective-permute-done((f32[8,128]{1,0:T(8,128)S(1)}, f32[8,128]{1,0:T(8,128)S(1)}, u32[]{:S(2)}, u32[]{:S(2)}) %collective-permute-start.5) | collective-permute-done | bytes 4128 | tf_op jit(solution)/shard_map/ppermute | solution.py:253
  34.4 1.6 %collective-permute-done.4.stat1_ref = f32[8,128]{1,0:T(8,128)S(1)} collective-permute-done((f32[8,128]{1,0:T(8,128)S(1)}, f32[8,128]{1,0:T(8,128)S(1)}, u32[]{:S(2)}, u32[]{:S(2)}) %collective-permute-start.4) | collective-permute-done | bytes 4128 | tf_op jit(solution)/shard_map/ppermute | solution.py:253
  36.0 0.0 copy-done
  36.0 6.3 %shard_map.69 = (f32[1,128]{1,0:T(1,128)S(1)}, bf16[32,128,128]{2,1,0:T(8,128)(2,1)}, f32[360,128]{1,0:T(8,128)S(1)}, bf16[360,128]{1,0:T(8,128)(2,1)S(1)}, bf16...) custom-call(s32[16]{0:T(128)} %bitcast.30, s32[1,128]{1,0:T(1,128)S(1)} %bitcast.27, ...), custom_call_target="tpu_custom_call" | custom-call | flops 5000000000 | bytes 5000000 | tf_op jit(solution)/shard_map/pallas_call | solution.py:298
  42.3 4.7 %all-to-all-start = ((bf16[32,128,128]{2,1,0:T(8,128)(2,1)}), bf16[32,128,128]{2,1,0:T(8,128)(2,1)S(1)}, u32[]{:S(2)}, u32[]{:S(2)}) async-start(bf16[32,128,128]{2,1,0:T(8,128)(2,1)} %get-tuple-element.35), calls=%async_computation | async-start | bytes 2097152 | tf_op jit(solution)/shard_map/all_to_all | solution.py:315
  47.0 0.1 collective-permute-start.7
  47.1 0.1 collective-permute-start.8
  47.2 3.1 %collective-permute-start.9 = (bf16[360,128]{1,0:T(8,128)(2,1)S(1)}, bf16[360,128]{1,0:T(8,128)(2,1)S(1)}, u32[]{:S(2)}, u32[]{:S(2)}) collective-permute-start(bf16[360,128]{1,0:T(8,128)(2,1)S(1)} %get-tuple-element.34), channel_id=1, source_target_pairs={{0,96},{32,0},{64,32},{96,64},{1,97},{33,1},{65,33},{97,65},{2,98}... | collective-permute-start | bytes 276488 | tf_op jit(solution)/shard_map/ppermute | solution.py:246
  50.3 4.8 %collective-permute-done.7.a_ref = bf16[360,128]{1,0:T(8,128)(2,1)S(1)} collective-permute-done((bf16[360,128]{1,0:T(8,128)(2,1)S(1)}, bf16[360,128]{1,0:T(8,128)(2,1)S(1)}, u32[]{:S(2)}, u32[]{:S(2)}) %collective-permute-start.7) | collective-permute-done | bytes 92192 | tf_op jit(solution)/shard_map/ppermute | solution.py:246
  55.1 0.0 collective-permute-done.8.b_ref
  55.1 0.6 collective-permute-done.9.c_ref
  55.8 2.4 %collective-permute-start.12 = (bf16[360,128]{1,0:T(8,128)(2,1)S(1)}, bf16[360,128]{1,0:T(8,128)(2,1)S(1)}, u32[]{:S(2)}, u32[]{:S(2)}) collective-permute-start(bf16[360,128]{1,0:T(8,128)(2,1)S(1)} %shard_map.70.own_ref), channel_id=1, source_target_pairs={{0,96},{32,0},{64,32},{96,64},{1,97},{33,1},{65,33},{97,65},{2,98}... | collective-permute-start | bytes 276488 | tf_op jit(solution)/shard_map/ppermute | solution.py:246
  58.2 0.0 collective-permute-start.11
  58.3 0.9 %collective-permute-start.10 = (bf16[360,128]{1,0:T(8,128)(2,1)S(1)}, bf16[360,128]{1,0:T(8,128)(2,1)S(1)}, u32[]{:S(2)}, u32[]{:S(2)}) collective-permute-start(bf16[360,128]{1,0:T(8,128)(2,1)S(1)} %shard_map.70.own_ref), channel_id=1, source_target_pairs={{0,32},{32,64},{64,96},{96,0},{1,33},{33,65},{65,97},{97,1},{2,34}... | collective-permute-start | bytes 276488 | tf_op jit(solution)/shard_map/ppermute | solution.py:246
  59.2 2.9 %collective-permute-done.12.c_ref = bf16[360,128]{1,0:T(8,128)(2,1)S(1)} collective-permute-done((bf16[360,128]{1,0:T(8,128)(2,1)S(1)}, bf16[360,128]{1,0:T(8,128)(2,1)S(1)}, u32[]{:S(2)}, u32[]{:S(2)}) %collective-permute-start.12) | collective-permute-done | bytes 92192 | tf_op jit(solution)/shard_map/ppermute | solution.py:246
  62.0 2.8 %collective-permute-done.11.b_ref = bf16[360,128]{1,0:T(8,128)(2,1)S(1)} collective-permute-done((bf16[360,128]{1,0:T(8,128)(2,1)S(1)}, bf16[360,128]{1,0:T(8,128)(2,1)S(1)}, u32[]{:S(2)}, u32[]{:S(2)}) %collective-permute-start.11) | collective-permute-done | bytes 92192 | tf_op jit(solution)/shard_map/ppermute | solution.py:246
  64.8 0.6 collective-permute-done.10.a_ref
  65.4 0.0 all-to-all-done.terms_ref
  65.4 1.1 %shard_map.71 = (f32[1440,128]{1,0:T(8,128)}, f32[128,128]{1,0:T(8,128)}, f32[1,4]{1,0:T(1,128)}) custom-call(f32[1,128]{1,0:T(1,128)S(1)} %get-tuple-element.30.loss_ref, bf16[360,128]{1,0:T(8,128)(2,1)S(1)} %shard_map.70.own_ref, bf16[360,128]{1,0:T(8,128)(2,1)S(1)} %collective-permute-done.10.a_ref, bf16[360,128]{1,0:T(8,128)(2,1)S(1)} %collective-permute-done.11.b_ref, ...), custom_call_target="tpu_custom_call" | custom-call | bytes 2000000 | tf_op jit(solution)/shard_map/pallas_call | solution.py:318
  (5 shorter events, 0.1 us)
Async XLA Ops:
  0.6 35.4 %copy-start = (s32[128]{0:T(128)S(1)}, s32[128]{0:T(128)}, u32[]{:S(2)}) copy-start(s32[128]{0:T(128)} %param.7) | copy-start | bytes 1540
  13.7 1.2 %collective-permute-start = (f32[8,128]{1,0:T(8,128)S(1)}, f32[8,128]{1,0:T(8,128)S(1)}, u32[]{:S(2)}, u32[]{:S(2)}) collective-permute-start(f32[8,128]{1,0:T(8,128)S(1)} %get-tuple-element.21), channel_id=1, source_target_pairs={{0,1},{1,0},{2,3},{3,2},{4,5},{5,4},{6,7},{7,6},{8,9},{9,8},{10,11... | collective-permute-start | bytes 12296 | tf_op jit(solution)/shard_map/ppermute | solution.py:293
  15.0 8.4 %collective-permute-start.3 = (f32[8,128]{1,0:T(8,128)S(1)}, f32[8,128]{1,0:T(8,128)S(1)}, u32[]{:S(2)}, u32[]{:S(2)}) collective-permute-start(f32[8,128]{1,0:T(8,128)S(1)} %add_select_fusion.1), channel_id=1, source_target_pairs={{0,6},{1,7},{2,0},{3,1},{4,2},{5,3},{6,4},{7,5},{8,14},{9,15},{10,... | collective-permute-start | bytes 12296 | tf_op jit(solution)/shard_map/ppermute | solution.py:253
  15.1 8.7 %collective-permute-start.2 = (f32[8,128]{1,0:T(8,128)S(1)}, f32[8,128]{1,0:T(8,128)S(1)}, u32[]{:S(2)}, u32[]{:S(2)}) collective-permute-start(f32[8,128]{1,0:T(8,128)S(1)} %add_select_fusion.1), channel_id=1, source_target_pairs={{0,4},{1,5},{2,6},{3,7},{4,0},{5,1},{6,2},{7,3},{8,12},{9,13},{10,... | collective-permute-start | bytes 12296 | tf_op jit(solution)/shard_map/ppermute | solution.py:253
  22.1 4.8 %collective-permute-start.1 = (f32[8,128]{1,0:T(8,128)S(1)}, f32[8,128]{1,0:T(8,128)S(1)}, u32[]{:S(2)}, u32[]{:S(2)}) collective-permute-start(f32[8,128]{1,0:T(8,128)S(1)} %add_select_fusion.1), channel_id=1, source_target_pairs={{0,2},{1,3},{2,4},{3,5},{4,6},{5,7},{6,0},{7,1},{8,10},{9,11},{10,... | collective-permute-start | bytes 12296 | tf_op jit(solution)/shard_map/ppermute | solution.py:253
  27.1 5.6 %collective-permute-start.6 = (f32[8,128]{1,0:T(8,128)S(1)}, f32[8,128]{1,0:T(8,128)S(1)}, u32[]{:S(2)}, u32[]{:S(2)}) collective-permute-start(f32[8,128]{1,0:T(8,128)S(1)} %add_select_fusion.stat0_ref), channel_id=1, source_target_pairs={{0,8},{1,9},{2,10},{3,11},{4,12},{5,13},{6,14},{7,15},{8,16},{9,17... | collective-permute-start | bytes 12296 | tf_op jit(solution)/shard_map/ppermute | solution.py:253
  29.3 5.1 %collective-permute-start.5 = (f32[8,128]{1,0:T(8,128)S(1)}, f32[8,128]{1,0:T(8,128)S(1)}, u32[]{:S(2)}, u32[]{:S(2)}) collective-permute-start(f32[8,128]{1,0:T(8,128)S(1)} %add_select_fusion.stat0_ref), channel_id=1, source_target_pairs={{0,16},{1,17},{2,18},{3,19},{4,20},{5,21},{6,22},{7,23},{8,24},{9,... | collective-permute-start | bytes 12296 | tf_op jit(solution)/shard_map/ppermute | solution.py:253
  32.4 3.6 %collective-permute-start.4 = (f32[8,128]{1,0:T(8,128)S(1)}, f32[8,128]{1,0:T(8,128)S(1)}, u32[]{:S(2)}, u32[]{:S(2)}) collective-permute-start(f32[8,128]{1,0:T(8,128)S(1)} %add_select_fusion.stat0_ref), channel_id=1, source_target_pairs={{0,24},{1,25},{2,26},{3,27},{4,28},{5,29},{6,30},{7,31},{8,0},{9,1... | collective-permute-start | bytes 12296 | tf_op jit(solution)/shard_map/ppermute | solution.py:253
  42.3 23.1 %all-to-all-start = ((bf16[32,128,128]{2,1,0:T(8,128)(2,1)}), bf16[32,128,128]{2,1,0:T(8,128)(2,1)S(1)}, u32[]{:S(2)}, u32[]{:S(2)}) async-start(bf16[32,128,128]{2,1,0:T(8,128)(2,1)} %get-tuple-element.35), calls=%async_computation | async-start | bytes 2097152 | tf_op jit(solution)/shard_map/all_to_all | solution.py:315
  47.0 8.1 %collective-permute-start.7 = (bf16[360,128]{1,0:T(8,128)(2,1)S(1)}, bf16[360,128]{1,0:T(8,128)(2,1)S(1)}, u32[]{:S(2)}, u32[]{:S(2)}) collective-permute-start(bf16[360,128]{1,0:T(8,128)(2,1)S(1)} %get-tuple-element.32), channel_id=1, source_target_pairs={{0,32},{32,64},{64,96},{96,0},{1,33},{33,65},{65,97},{97,1},{2,34}... | collective-permute-start | bytes 276488 | tf_op jit(solution)/shard_map/ppermute | solution.py:246
  47.1 8.0 %collective-permute-start.8 = (bf16[360,128]{1,0:T(8,128)(2,1)S(1)}, bf16[360,128]{1,0:T(8,128)(2,1)S(1)}, u32[]{:S(2)}, u32[]{:S(2)}) collective-permute-start(bf16[360,128]{1,0:T(8,128)(2,1)S(1)} %get-tuple-element.33), channel_id=1, source_target_pairs={{0,64},{32,96},{64,0},{96,32},{1,65},{33,97},{65,1},{97,33},{2,66}... | collective-permute-start | bytes 276488 | tf_op jit(solution)/shard_map/ppermute | solution.py:246
  47.2 8.5 %collective-permute-start.9 = (bf16[360,128]{1,0:T(8,128)(2,1)S(1)}, bf16[360,128]{1,0:T(8,128)(2,1)S(1)}, u32[]{:S(2)}, u32[]{:S(2)}) collective-permute-start(bf16[360,128]{1,0:T(8,128)(2,1)S(1)} %get-tuple-element.34), channel_id=1, source_target_pairs={{0,96},{32,0},{64,32},{96,64},{1,97},{33,1},{65,33},{97,65},{2,98}... | collective-permute-start | bytes 276488 | tf_op jit(solution)/shard_map/ppermute | solution.py:246
  55.8 6.2 %collective-permute-start.12 = (bf16[360,128]{1,0:T(8,128)(2,1)S(1)}, bf16[360,128]{1,0:T(8,128)(2,1)S(1)}, u32[]{:S(2)}, u32[]{:S(2)}) collective-permute-start(bf16[360,128]{1,0:T(8,128)(2,1)S(1)} %shard_map.70.own_ref), channel_id=1, source_target_pairs={{0,96},{32,0},{64,32},{96,64},{1,97},{33,1},{65,33},{97,65},{2,98}... | collective-permute-start | bytes 276488 | tf_op jit(solution)/shard_map/ppermute | solution.py:246
  58.2 6.6 %collective-permute-start.11 = (bf16[360,128]{1,0:T(8,128)(2,1)S(1)}, bf16[360,128]{1,0:T(8,128)(2,1)S(1)}, u32[]{:S(2)}, u32[]{:S(2)}) collective-permute-start(bf16[360,128]{1,0:T(8,128)(2,1)S(1)} %shard_map.70.own_ref), channel_id=1, source_target_pairs={{0,64},{32,96},{64,0},{96,32},{1,65},{33,97},{65,1},{97,33},{2,66}... | collective-permute-start | bytes 276488 | tf_op jit(solution)/shard_map/ppermute | solution.py:246
  58.3 7.2 %collective-permute-start.10 = (bf16[360,128]{1,0:T(8,128)(2,1)S(1)}, bf16[360,128]{1,0:T(8,128)(2,1)S(1)}, u32[]{:S(2)}, u32[]{:S(2)}) collective-permute-start(bf16[360,128]{1,0:T(8,128)(2,1)S(1)} %shard_map.70.own_ref), channel_id=1, source_target_pairs={{0,32},{32,64},{64,96},{96,0},{1,33},{33,65},{65,97},{97,1},{2,34}... | collective-permute-start | bytes 276488 | tf_op jit(solution)/shard_map/ppermute | solution.py:246

commit v5 on v4

--- a/solution.py
+++ b/solution.py
@@ -153,7 +153,7 @@
     blocks = tot_ref.shape[0]
     groups = blocks // GROUP
     scaled_refs, rest = rest[:groups], rest[groups:]
-    loss_ref, gq_ref, own_ref, send1_ref, send2_ref, send3_ref, *rest = rest
+    loss_ref, keep_ref, give_ref, own_ref, send1_ref, send2_ref, send3_ref, *rest = rest
     mask_s, order, weight_ref, gp_ref, dsim_ref, sem = rest
     fetch = pltpu.make_async_copy(mask_hbm, mask_s, sem)
     fetch.start()
@@ -169,6 +169,7 @@
     gp_ref[...] = jnp.zeros_like(gp_ref)
     fetch.wait()
     count = list_tasks(mask_s, order)
+    core = lax.rem(lax.axis_index("pa"), 2)
     for group, scaled_ref in enumerate(scaled_refs):
 
         @pl.when(count > group * GROUP)
@@ -179,17 +180,17 @@
                 dsim_ref[:, i * QT : (i + 1) * QT] = dsim.reshape(PT, QT)
             queries = jnp.concatenate([block_rows(q_ref, k) for k in tasks], axis=0)
             gp_ref[...] += jnp.dot(dsim_ref[...], queries, preferred_element_type=f32)
-            turned = jnp.dot(turn_ref[...], dsim_ref[...], preferred_element_type=f32).astype(bf16)
+            turned = jnp.dot(turn_ref[...], dsim_ref[...], preferred_element_type=f32)
             for i, k in enumerate(tasks):
-                for j in range(2):
-                    start = i * QT + j * D
-                    gq_ref[2 * k + j] = turned[:, start : start + D]
+                first, second = (turned[:, i * QT + j * D : i * QT + (j + 1) * D] for j in range(2))
+                keep_ref[k] = jnp.where(core == 0, first, second)
+                give_ref[k] = jnp.where(core == 0, second, first).astype(bf16)
 
         @pl.when(count <= group * GROUP)
         def _(group=group):
             for i in range(GROUP):
-                for j in range(2):
-                    gq_ref[2 * order[group * GROUP + i] + j] = jnp.zeros((D, 4 * LQ), bf16)
+                keep_ref[order[group * GROUP + i]] = jnp.zeros(keep_ref.shape[1:], f32)
+                give_ref[order[group * GROUP + i]] = jnp.zeros(give_ref.shape[1:], bf16)
 
     mine = lax.axis_index("pb")
     piece = PT // 4
@@ -209,6 +210,10 @@
 def sum_kernel(own_ref, a_ref, b_ref, c_ref, out_ref):
     total = own_ref[...] + a_ref[...].astype(f32) + b_ref[...].astype(f32) + c_ref[...].astype(f32)
     out_ref[...] = total.astype(bf16)
+
+
+def both_kernel(keep_ref, got_ref, out_ref):
+    out_ref[...] = (keep_ref[...] + got_ref[...].astype(f32)).astype(bf16)
 
 
 def last_kernel(loss_ref, own_ref, a_ref, b_ref, c_ref, terms_ref, gp_ref, gq_ref, rows_ref):
@@ -295,9 +300,18 @@
     stats = (stat, *(turn_digit(stat, s, 8) for s in (3, 2, 1)))
     turned_p = call(turn_kernel, shape((D, PT), bf16), (VMEM,), nbytes=100_000)(near_p)
     piece = shape((PT // 4, D), bf16)
-    loss, gq, own, send1, send2, send3 = call(
+    half = shape((blocks, D, own_rows * LQ), bf16)
+    loss, keep, give, own, send1, send2, send3 = call(
         grads_kernel,
-        (shape((1, rows), f32), shape((peers, D, own_rows * LQ), bf16), shape((PT // 4, D), f32), piece, piece, piece),
+        (
+            shape((1, rows), f32),
+            shape((blocks, D, own_rows * LQ), f32),
+            half,
+            shape((PT // 4, D), f32),
+            piece,
+            piece,
+            piece,
+        ),
         (ANY,) + (VMEM,) * (9 + groups),
         [
             ints,
@@ -312,8 +326,11 @@
     )(mask, pos, *stats, logit, tot, near_q, turned_p, *scaled)
     sends = {1: send1, 2: send2, 3: send3}
     got = [turn(sends[s], s) for s in (1, 2, 3)]
-    gq_terms = lax.all_to_all(gq, "pa", 0, 0, tiled=True)
-    mine = call(sum_kernel, piece, (VMEM,) * 4, nbytes=1_000_000)(own, *got)
+    got_half = lax.ppermute(give, "pa", [(i, i ^ 1) for i in range(peers)])
+    both = call(both_kernel, half, (VMEM,) * 2, flops=10_000_000_000)(keep, got_half)
+    same_core = [list(range(core, peers, 2)) for core in range(2)]
+    gq_terms = lax.all_to_all(both, "pa", 0, 0, axis_index_groups=same_core, tiled=True)
+    mine = call(sum_kernel, piece, (VMEM,) * 4, flops=30_000_000_000)(own, *got)
     others = [turn(mine, s) for s in (1, 2, 3)]
     flat, grad_q, loss_rows = call(
         last_kernel,

time: 66.7 us -> 63.4 us (0.951)
  starting transfers between devices: 25.2 us -> 30.9 us
  Pallas kernels: 20.7 us -> 15.5 us
  waiting for transfers between devices: 19.7 us -> 15.6 us
    ppermute x6, waiting for transfers between devices: 11.7 us -> 4.49 us  [turn(): return lax.ppermute(x, 'pb', [(i, (i + s) % 4) for i in range(4)])]
    ppermute x1, starting transfers between devices: 0.09 us -> 6.56 us  [on_device(): lax.ppermute(send, 'pa', [(i, i ^ 1) for i in range(peers)])]
    pallas_call x1, Pallas kernels: 13.1 us -> 9.36 us  [on_device(): call(scores_kernel, (packed, packed, wide, shape((rows * LQ, D), bf16), s...]
    ppermute x6, starting transfers between devices: 13.8 us -> 10.7 us  [turn_digit(): lax.ppermute(x, 'pa', [(i, to(i)) for i in range(lax.axis_size('pa'))])]
    all_to_all x1, waiting for transfers between devices: 0.01 us -> 2.6 us  [on_device(): lax.all_to_all(both, 'pa', 0, 0, axis_index_groups=same_core, tiled=True)]
    pallas_call x2 -> x3, Pallas kernels: 6.35 us -> 4.95 us  [the longest x1 3.99 us: on_device(): call(grads_kernel, (shape((1, rows), f32), shape((blocks, D, own_rows * L...]
    all_to_all x1, starting transfers between devices: 4.69 us -> 5.87 us  [on_device(): lax.all_to_all(both, 'pa', 0, 0, axis_index_groups=same_core, tiled=True)]
    ppermute x6, starting transfers between devices: 6.65 us -> 7.7 us  [turn(): return lax.ppermute(x, 'pb', [(i, (i + s) % 4) for i in range(4)])]
  transfers between devices with their start and end apart: 14 -> 15, of which waited for: 10 -> 9; matrix products, arithmetic and copies ran while one was open for 0% -> 0% of each run, Pallas kernels for 0% -> 2%
where the time goes in v5:
time: 63.4 us; the launch traced here: 63 us
  starting transfers between devices  30.9 us (49%)
  waiting for transfers between devices  15.6 us (25%)
  Pallas kernels  15.5 us (24%)
  between operations  0.75 us (1%)
    ppermute x6, starting transfers between devices, turn_digit(): lax.ppermute(x, 'pa', [(i, to(i)) for i in range(lax.axis_size('pa'))])  10.7 us
    pallas_call x1, Pallas kernels, on_device(): call(scores_kernel, (packed, packed, wide, shape((rows * LQ, D), bf16), s...  9.36 us
    ppermute x6, starting transfers between devices, turn(): return lax.ppermute(x, 'pb', [(i, (i + s) % 4) for i in range(4)])  7.7 us
    ppermute x6, waiting for transfers between devices, turn_digit(): lax.ppermute(x, 'pa', [(i, to(i)) for i in range(lax.axis_size('pa'))])  7.7 us
    ppermute x1, starting transfers between devices, on_device(): lax.ppermute(send, 'pa', [(i, i ^ 1) for i in range(peers)])  6.56 us
    all_to_all x1, starting transfers between devices, on_device(): lax.all_to_all(both, 'pa', 0, 0, axis_index_groups=same_core, tiled=True)  5.87 us
    ppermute x6, waiting for transfers between devices, turn(): return lax.ppermute(x, 'pb', [(i, (i + s) % 4) for i in range(4)])  4.49 us
    pallas_call x1, Pallas kernels, on_device(): call(grads_kernel, (shape((1, rows), f32), shape((blocks, D, own_rows * L...  3.99 us
  transfers between devices with their start and end apart: 15, of which 9 were waited for; matrix products, arithmetic and copies ran while one was open for 0% of the time, Pallas kernels for 2%

profile of v5, /device:TPU:0, one launch (start us, length us, event | category | flops | bytes accessed | tf_op | source)
XLA Modules:
  0.0 63.0 jit_solution(7369621778290990311)
XLA Ops:
  0.6 0.0 copy-start
  0.6 9.4 %shard_map.67 = (f32[8,128]{1,0:T(8,128)S(1)}, f32[8,128]{1,0:T(8,128)S(1)}, f32[16,8,256]{2,1,0:T(8,128)S(1)}, bf16[4096,128]{1,0:T(8,128)(2,1)S(1)}, bf16[1440...) custom-call(s32[16]{0:T(128)} %bitcast.29, ...), custom_call_target="tpu_custom_call" | custom-call | flops 2000000000 | bytes 3000000 | tf_op jit(solution)/shard_map/pallas_call | solution.py:276
  10.0 6.6 %collective-permute-start = (f32[8,128]{1,0:T(8,128)S(1)}, f32[8,128]{1,0:T(8,128)S(1)}, u32[]{:S(2)}, u32[]{:S(2)}) collective-permute-start(f32[8,128]{1,0:T(8,128)S(1)} %get-tuple-element.22), channel_id=1, source_target_pairs={{0,1},{1,0},{2,3},{3,2},{4,5},{5,4},{6,7},{7,6},{8,9},{9,8},{10,11... | collective-permute-start | bytes 12296 | tf_op jit(solution)/shard_map/ppermute | solution.py:298
  16.6 0.8 %collective-permute-done = f32[8,128]{1,0:T(8,128)S(1)} collective-permute-done((f32[8,128]{1,0:T(8,128)S(1)}, f32[8,128]{1,0:T(8,128)S(1)}, u32[]{:S(2)}, u32[]{:S(2)}) %collective-permute-start) | collective-permute-done | bytes 4128 | tf_op jit(solution)/shard_map/ppermute | solution.py:298
  17.4 0.1 add_select_fusion.1
  17.5 0.0 collective-permute-start.3
  17.5 4.5 %collective-permute-start.2 = (f32[8,128]{1,0:T(8,128)S(1)}, f32[8,128]{1,0:T(8,128)S(1)}, u32[]{:S(2)}, u32[]{:S(2)}) collective-permute-start(f32[8,128]{1,0:T(8,128)S(1)} %add_select_fusion.1), channel_id=1, source_target_pairs={{0,4},{1,5},{2,6},{3,7},{4,0},{5,1},{6,2},{7,3},{8,12},{9,13},{10,... | collective-permute-start | bytes 12296 | tf_op jit(solution)/shard_map/ppermute | solution.py:258
  22.0 0.0 collective-permute-start.1
  22.0 0.0 collective-permute-done.3
  22.0 1.6 %collective-permute-done.2 = f32[8,128]{1,0:T(8,128)S(1)} collective-permute-done((f32[8,128]{1,0:T(8,128)S(1)}, f32[8,128]{1,0:T(8,128)S(1)}, u32[]{:S(2)}, u32[]{:S(2)}) %collective-permute-start.2) | collective-permute-done | bytes 4128 | tf_op jit(solution)/shard_map/ppermute | solution.py:258
  23.6 3.2 %collective-permute-done.1 = f32[8,128]{1,0:T(8,128)S(1)} collective-permute-done((f32[8,128]{1,0:T(8,128)S(1)}, f32[8,128]{1,0:T(8,128)S(1)}, u32[]{:S(2)}, u32[]{:S(2)}) %collective-permute-start.1) | collective-permute-done | bytes 4128 | tf_op jit(solution)/shard_map/ppermute | solution.py:258
  26.8 0.1 add_select_fusion.stat0_ref
  26.9 0.3 collective-permute-start.6
  27.2 5.4 %collective-permute-start.5 = (f32[8,128]{1,0:T(8,128)S(1)}, f32[8,128]{1,0:T(8,128)S(1)}, u32[]{:S(2)}, u32[]{:S(2)}) collective-permute-start(f32[8,128]{1,0:T(8,128)S(1)} %add_select_fusion.stat0_ref), channel_id=1, source_target_pairs={{0,16},{1,17},{2,18},{3,19},{4,20},{5,21},{6,22},{7,23},{8,24},{9,... | collective-permute-start | bytes 12296 | tf_op jit(solution)/shard_map/ppermute | solution.py:258
  32.6 0.5 collective-permute-start.4
  33.1 0.2 shard_map.68.turn_ref
  33.3 0.0 collective-permute-done.6.stat3_ref
  33.3 0.9 %collective-permute-done.5.stat2_ref = f32[8,128]{1,0:T(8,128)S(1)} collective-permute-done((f32[8,128]{1,0:T(8,128)S(1)}, f32[8,128]{1,0:T(8,128)S(1)}, u32[]{:S(2)}, u32[]{:S(2)}) %collective-permute-start.5) | collective-permute-done | bytes 4128 | tf_op jit(solution)/shard_map/ppermute | solution.py:258
  34.2 2.0 %collective-permute-done.4.stat1_ref = f32[8,128]{1,0:T(8,128)S(1)} collective-permute-done((f32[8,128]{1,0:T(8,128)S(1)}, f32[8,128]{1,0:T(8,128)S(1)}, u32[]{:S(2)}, u32[]{:S(2)}) %collective-permute-start.4) | collective-permute-done | bytes 4128 | tf_op jit(solution)/shard_map/ppermute | solution.py:258
  36.2 0.0 copy-done
  36.2 4.0 %shard_map.69 = (f32[1,128]{1,0:T(1,128)S(1)}, f32[16,128,128]{2,1,0:T(8,128)S(1)}, bf16[16,128,128]{2,1,0:T(8,128)(2,1)S(1)}, f32[360,128]{1,0:T(8,128)S(1)}, b...) custom-call(s32[16]{0:T(128)} %bitcast.30, s32[1,128]{1,0:T(1,128)S(1)} %bitcast.27, ...), custom_call_target="tpu_custom_call" | custom-call | flops 5000000000 | bytes 5000000 | tf_op jit(solution)/shard_map/pallas_call | solution.py:304
  40.2 0.1 collective-permute-start.13
  40.3 0.1 collective-permute-start.7
  40.4 0.1 collective-permute-start.8
  40.5 3.1 %collective-permute-start.9 = (bf16[360,128]{1,0:T(8,128)(2,1)S(1)}, bf16[360,128]{1,0:T(8,128)(2,1)S(1)}, u32[]{:S(2)}, u32[]{:S(2)}) collective-permute-start(bf16[360,128]{1,0:T(8,128)(2,1)S(1)} %get-tuple-element.35), channel_id=1, source_target_pairs={{0,96},{32,0},{64,32},{96,64},{1,97},{33,1},{65,33},{97,65},{2,98}... | collective-permute-start | bytes 276488 | tf_op jit(solution)/shard_map/ppermute | solution.py:251
  43.6 0.0 collective-permute-done.13.got_ref
  43.6 0.9 %shard_map.71 = bf16[16,128,128]{2,1,0:T(8,128)(2,1)} custom-call(f32[16,128,128]{2,1,0:T(8,128)S(1)} %get-tuple-element.36.keep_ref, bf16[16,128,128]{2,1,0:T(8,128)(2,1)S(1)} %collective-permute-done.13.got_ref), custom_call_target="tpu_custom_call" | custom-call | flops 10000000000 | tf_op jit(solution)/shard_map/pallas_call | solution.py:330
  44.5 5.9 %all-to-all-start = ((bf16[16,128,128]{2,1,0:T(8,128)(2,1)}), bf16[16,128,128]{2,1,0:T(8,128)(2,1)S(1)}, u32[]{:S(2)}, u32[]{:S(2)}) async-start(bf16[16,128,128]{2,1,0:T(8,128)(2,1)} %shard_map.71), calls=%async_computation | async-start | bytes 1048576 | tf_op jit(solution)/shard_map/all_to_all | solution.py:332
  50.4 0.0 collective-permute-done.7.a_ref
  50.4 0.0 collective-permute-done.8.b_ref
  50.4 0.0 collective-permute-done.9.c_ref
  50.4 0.1 shard_map.70.own_ref
  50.5 1.2 %collective-permute-start.12 = (bf16[360,128]{1,0:T(8,128)(2,1)S(1)}, bf16[360,128]{1,0:T(8,128)(2,1)S(1)}, u32[]{:S(2)}, u32[]{:S(2)}) collective-permute-start(bf16[360,128]{1,0:T(8,128)(2,1)S(1)} %shard_map.70.own_ref), channel_id=1, source_target_pairs={{0,96},{32,0},{64,32},{96,64},{1,97},{33,1},{65,33},{97,65},{2,98}... | collective-permute-start | bytes 276488 | tf_op jit(solution)/shard_map/ppermute | solution.py:251
  51.6 1.9 %collective-permute-start.11 = (bf16[360,128]{1,0:T(8,128)(2,1)S(1)}, bf16[360,128]{1,0:T(8,128)(2,1)S(1)}, u32[]{:S(2)}, u32[]{:S(2)}) collective-permute-start(bf16[360,128]{1,0:T(8,128)(2,1)S(1)} %shard_map.70.own_ref), channel_id=1, source_target_pairs={{0,64},{32,96},{64,0},{96,32},{1,65},{33,97},{65,1},{97,33},{2,66}... | collective-permute-start | bytes 276488 | tf_op jit(solution)/shard_map/ppermute | solution.py:251
  53.6 1.3 %collective-permute-start.10 = (bf16[360,128]{1,0:T(8,128)(2,1)S(1)}, bf16[360,128]{1,0:T(8,128)(2,1)S(1)}, u32[]{:S(2)}, u32[]{:S(2)}) collective-permute-start(bf16[360,128]{1,0:T(8,128)(2,1)S(1)} %shard_map.70.own_ref), channel_id=1, source_target_pairs={{0,32},{32,64},{64,96},{96,0},{1,33},{33,65},{65,97},{97,1},{2,34}... | collective-permute-start | bytes 276488 | tf_op jit(solution)/shard_map/ppermute | solution.py:251
  54.9 0.9 %collective-permute-done.12.c_ref = bf16[360,128]{1,0:T(8,128)(2,1)S(1)} collective-permute-done((bf16[360,128]{1,0:T(8,128)(2,1)S(1)}, bf16[360,128]{1,0:T(8,128)(2,1)S(1)}, u32[]{:S(2)}, u32[]{:S(2)}) %collective-permute-start.12) | collective-permute-done | bytes 92192 | tf_op jit(solution)/shard_map/ppermute | solution.py:251
  55.8 2.6 %collective-permute-done.11.b_ref = bf16[360,128]{1,0:T(8,128)(2,1)S(1)} collective-permute-done((bf16[360,128]{1,0:T(8,128)(2,1)S(1)}, bf16[360,128]{1,0:T(8,128)(2,1)S(1)}, u32[]{:S(2)}, u32[]{:S(2)}) %collective-permute-start.11) | collective-permute-done | bytes 92192 | tf_op jit(solution)/shard_map/ppermute | solution.py:251
  58.3 1.0 %collective-permute-done.10.a_ref = bf16[360,128]{1,0:T(8,128)(2,1)S(1)} collective-permute-done((bf16[360,128]{1,0:T(8,128)(2,1)S(1)}, bf16[360,128]{1,0:T(8,128)(2,1)S(1)}, u32[]{:S(2)}, u32[]{:S(2)}) %collective-permute-start.10) | collective-permute-done | bytes 92192 | tf_op jit(solution)/shard_map/ppermute | solution.py:251
  59.4 2.6 %all-to-all-done.terms_ref = bf16[16,128,128]{2,1,0:T(8,128)(2,1)S(1)} async-done(((bf16[16,128,128]{2,1,0:T(8,128)(2,1)}), bf16[16,128,128]{2,1,0:T(8,128)(2,1)S(1)}, u32[]{:S(2)}, u32[]{:S(2)}) %all-to-all-start) | async-done | bytes 524320 | tf_op jit(solution)/shard_map/all_to_all | solution.py:332
  62.0 1.0 %shard_map.72 = (f32[1440,128]{1,0:T(8,128)}, f32[128,128]{1,0:T(8,128)}, f32[1,4]{1,0:T(1,128)}) custom-call(f32[1,128]{1,0:T(1,128)S(1)} %get-tuple-element.31.loss_ref, bf16[360,128]{1,0:T(8,128)(2,1)S(1)} %shard_map.70.own_ref, bf16[360,128]{1,0:T(8,128)(2,1)S(1)} %collective-permute-done.10.a_ref, bf16[360,128]{1,0:T(8,128)(2,1)S(1)} %collective-permute-done.11.b_ref, ...), custom_call_target="tpu_custom_call" | custom-call | bytes 2000000 | tf_op jit(solution)/shard_map/pallas_call | solution.py:335
  (4 shorter events, 0.0 us)
Async XLA Ops:
  0.6 35.6 %copy-start = (s32[128]{0:T(128)S(1)}, s32[128]{0:T(128)}, u32[]{:S(2)}) copy-start(s32[128]{0:T(128)} %param.7) | copy-start | bytes 1540
  10.0 7.4 %collective-permute-start = (f32[8,128]{1,0:T(8,128)S(1)}, f32[8,128]{1,0:T(8,128)S(1)}, u32[]{:S(2)}, u32[]{:S(2)}) collective-permute-start(f32[8,128]{1,0:T(8,128)S(1)} %get-tuple-element.22), channel_id=1, source_target_pairs={{0,1},{1,0},{2,3},{3,2},{4,5},{5,4},{6,7},{7,6},{8,9},{9,8},{10,11... | collective-permute-start | bytes 12296 | tf_op jit(solution)/shard_map/ppermute | solution.py:298
  17.5 4.5 %collective-permute-start.3 = (f32[8,128]{1,0:T(8,128)S(1)}, f32[8,128]{1,0:T(8,128)S(1)}, u32[]{:S(2)}, u32[]{:S(2)}) collective-permute-start(f32[8,128]{1,0:T(8,128)S(1)} %add_select_fusion.1), channel_id=1, source_target_pairs={{0,6},{1,7},{2,0},{3,1},{4,2},{5,3},{6,4},{7,5},{8,14},{9,15},{10,... | collective-permute-start | bytes 12296 | tf_op jit(solution)/shard_map/ppermute | solution.py:258
  17.5 6.1 %collective-permute-start.2 = (f32[8,128]{1,0:T(8,128)S(1)}, f32[8,128]{1,0:T(8,128)S(1)}, u32[]{:S(2)}, u32[]{:S(2)}) collective-permute-start(f32[8,128]{1,0:T(8,128)S(1)} %add_select_fusion.1), channel_id=1, source_target_pairs={{0,4},{1,5},{2,6},{3,7},{4,0},{5,1},{6,2},{7,3},{8,12},{9,13},{10,... | collective-permute-start | bytes 12296 | tf_op jit(solution)/shard_map/ppermute | solution.py:258
  22.0 4.8 %collective-permute-start.1 = (f32[8,128]{1,0:T(8,128)S(1)}, f32[8,128]{1,0:T(8,128)S(1)}, u32[]{:S(2)}, u32[]{:S(2)}) collective-permute-start(f32[8,128]{1,0:T(8,128)S(1)} %add_select_fusion.1), channel_id=1, source_target_pairs={{0,2},{1,3},{2,4},{3,5},{4,6},{5,7},{6,0},{7,1},{8,10},{9,11},{10,... | collective-permute-start | bytes 12296 | tf_op jit(solution)/shard_map/ppermute | solution.py:258
  26.9 6.4 %collective-permute-start.6 = (f32[8,128]{1,0:T(8,128)S(1)}, f32[8,128]{1,0:T(8,128)S(1)}, u32[]{:S(2)}, u32[]{:S(2)}) collective-permute-start(f32[8,128]{1,0:T(8,128)S(1)} %add_select_fusion.stat0_ref), channel_id=1, source_target_pairs={{0,8},{1,9},{2,10},{3,11},{4,12},{5,13},{6,14},{7,15},{8,16},{9,17... | collective-permute-start | bytes 12296 | tf_op jit(solution)/shard_map/ppermute | solution.py:258
  27.2 7.1 %collective-permute-start.5 = (f32[8,128]{1,0:T(8,128)S(1)}, f32[8,128]{1,0:T(8,128)S(1)}, u32[]{:S(2)}, u32[]{:S(2)}) collective-permute-start(f32[8,128]{1,0:T(8,128)S(1)} %add_select_fusion.stat0_ref), channel_id=1, source_target_pairs={{0,16},{1,17},{2,18},{3,19},{4,20},{5,21},{6,22},{7,23},{8,24},{9,... | collective-permute-start | bytes 12296 | tf_op jit(solution)/shard_map/ppermute | solution.py:258
  32.6 3.6 %collective-permute-start.4 = (f32[8,128]{1,0:T(8,128)S(1)}, f32[8,128]{1,0:T(8,128)S(1)}, u32[]{:S(2)}, u32[]{:S(2)}) collective-permute-start(f32[8,128]{1,0:T(8,128)S(1)} %add_select_fusion.stat0_ref), channel_id=1, source_target_pairs={{0,24},{1,25},{2,26},{3,27},{4,28},{5,29},{6,30},{7,31},{8,0},{9,1... | collective-permute-start | bytes 12296 | tf_op jit(solution)/shard_map/ppermute | solution.py:258
  40.2 3.4 %collective-permute-start.13 = (bf16[16,128,128]{2,1,0:T(8,128)(2,1)S(1)}, bf16[16,128,128]{2,1,0:T(8,128)(2,1)S(1)}, u32[]{:S(2)}, u32[]{:S(2)}) collective-permute-start(bf16[16,128,128]{2,1,0:T(8,128)(2,1)S(1)} %get-tuple-element.37), channel_id=1, source_target_pairs={{0,1},{1,0},{2,3},{3,2},{4,5},{5,4},{6,7},{7,6},{8,9},{9,8},{10,11... | collective-permute-start | bytes 1572872 | tf_op jit(solution)/shard_map/ppermute | solution.py:329
  40.3 10.1 %collective-permute-start.7 = (bf16[360,128]{1,0:T(8,128)(2,1)S(1)}, bf16[360,128]{1,0:T(8,128)(2,1)S(1)}, u32[]{:S(2)}, u32[]{:S(2)}) collective-permute-start(bf16[360,128]{1,0:T(8,128)(2,1)S(1)} %get-tuple-element.33), channel_id=1, source_target_pairs={{0,32},{32,64},{64,96},{96,0},{1,33},{33,65},{65,97},{97,1},{2,34}... | collective-permute-start | bytes 276488 | tf_op jit(solution)/shard_map/ppermute | solution.py:251
  40.4 10.0 %collective-permute-start.8 = (bf16[360,128]{1,0:T(8,128)(2,1)S(1)}, bf16[360,128]{1,0:T(8,128)(2,1)S(1)}, u32[]{:S(2)}, u32[]{:S(2)}) collective-permute-start(bf16[360,128]{1,0:T(8,128)(2,1)S(1)} %get-tuple-element.34), channel_id=1, source_target_pairs={{0,64},{32,96},{64,0},{96,32},{1,65},{33,97},{65,1},{97,33},{2,66}... | collective-permute-start | bytes 276488 | tf_op jit(solution)/shard_map/ppermute | solution.py:251
  40.5 9.9 %collective-permute-start.9 = (bf16[360,128]{1,0:T(8,128)(2,1)S(1)}, bf16[360,128]{1,0:T(8,128)(2,1)S(1)}, u32[]{:S(2)}, u32[]{:S(2)}) collective-permute-start(bf16[360,128]{1,0:T(8,128)(2,1)S(1)} %get-tuple-element.35), channel_id=1, source_target_pairs={{0,96},{32,0},{64,32},{96,64},{1,97},{33,1},{65,33},{97,65},{2,98}... | collective-permute-start | bytes 276488 | tf_op jit(solution)/shard_map/ppermute | solution.py:251
  44.5 17.5 %all-to-all-start = ((bf16[16,128,128]{2,1,0:T(8,128)(2,1)}), bf16[16,128,128]{2,1,0:T(8,128)(2,1)S(1)}, u32[]{:S(2)}, u32[]{:S(2)}) async-start(bf16[16,128,128]{2,1,0:T(8,128)(2,1)} %shard_map.71), calls=%async_computation | async-start | bytes 1048576 | tf_op jit(solution)/shard_map/all_to_all | solution.py:332
  50.5 5.3 %collective-permute-start.12 = (bf16[360,128]{1,0:T(8,128)(2,1)S(1)}, bf16[360,128]{1,0:T(8,128)(2,1)S(1)}, u32[]{:S(2)}, u32[]{:S(2)}) collective-permute-start(bf16[360,128]{1,0:T(8,128)(2,1)S(1)} %shard_map.70.own_ref), channel_id=1, source_target_pairs={{0,96},{32,0},{64,32},{96,64},{1,97},{33,1},{65,33},{97,65},{2,98}... | collective-permute-start | bytes 276488 | tf_op jit(solution)/shard_map/ppermute | solution.py:251
  51.6 6.7 %collective-permute-start.11 = (bf16[360,128]{1,0:T(8,128)(2,1)S(1)}, bf16[360,128]{1,0:T(8,128)(2,1)S(1)}, u32[]{:S(2)}, u32[]{:S(2)}) collective-permute-start(bf16[360,128]{1,0:T(8,128)(2,1)S(1)} %shard_map.70.own_ref), channel_id=1, source_target_pairs={{0,64},{32,96},{64,0},{96,32},{1,65},{33,97},{65,1},{97,33},{2,66}... | collective-permute-start | bytes 276488 | tf_op jit(solution)/shard_map/ppermute | solution.py:251
  53.6 5.8 %collective-permute-start.10 = (bf16[360,128]{1,0:T(8,128)(2,1)S(1)}, bf16[360,128]{1,0:T(8,128)(2,1)S(1)}, u32[]{:S(2)}, u32[]{:S(2)}) collective-permute-start(bf16[360,128]{1,0:T(8,128)(2,1)S(1)} %shard_map.70.own_ref), channel_id=1, source_target_pairs={{0,32},{32,64},{64,96},{96,0},{1,33},{33,65},{65,97},{97,1},{2,34}... | collective-permute-start | bytes 276488 | tf_op jit(solution)/shard_map/ppermute | solution.py:251

commit v6 on v5

--- a/solution.py
+++ b/solution.py
@@ -184,13 +184,13 @@
             for i, k in enumerate(tasks):
                 first, second = (turned[:, i * QT + j * D : i * QT + (j + 1) * D] for j in range(2))
                 keep_ref[k] = jnp.where(core == 0, first, second)
-                give_ref[k] = jnp.where(core == 0, second, first).astype(bf16)
+                give_ref[k] = jnp.where(core == 0, second, first)
 
         @pl.when(count <= group * GROUP)
         def _(group=group):
             for i in range(GROUP):
                 keep_ref[order[group * GROUP + i]] = jnp.zeros(keep_ref.shape[1:], f32)
-                give_ref[order[group * GROUP + i]] = jnp.zeros(give_ref.shape[1:], bf16)
+                give_ref[order[group * GROUP + i]] = jnp.zeros(give_ref.shape[1:], f32)
 
     mine = lax.axis_index("pb")
     piece = PT // 4
@@ -213,22 +213,25 @@
 
 
 def both_kernel(keep_ref, got_ref, out_ref):
-    out_ref[...] = (keep_ref[...] + got_ref[...].astype(f32)).astype(bf16)
-
-
-def last_kernel(loss_ref, own_ref, a_ref, b_ref, c_ref, terms_ref, gp_ref, gq_ref, rows_ref):
+    out_ref[...] = (keep_ref[...] + got_ref[...]).astype(bf16)
+
+
+def place_kernel(loss_ref, own_ref, a_ref, b_ref, c_ref, gp_ref, rows_ref):
     mine = lax.axis_index("pb")
     piece = PT // 4
     for s, ref in ((0, own_ref), (1, a_ref), (2, b_ref), (3, c_ref)):
         owner = lax.rem(mine + 4 - s, 4)
         gp_ref[pl.ds(pl.multiple_of(owner * piece, B), piece), :] = ref[...].astype(f32)
+    count, own = loss_ref.shape[1], rows_ref.shape[1]
+    pick = iota((count, own), 0) == iota((count, own), 1) + own * lax.axis_index("pa")
+    rows_ref[...] = exact_dot(loss_ref[...], pick.astype(f32))
+
+
+def rows_kernel(terms_ref, gq_ref):
     total = terms_ref[0].astype(f32)
     for i in range(1, terms_ref.shape[0]):
         total += terms_ref[i].astype(f32)
     gq_ref[...] = total.T
-    count, own = loss_ref.shape[1], rows_ref.shape[1]
-    pick = iota((count, own), 0) == iota((count, own), 1) + own * lax.axis_index("pa")
-    rows_ref[...] = exact_dot(loss_ref[...], pick.astype(f32))
 
 
 def in_hbm(x):
@@ -300,12 +303,12 @@
     stats = (stat, *(turn_digit(stat, s, 8) for s in (3, 2, 1)))
     turned_p = call(turn_kernel, shape((D, PT), bf16), (VMEM,), nbytes=100_000)(near_p)
     piece = shape((PT // 4, D), bf16)
-    half = shape((blocks, D, own_rows * LQ), bf16)
+    half = shape((blocks, D, own_rows * LQ), f32)
     loss, keep, give, own, send1, send2, send3 = call(
         grads_kernel,
         (
             shape((1, rows), f32),
-            shape((blocks, D, own_rows * LQ), f32),
+            half,
             half,
             shape((PT // 4, D), f32),
             piece,
@@ -325,19 +328,17 @@
         nbytes=5_000_000,
     )(mask, pos, *stats, logit, tot, near_q, turned_p, *scaled)
     sends = {1: send1, 2: send2, 3: send3}
-    got = [turn(sends[s], s) for s in (1, 2, 3)]
+    got = [turn(sends[s], s) for s in (3, 2, 1)]
     got_half = lax.ppermute(give, "pa", [(i, i ^ 1) for i in range(peers)])
-    both = call(both_kernel, half, (VMEM,) * 2, flops=10_000_000_000)(keep, got_half)
+    both = call(both_kernel, shape(half.shape, bf16), (VMEM,) * 2, flops=10_000_000_000)(keep, got_half)
     same_core = [list(range(core, peers, 2)) for core in range(2)]
     gq_terms = lax.all_to_all(both, "pa", 0, 0, axis_index_groups=same_core, tiled=True)
     mine = call(sum_kernel, piece, (VMEM,) * 4, flops=30_000_000_000)(own, *got)
     others = [turn(mine, s) for s in (1, 2, 3)]
-    flat, grad_q, loss_rows = call(
-        last_kernel,
-        (shape((PT, D), f32), shape((own_rows * LQ, D), f32), shape((1, own_rows), f32)),
-        (VMEM,) * 6,
-        nbytes=2_000_000,
-    )(loss, mine, *others, gq_terms)
+    flat, loss_rows = call(
+        place_kernel, (shape((PT, D), f32), shape((1, own_rows), f32)), (VMEM,) * 5, nbytes=1_000_000
+    )(loss, mine, *others)
+    grad_q = call(rows_kernel, shape((own_rows * LQ, D), f32), (VMEM,), nbytes=1_000_000)(gq_terms)
     grad_p = jnp.swapaxes(flat.reshape(LP, B, D), 0, 1)
     return loss_rows.reshape(own_rows), grad_q.reshape(own_rows, LQ, D), grad_p
 

time: 63.4 us -> 62.8 us (level)
  Pallas kernels: 15.5 us -> 26.4 us
  starting transfers between devices: 30.9 us -> 20.5 us
  waiting for transfers between devices: 15.6 us -> 14.7 us
    pallas_call x1, Pallas kernels: 9.36 us -> 16.8 us  [on_device(): call(scores_kernel, (packed, packed, wide, shape((rows * LQ, D), bf16), s...]
    ppermute x1, starting transfers between devices: 6.56 us -> 0.09 us  [on_device(): lax.ppermute(send, 'pa', [(i, i ^ 1) for i in range(peers)])]
    pallas_call x3 -> x4, Pallas kernels: 5.91 us -> 9.39 us  [the longest x1 6.67 us: on_device(): call(grads_kernel, (shape((1, rows), f32), half, half, shape((PT // 4, D)...]
    all_to_all x1, starting transfers between devices: 5.87 us -> 3.57 us  [on_device(): lax.all_to_all(both, 'pa', 0, 0, axis_index_groups=same_core, tiled=True)]
    ppermute x6, waiting for transfers between devices: 7.7 us -> 5.7 us  [turn_digit(): lax.ppermute(x, 'pa', [(i, to(i)) for i in range(lax.axis_size('pa'))])]
    ppermute x6, starting transfers between devices: 7.7 us -> 5.86 us  [turn(): return lax.ppermute(x, 'pb', [(i, (i + s) % 4) for i in range(4)])]
    ppermute x6, waiting for transfers between devices: 4.49 us -> 6.29 us  [turn(): return lax.ppermute(x, 'pb', [(i, (i + s) % 4) for i in range(4)])]
    all_to_all x1, waiting for transfers between devices: 2.6 us -> 0.98 us  [on_device(): lax.all_to_all(both, 'pa', 0, 0, axis_index_groups=same_core, tiled=True)]
  transfers between devices with their start and end apart: 15 -> 15, of which waited for: 9 -> 11; matrix products, arithmetic and copies ran while one was open for 0% -> 0% of each run, Pallas kernels for 2% -> 4%
where the time goes in v6:
time: 62.8 us; the launch traced here: 62.5 us
  Pallas kernels  26.4 us (42%)
  starting transfers between devices  20.5 us (33%)
  waiting for transfers between devices  14.7 us (23%)
  between operations  0.76 us (1%)
    pallas_call x1, Pallas kernels, on_device(): call(scores_kernel, (packed, packed, wide, shape((rows * LQ, D), bf16), s...  16.8 us
    ppermute x6, starting transfers between devices, turn_digit(): lax.ppermute(x, 'pa', [(i, to(i)) for i in range(lax.axis_size('pa'))])  10.9 us
    pallas_call x1, Pallas kernels, on_device(): call(grads_kernel, (shape((1, rows), f32), half, half, shape((PT // 4, D)...  6.67 us
    ppermute x6, waiting for transfers between devices, turn(): return lax.ppermute(x, 'pb', [(i, (i + s) % 4) for i in range(4)])  6.29 us
    ppermute x6, starting transfers between devices, turn(): return lax.ppermute(x, 'pb', [(i, (i + s) % 4) for i in range(4)])  5.86 us
    ppermute x6, waiting for transfers between devices, turn_digit(): lax.ppermute(x, 'pa', [(i, to(i)) for i in range(lax.axis_size('pa'))])  5.7 us
    all_to_all x1, starting transfers between devices, on_device(): lax.all_to_all(both, 'pa', 0, 0, axis_index_groups=same_core, tiled=True)  3.57 us
  transfers between devices with their start and end apart: 15, of which 11 were waited for; matrix products, arithmetic and copies ran while one was open for 0% of the time, Pallas kernels for 4%

profile of v6, /device:TPU:0, one launch (start us, length us, event | category | flops | bytes accessed | tf_op | source)
XLA Modules:
  0.0 62.5 jit_solution(6732350318910512182)
XLA Ops:
  0.6 0.0 copy-start
  0.6 16.8 %shard_map.67 = (f32[8,128]{1,0:T(8,128)S(1)}, f32[8,128]{1,0:T(8,128)S(1)}, f32[16,8,256]{2,1,0:T(8,128)S(1)}, bf16[4096,128]{1,0:T(8,128)(2,1)S(1)}, bf16[1440...) custom-call(s32[16]{0:T(128)} %bitcast.30, ...), custom_call_target="tpu_custom_call" | custom-call | flops 2000000000 | bytes 3000000 | tf_op jit(solution)/shard_map/pallas_call | solution.py:279
  17.4 0.1 collective-permute-start
  17.5 1.1 %collective-permute-done = f32[8,128]{1,0:T(8,128)S(1)} collective-permute-done((f32[8,128]{1,0:T(8,128)S(1)}, f32[8,128]{1,0:T(8,128)S(1)}, u32[]{:S(2)}, u32[]{:S(2)}) %collective-permute-start) | collective-permute-done | bytes 4128 | tf_op jit(solution)/shard_map/ppermute | solution.py:301
  18.7 0.1 add_select_fusion.1
  18.8 3.1 %collective-permute-start.3 = (f32[8,128]{1,0:T(8,128)S(1)}, f32[8,128]{1,0:T(8,128)S(1)}, u32[]{:S(2)}, u32[]{:S(2)}) collective-permute-start(f32[8,128]{1,0:T(8,128)S(1)} %add_select_fusion.1), channel_id=1, source_target_pairs={{0,6},{1,7},{2,0},{3,1},{4,2},{5,3},{6,4},{7,5},{8,14},{9,15},{10,... | collective-permute-start | bytes 12296 | tf_op jit(solution)/shard_map/ppermute | solution.py:261
  21.9 0.0 collective-permute-start.2
  21.9 0.9 %collective-permute-start.1 = (f32[8,128]{1,0:T(8,128)S(1)}, f32[8,128]{1,0:T(8,128)S(1)}, u32[]{:S(2)}, u32[]{:S(2)}) collective-permute-start(f32[8,128]{1,0:T(8,128)S(1)} %add_select_fusion.1), channel_id=1, source_target_pairs={{0,2},{1,3},{2,4},{3,5},{4,6},{5,7},{6,0},{7,1},{8,10},{9,11},{10,... | collective-permute-start | bytes 12296 | tf_op jit(solution)/shard_map/ppermute | solution.py:261
  22.8 0.4 collective-permute-done.3
  23.2 3.8 %collective-permute-done.2 = f32[8,128]{1,0:T(8,128)S(1)} collective-permute-done((f32[8,128]{1,0:T(8,128)S(1)}, f32[8,128]{1,0:T(8,128)S(1)}, u32[]{:S(2)}, u32[]{:S(2)}) %collective-permute-start.2) | collective-permute-done | bytes 4128 | tf_op jit(solution)/shard_map/ppermute | solution.py:261
  27.0 0.0 collective-permute-done.1
  27.0 0.1 add_select_fusion.stat0_ref
  27.1 2.2 %collective-permute-start.6 = (f32[8,128]{1,0:T(8,128)S(1)}, f32[8,128]{1,0:T(8,128)S(1)}, u32[]{:S(2)}, u32[]{:S(2)}) collective-permute-start(f32[8,128]{1,0:T(8,128)S(1)} %add_select_fusion.stat0_ref), channel_id=1, source_target_pairs={{0,8},{1,9},{2,10},{3,11},{4,12},{5,13},{6,14},{7,15},{8,16},{9,17... | collective-permute-start | bytes 12296 | tf_op jit(solution)/shard_map/ppermute | solution.py:261
  29.3 2.7 %collective-permute-start.5 = (f32[8,128]{1,0:T(8,128)S(1)}, f32[8,128]{1,0:T(8,128)S(1)}, u32[]{:S(2)}, u32[]{:S(2)}) collective-permute-start(f32[8,128]{1,0:T(8,128)S(1)} %add_select_fusion.stat0_ref), channel_id=1, source_target_pairs={{0,16},{1,17},{2,18},{3,19},{4,20},{5,21},{6,22},{7,23},{8,24},{9,... | collective-permute-start | bytes 12296 | tf_op jit(solution)/shard_map/ppermute | solution.py:261
  32.1 1.9 %collective-permute-start.4 = (f32[8,128]{1,0:T(8,128)S(1)}, f32[8,128]{1,0:T(8,128)S(1)}, u32[]{:S(2)}, u32[]{:S(2)}) collective-permute-start(f32[8,128]{1,0:T(8,128)S(1)} %add_select_fusion.stat0_ref), channel_id=1, source_target_pairs={{0,24},{1,25},{2,26},{3,27},{4,28},{5,29},{6,30},{7,31},{8,0},{9,1... | collective-permute-start | bytes 12296 | tf_op jit(solution)/shard_map/ppermute | solution.py:261
  33.9 0.2 shard_map.68.turn_ref
  34.1 0.0 collective-permute-done.6.stat3_ref
  34.1 0.3 collective-permute-done.5.stat2_ref
  34.4 1.2 %collective-permute-done.4.stat1_ref = f32[8,128]{1,0:T(8,128)S(1)} collective-permute-done((f32[8,128]{1,0:T(8,128)S(1)}, f32[8,128]{1,0:T(8,128)S(1)}, u32[]{:S(2)}, u32[]{:S(2)}) %collective-permute-start.4) | collective-permute-done | bytes 4128 | tf_op jit(solution)/shard_map/ppermute | solution.py:261
  35.7 0.0 copy-done
  35.7 6.7 %shard_map.69 = (f32[1,128]{1,0:T(1,128)S(1)}, f32[16,128,128]{2,1,0:T(8,128)S(1)}, f32[16,128,128]{2,1,0:T(8,128)S(1)}, f32[360,128]{1,0:T(8,128)S(1)}, bf16[36...) custom-call(s32[16]{0:T(128)} %bitcast.31, s32[1,128]{1,0:T(1,128)S(1)} %bitcast.27, ...), custom_call_target="tpu_custom_call" | custom-call | flops 5000000000 | bytes 5000000 | tf_op jit(solution)/shard_map/pallas_call | solution.py:307
  42.4 0.1 collective-permute-start.13
  42.5 0.1 collective-permute-start.7
  42.5 0.1 collective-permute-start.8
  42.6 1.9 %collective-permute-start.9 = (bf16[360,128]{1,0:T(8,128)(2,1)S(1)}, bf16[360,128]{1,0:T(8,128)(2,1)S(1)}, u32[]{:S(2)}, u32[]{:S(2)}) collective-permute-start(bf16[360,128]{1,0:T(8,128)(2,1)S(1)} %get-tuple-element.34), channel_id=1, source_target_pairs={{0,32},{32,64},{64,96},{96,0},{1,33},{33,65},{65,97},{97,1},{2,34}... | collective-permute-start | bytes 276488 | tf_op jit(solution)/shard_map/ppermute | solution.py:254
  44.5 0.5 collective-permute-done.13.got_ref
  45.1 1.0 %shard_map.72 = bf16[16,128,128]{2,1,0:T(8,128)(2,1)} custom-call(f32[16,128,128]{2,1,0:T(8,128)S(1)} %get-tuple-element.36.keep_ref, f32[16,128,128]{2,1,0:T(8,128)S(1)} %collective-permute-done.13.got_ref), custom_call_target="tpu_custom_call" | custom-call | flops 10000000000 | tf_op jit(solution)/shard_map/pallas_call | solution.py:333
  46.1 3.6 %all-to-all-start = ((bf16[16,128,128]{2,1,0:T(8,128)(2,1)}), bf16[16,128,128]{2,1,0:T(8,128)(2,1)S(1)}, u32[]{:S(2)}, u32[]{:S(2)}) async-start(bf16[16,128,128]{2,1,0:T(8,128)(2,1)} %shard_map.72), calls=%async_computation | async-start | bytes 1048576 | tf_op jit(solution)/shard_map/all_to_all | solution.py:335
  49.7 0.0 collective-permute-done.7.a_ref
  49.7 0.0 collective-permute-done.8.b_ref
  49.7 1.3 %collective-permute-done.9.c_ref = bf16[360,128]{1,0:T(8,128)(2,1)S(1)} collective-permute-done((bf16[360,128]{1,0:T(8,128)(2,1)S(1)}, bf16[360,128]{1,0:T(8,128)(2,1)S(1)}, u32[]{:S(2)}, u32[]{:S(2)}) %collective-permute-start.9) | collective-permute-done | bytes 92192 | tf_op jit(solution)/shard_map/ppermute | solution.py:254
  51.0 1.3 %collective-permute-start.12 = (bf16[360,128]{1,0:T(8,128)(2,1)S(1)}, bf16[360,128]{1,0:T(8,128)(2,1)S(1)}, u32[]{:S(2)}, u32[]{:S(2)}) collective-permute-start(bf16[360,128]{1,0:T(8,128)(2,1)S(1)} %shard_map.70.own_ref), channel_id=1, source_target_pairs={{0,96},{32,0},{64,32},{96,64},{1,97},{33,1},{65,33},{97,65},{2,98}... | collective-permute-start | bytes 276488 | tf_op jit(solution)/shard_map/ppermute | solution.py:254
  52.3 1.2 %collective-permute-start.11 = (bf16[360,128]{1,0:T(8,128)(2,1)S(1)}, bf16[360,128]{1,0:T(8,128)(2,1)S(1)}, u32[]{:S(2)}, u32[]{:S(2)}) collective-permute-start(bf16[360,128]{1,0:T(8,128)(2,1)S(1)} %shard_map.70.own_ref), channel_id=1, source_target_pairs={{0,64},{32,96},{64,0},{96,32},{1,65},{33,97},{65,1},{97,33},{2,66}... | collective-permute-start | bytes 276488 | tf_op jit(solution)/shard_map/ppermute | solution.py:254
  53.5 1.3 %collective-permute-start.10 = (bf16[360,128]{1,0:T(8,128)(2,1)S(1)}, bf16[360,128]{1,0:T(8,128)(2,1)S(1)}, u32[]{:S(2)}, u32[]{:S(2)}) collective-permute-start(bf16[360,128]{1,0:T(8,128)(2,1)S(1)} %shard_map.70.own_ref), channel_id=1, source_target_pairs={{0,32},{32,64},{64,96},{96,0},{1,33},{33,65},{65,97},{97,1},{2,34}... | collective-permute-start | bytes 276488 | tf_op jit(solution)/shard_map/ppermute | solution.py:254
  54.8 1.8 %collective-permute-done.12.c_ref = bf16[360,128]{1,0:T(8,128)(2,1)S(1)} collective-permute-done((bf16[360,128]{1,0:T(8,128)(2,1)S(1)}, bf16[360,128]{1,0:T(8,128)(2,1)S(1)}, u32[]{:S(2)}, u32[]{:S(2)}) %collective-permute-start.12) | collective-permute-done | bytes 92192 | tf_op jit(solution)/shard_map/ppermute | solution.py:254
  56.6 2.7 %collective-permute-done.11.b_ref = bf16[360,128]{1,0:T(8,128)(2,1)S(1)} collective-permute-done((bf16[360,128]{1,0:T(8,128)(2,1)S(1)}, bf16[360,128]{1,0:T(8,128)(2,1)S(1)}, u32[]{:S(2)}, u32[]{:S(2)}) %collective-permute-start.11) | collective-permute-done | bytes 92192 | tf_op jit(solution)/shard_map/ppermute | solution.py:254
  59.3 0.5 collective-permute-done.10.a_ref
  59.8 1.0 %shard_map.71 = (f32[1440,128]{1,0:T(8,128)}, f32[1,4]{1,0:T(1,128)}) custom-call(f32[1,128]{1,0:T(1,128)S(1)} %get-tuple-element.30.loss_ref, bf16[360,128]{1,0:T(8,128)(2,1)S(1)} %shard_map.70.own_ref, bf16[360,128]{1,0:T(8,128)(2,1)S(1)} %collective-permute-done.10.a_ref, bf16[360,128]{1,0:T(8,128)(2,1)S(1)} %collective-permute-done.11.b_ref, ...), custom_call_target="tpu_custom_call" | custom-call | bytes 1000000 | tf_op jit(solution)/shard_map/pallas_call | solution.py:338
  60.8 1.0 %all-to-all-done.terms_ref = bf16[16,128,128]{2,1,0:T(8,128)(2,1)S(1)} async-done(((bf16[16,128,128]{2,1,0:T(8,128)(2,1)}), bf16[16,128,128]{2,1,0:T(8,128)(2,1)S(1)}, u32[]{:S(2)}, u32[]{:S(2)}) %all-to-all-start) | async-done | bytes 524320 | tf_op jit(solution)/shard_map/all_to_all | solution.py:335
  61.7 0.8 %shard_map.73 = f32[128,128]{1,0:T(8,128)} custom-call(bf16[16,128,128]{2,1,0:T(8,128)(2,1)S(1)} %all-to-all-done.terms_ref), custom_call_target="tpu_custom_call" | custom-call | bytes 1000000 | tf_op jit(solution)/shard_map/pallas_call | solution.py:341
  (5 shorter events, 0.1 us)
Async XLA Ops:
  0.6 35.0 %copy-start = (s32[128]{0:T(128)S(1)}, s32[128]{0:T(128)}, u32[]{:S(2)}) copy-start(s32[128]{0:T(128)} %param.7) | copy-start | bytes 1540
  17.4 1.2 %collective-permute-start = (f32[8,128]{1,0:T(8,128)S(1)}, f32[8,128]{1,0:T(8,128)S(1)}, u32[]{:S(2)}, u32[]{:S(2)}) collective-permute-start(f32[8,128]{1,0:T(8,128)S(1)} %get-tuple-element.21), channel_id=1, source_target_pairs={{0,1},{1,0},{2,3},{3,2},{4,5},{5,4},{6,7},{7,6},{8,9},{9,8},{10,11... | collective-permute-start | bytes 12296 | tf_op jit(solution)/shard_map/ppermute | solution.py:301
  18.8 4.4 %collective-permute-start.3 = (f32[8,128]{1,0:T(8,128)S(1)}, f32[8,128]{1,0:T(8,128)S(1)}, u32[]{:S(2)}, u32[]{:S(2)}) collective-permute-start(f32[8,128]{1,0:T(8,128)S(1)} %add_select_fusion.1), channel_id=1, source_target_pairs={{0,6},{1,7},{2,0},{3,1},{4,2},{5,3},{6,4},{7,5},{8,14},{9,15},{10,... | collective-permute-start | bytes 12296 | tf_op jit(solution)/shard_map/ppermute | solution.py:261
  21.9 5.1 %collective-permute-start.2 = (f32[8,128]{1,0:T(8,128)S(1)}, f32[8,128]{1,0:T(8,128)S(1)}, u32[]{:S(2)}, u32[]{:S(2)}) collective-permute-start(f32[8,128]{1,0:T(8,128)S(1)} %add_select_fusion.1), channel_id=1, source_target_pairs={{0,4},{1,5},{2,6},{3,7},{4,0},{5,1},{6,2},{7,3},{8,12},{9,13},{10,... | collective-permute-start | bytes 12296 | tf_op jit(solution)/shard_map/ppermute | solution.py:261
  21.9 5.1 %collective-permute-start.1 = (f32[8,128]{1,0:T(8,128)S(1)}, f32[8,128]{1,0:T(8,128)S(1)}, u32[]{:S(2)}, u32[]{:S(2)}) collective-permute-start(f32[8,128]{1,0:T(8,128)S(1)} %add_select_fusion.1), channel_id=1, source_target_pairs={{0,2},{1,3},{2,4},{3,5},{4,6},{5,7},{6,0},{7,1},{8,10},{9,11},{10,... | collective-permute-start | bytes 12296 | tf_op jit(solution)/shard_map/ppermute | solution.py:261
  27.1 7.0 %collective-permute-start.6 = (f32[8,128]{1,0:T(8,128)S(1)}, f32[8,128]{1,0:T(8,128)S(1)}, u32[]{:S(2)}, u32[]{:S(2)}) collective-permute-start(f32[8,128]{1,0:T(8,128)S(1)} %add_select_fusion.stat0_ref), channel_id=1, source_target_pairs={{0,8},{1,9},{2,10},{3,11},{4,12},{5,13},{6,14},{7,15},{8,16},{9,17... | collective-permute-start | bytes 12296 | tf_op jit(solution)/shard_map/ppermute | solution.py:261
  29.3 5.1 %collective-permute-start.5 = (f32[8,128]{1,0:T(8,128)S(1)}, f32[8,128]{1,0:T(8,128)S(1)}, u32[]{:S(2)}, u32[]{:S(2)}) collective-permute-start(f32[8,128]{1,0:T(8,128)S(1)} %add_select_fusion.stat0_ref), channel_id=1, source_target_pairs={{0,16},{1,17},{2,18},{3,19},{4,20},{5,21},{6,22},{7,23},{8,24},{9,... | collective-permute-start | bytes 12296 | tf_op jit(solution)/shard_map/ppermute | solution.py:261
  32.1 3.6 %collective-permute-start.4 = (f32[8,128]{1,0:T(8,128)S(1)}, f32[8,128]{1,0:T(8,128)S(1)}, u32[]{:S(2)}, u32[]{:S(2)}) collective-permute-start(f32[8,128]{1,0:T(8,128)S(1)} %add_select_fusion.stat0_ref), channel_id=1, source_target_pairs={{0,24},{1,25},{2,26},{3,27},{4,28},{5,29},{6,30},{7,31},{8,0},{9,1... | collective-permute-start | bytes 12296 | tf_op jit(solution)/shard_map/ppermute | solution.py:261
  42.4 2.7 %collective-permute-start.13 = (f32[16,128,128]{2,1,0:T(8,128)S(1)}, f32[16,128,128]{2,1,0:T(8,128)S(1)}, u32[]{:S(2)}, u32[]{:S(2)}) collective-permute-start(f32[16,128,128]{2,1,0:T(8,128)S(1)} %get-tuple-element.37), channel_id=1, source_target_pairs={{0,1},{1,0},{2,3},{3,2},{4,5},{5,4},{6,7},{7,6},{8,9},{9,8},{10,11... | collective-permute-start | bytes 3145736 | tf_op jit(solution)/shard_map/ppermute | solution.py:332
  42.5 7.2 %collective-permute-start.7 = (bf16[360,128]{1,0:T(8,128)(2,1)S(1)}, bf16[360,128]{1,0:T(8,128)(2,1)S(1)}, u32[]{:S(2)}, u32[]{:S(2)}) collective-permute-start(bf16[360,128]{1,0:T(8,128)(2,1)S(1)} %get-tuple-element.32), channel_id=1, source_target_pairs={{0,96},{32,0},{64,32},{96,64},{1,97},{33,1},{65,33},{97,65},{2,98}... | collective-permute-start | bytes 276488 | tf_op jit(solution)/shard_map/ppermute | solution.py:254
  42.5 7.1 %collective-permute-start.8 = (bf16[360,128]{1,0:T(8,128)(2,1)S(1)}, bf16[360,128]{1,0:T(8,128)(2,1)S(1)}, u32[]{:S(2)}, u32[]{:S(2)}) collective-permute-start(bf16[360,128]{1,0:T(8,128)(2,1)S(1)} %get-tuple-element.33), channel_id=1, source_target_pairs={{0,64},{32,96},{64,0},{96,32},{1,65},{33,97},{65,1},{97,33},{2,66}... | collective-permute-start | bytes 276488 | tf_op jit(solution)/shard_map/ppermute | solution.py:254
  42.6 8.4 %collective-permute-start.9 = (bf16[360,128]{1,0:T(8,128)(2,1)S(1)}, bf16[360,128]{1,0:T(8,128)(2,1)S(1)}, u32[]{:S(2)}, u32[]{:S(2)}) collective-permute-start(bf16[360,128]{1,0:T(8,128)(2,1)S(1)} %get-tuple-element.34), channel_id=1, source_target_pairs={{0,32},{32,64},{64,96},{96,0},{1,33},{33,65},{65,97},{97,1},{2,34}... | collective-permute-start | bytes 276488 | tf_op jit(solution)/shard_map/ppermute | solution.py:254
  46.1 15.7 %all-to-all-start = ((bf16[16,128,128]{2,1,0:T(8,128)(2,1)}), bf16[16,128,128]{2,1,0:T(8,128)(2,1)S(1)}, u32[]{:S(2)}, u32[]{:S(2)}) async-start(bf16[16,128,128]{2,1,0:T(8,128)(2,1)} %shard_map.72), calls=%async_computation | async-start | bytes 1048576 | tf_op jit(solution)/shard_map/all_to_all | solution.py:335
  51.0 5.6 %collective-permute-start.12 = (bf16[360,128]{1,0:T(8,128)(2,1)S(1)}, bf16[360,128]{1,0:T(8,128)(2,1)S(1)}, u32[]{:S(2)}, u32[]{:S(2)}) collective-permute-start(bf16[360,128]{1,0:T(8,128)(2,1)S(1)} %shard_map.70.own_ref), channel_id=1, source_target_pairs={{0,96},{32,0},{64,32},{96,64},{1,97},{33,1},{65,33},{97,65},{2,98}... | collective-permute-start | bytes 276488 | tf_op jit(solution)/shard_map/ppermute | solution.py:254
  52.3 7.0 %collective-permute-start.11 = (bf16[360,128]{1,0:T(8,128)(2,1)S(1)}, bf16[360,128]{1,0:T(8,128)(2,1)S(1)}, u32[]{:S(2)}, u32[]{:S(2)}) collective-permute-start(bf16[360,128]{1,0:T(8,128)(2,1)S(1)} %shard_map.70.own_ref), channel_id=1, source_target_pairs={{0,64},{32,96},{64,0},{96,32},{1,65},{33,97},{65,1},{97,33},{2,66}... | collective-permute-start | bytes 276488 | tf_op jit(solution)/shard_map/ppermute | solution.py:254
  53.5 6.3 %collective-permute-start.10 = (bf16[360,128]{1,0:T(8,128)(2,1)S(1)}, bf16[360,128]{1,0:T(8,128)(2,1)S(1)}, u32[]{:S(2)}, u32[]{:S(2)}) collective-permute-start(bf16[360,128]{1,0:T(8,128)(2,1)S(1)} %shard_map.70.own_ref), channel_id=1, source_target_pairs={{0,32},{32,64},{64,96},{96,0},{1,33},{33,65},{65,97},{97,1},{2,34}... | collective-permute-start | bytes 276488 | tf_op jit(solution)/shard_map/ppermute | solution.py:254

commit v7 on v6

--- a/solution.py
+++ b/solution.py
@@ -78,10 +78,10 @@
     return lax.dot_general(p_ref[...], block_rows(q_ref, k), turned_dims, preferred_element_type=f32)
 
 
-def scores_kernel(mask_hbm, pos_hbm, q_hbm, p_hbm, send_ref, logit_ref, tot_ref, q_ref, p_ref, *rest):
+def scores_kernel(mask_hbm, pos_hbm, q_hbm, p_hbm, send_ref, logit_ref, tot_ref, q_ref, turn_ref, *rest):
     blocks = tot_ref.shape[0]
     groups = blocks // GROUP
-    scaled_refs, (mask_s, pos_ref, order, top_ref, sim_ref, sems) = rest[:groups], rest[groups:]
+    scaled_refs, (mask_s, pos_ref, p_ref, order, top_ref, sim_ref, sems) = rest[:groups], rest[groups:]
     pairs = ((mask_hbm, mask_s), (pos_hbm, pos_ref), (p_hbm, p_ref), (q_hbm, q_ref))
     mask_wait, pos_wait, p_wait, q_wait = fetch_all(pairs, sems)
     top_ref[...] = jnp.zeros_like(top_ref)
@@ -90,6 +90,7 @@
     count = list_tasks(mask_s, order)
     pos_wait()
     p_wait()
+    turn_ref[...] = p_ref[...].astype(f32).T.astype(bf16)
     q_wait()
     for group, scaled_ref in enumerate(scaled_refs):
 
@@ -135,20 +136,11 @@
     local_pos = jnp.sum(jnp.where(positive, logit, 0.0), axis=0, keepdims=True)
     row = iota(logit.shape, 0)
     send = jnp.where(row == 0, local_top, jnp.where(row == 1, local_total, local_pos))
-    send_ref[...] = jnp.where(row < 3, send, 0.0)
-
-
-def merged(*stats):
-    row = iota(stats[0].shape, 0)
-    top = stats[0][:1]
-    for x in stats[1:]:
-        top = jnp.maximum(top, x[:1])
-    total = sum(x * jnp.where(row == 1, jnp.exp(x[:1] - top), 1.0) for x in stats)
-    return jnp.where(row == 0, top, total)
+    send_ref[...] = jnp.broadcast_to(jnp.where(row < 3, send, 0.0)[None], send_ref.shape)
 
 
 def grads_kernel(
-    mask_hbm, pos_ref, stat0_ref, stat1_ref, stat2_ref, stat3_ref, logit_ref, tot_ref, q_ref, turn_ref, *rest
+    mask_hbm, pos_ref, stat_ref, logit_ref, tot_ref, q_ref, turn_ref, *rest
 ):
     blocks = tot_ref.shape[0]
     groups = blocks // GROUP
@@ -157,8 +149,11 @@
     mask_s, order, weight_ref, gp_ref, dsim_ref, sem = rest
     fetch = pltpu.make_async_copy(mask_hbm, mask_s, sem)
     fetch.start()
-    stat = merged(stat0_ref[...], stat1_ref[...], stat2_ref[...], stat3_ref[...])
-    glob_top, glob_total, glob_pos = stat[:1], stat[1:2], stat[2:3]
+    stat = stat_ref[...]
+    top = jnp.max(stat, axis=0)[:1]
+    row = iota(stat.shape, 1)
+    sums = jnp.sum(stat * jnp.where(row == 1, jnp.exp(stat[:, :1] - top[None]), 1.0), axis=0)
+    glob_top, glob_total, glob_pos = top, sums[1:2], sums[2:3]
     loss_ref[...] = glob_top + jnp.log(glob_total) - glob_pos
     logit = logit_ref[...]
     active = logit > very_low / 2
@@ -203,10 +198,6 @@
         send[...] = rows_of(lax.rem(mine + s, 4)).astype(bf16)
 
 
-def turn_kernel(p_ref, out_ref):
-    out_ref[...] = p_ref[...].astype(f32).T.astype(bf16)
-
-
 def sum_kernel(own_ref, a_ref, b_ref, c_ref, out_ref):
     total = own_ref[...] + a_ref[...].astype(f32) + b_ref[...].astype(f32) + c_ref[...].astype(f32)
     out_ref[...] = total.astype(bf16)
@@ -252,13 +243,6 @@
 
 def turn(x, s):
     return lax.ppermute(x, "pb", [(i, (i + s) % 4) for i in range(4)])
-
-
-def turn_digit(x, s, unit):
-    def to(i):
-        return i + unit * ((i // unit + s) % 4 - i // unit % 4)
-
-    return lax.ppermute(x, "pa", [(i, to(i)) for i in range(lax.axis_size("pa"))])
 
 
 def on_device(queries, passages, pair_mask, positive):
@@ -276,20 +260,21 @@
     mask, flat_q, flat_p = (in_hbm(x) for x in (mask, flat_q, flat_p))
     wide = shape((blocks, B, QT), f32)
     packed = shape((B, rows), f32)
-    send, logit, tot, near_q, near_p, *scaled = call(
+    send, logit, tot, near_q, turned_p, *scaled = call(
         scores_kernel,
         (
-            packed,
+            shape((peers, B, rows), f32),
             packed,
             wide,
             shape((rows * LQ, D), bf16),
-            shape((PT, D), bf16),
+            shape((D, PT), bf16),
             *(shape((GROUP, PT, QT), f32),) * groups,
         ),
         (ANY,) * 4,
         [
             ints,
             pltpu.VMEM((1, rows), jnp.int32),
+            pltpu.VMEM((PT, D), bf16),
             ints,
             pltpu.VMEM((blocks, B, QT), f32),
             pltpu.VMEM((PT, QT), f32),
@@ -298,10 +283,7 @@
         flops=2_000_000_000,
         nbytes=3_000_000,
     )(mask, in_hbm(pos), flat_q, flat_p)
-    stat = merged(send, lax.ppermute(send, "pa", [(i, i ^ 1) for i in range(peers)]))
-    stat = merged(stat, *(turn_digit(stat, s, 2) for s in (1, 2, 3)))
-    stats = (stat, *(turn_digit(stat, s, 8) for s in (3, 2, 1)))
-    turned_p = call(turn_kernel, shape((D, PT), bf16), (VMEM,), nbytes=100_000)(near_p)
+    stats = lax.all_to_all(send, "pa", 0, 0, tiled=True)
     piece = shape((PT // 4, D), bf16)
     half = shape((blocks, D, own_rows * LQ), f32)
     loss, keep, give, own, send1, send2, send3 = call(
@@ -315,7 +297,7 @@
             piece,
             piece,
         ),
-        (ANY,) + (VMEM,) * (9 + groups),
+        (ANY,) + (VMEM,) * (6 + groups),
         [
             ints,
             ints,
@@ -326,7 +308,7 @@
         ],
         flops=5_000_000_000,
         nbytes=5_000_000,
-    )(mask, pos, *stats, logit, tot, near_q, turned_p, *scaled)
+    )(mask, pos, stats, logit, tot, near_q, turned_p, *scaled)
     sends = {1: send1, 2: send2, 3: send3}
     got = [turn(sends[s], s) for s in (3, 2, 1)]
     got_half = lax.ppermute(give, "pa", [(i, i ^ 1) for i in range(peers)])

time: 62.8 us -> 60.3 us (0.960)
  blocking collectives: 0 us -> 27.2 us
  Pallas kernels: 26.4 us -> 11 us
  waiting for transfers between devices: 14.7 us -> 5.97 us
  starting transfers between devices: 20.5 us -> 15 us
    all_to_all x0 -> x1, blocking collectives: none -> 27.2 us  [on_device(): stats = lax.all_to_all(send, 'pa', 0, 0, tiled=True)]
    pallas_call x2 -> x1, Pallas kernels: 17 us -> 5.67 us  [on_device(): call(scores_kernel, (shape((peers, B, rows), f32), packed, wide, shape((r...]
    ppermute x7 -> x0, starting transfers between devices: 11 us -> none  [the longest x6 10.9 us: turn_digit(): lax.ppermute(x, 'pa', [(i, to(i)) for i in range(lax.axis_size('pa'))])]
    ppermute x7 -> x0, waiting for transfers between devices: 6.84 us -> none  [the longest x6 5.7 us: turn_digit(): lax.ppermute(x, 'pa', [(i, to(i)) for i in range(lax.axis_size('pa'))])]
    pallas_call x1, Pallas kernels: 6.67 us -> 2.7 us  [on_device(): call(grads_kernel, (shape((1, rows), f32), half, half, shape((PT // 4, D)...]
    all_to_all x1, starting transfers between devices: 3.57 us -> 6.24 us  [on_device(): lax.all_to_all(both, 'pa', 0, 0, axis_index_groups=same_core, tiled=True)]
    ppermute x6, waiting for transfers between devices: 6.29 us -> 4.5 us  [turn(): return lax.ppermute(x, 'pb', [(i, (i + s) % 4) for i in range(4)])]
    ppermute x1, starting transfers between devices: 0.09 us -> 1.61 us  [on_device(): got_half = lax.ppermute(give, 'pa', [(i, i ^ 1) for i in range(peers)])]
  transfers between devices with their start and end apart: 15 -> 8, of which waited for: 11 -> 5; matrix products, arithmetic and copies ran while one was open for 0% -> 0% of each run, Pallas kernels for 4% -> 3%
where the time goes in v7:
time: 60.3 us; the launch traced here: 59.9 us
  blocking collectives  27.2 us (45%)
  starting transfers between devices  15 us (25%)
  Pallas kernels  11 us (18%)
  waiting for transfers between devices  5.97 us (10%)
  between operations  0.7 us (1%)
    all_to_all x1, blocking collectives, on_device(): stats = lax.all_to_all(send, 'pa', 0, 0, tiled=True)  27.2 us
    ppermute x6, starting transfers between devices, turn(): return lax.ppermute(x, 'pb', [(i, (i + s) % 4) for i in range(4)])  7.11 us
    all_to_all x1, starting transfers between devices, on_device(): lax.all_to_all(both, 'pa', 0, 0, axis_index_groups=same_core, tiled=True)  6.24 us
    pallas_call x1, Pallas kernels, on_device(): call(scores_kernel, (shape((peers, B, rows), f32), packed, wide, shape((r...  5.67 us
    ppermute x6, waiting for transfers between devices, turn(): return lax.ppermute(x, 'pb', [(i, (i + s) % 4) for i in range(4)])  4.5 us
    pallas_call x1, Pallas kernels, on_device(): call(grads_kernel, (shape((1, rows), f32), half, half, shape((PT // 4, D)...  2.7 us
    ppermute x1, starting transfers between devices, on_device(): got_half = lax.ppermute(give, 'pa', [(i, i ^ 1) for i in range(peers)])  1.61 us
    all_to_all x1, waiting for transfers between devices, on_device(): lax.all_to_all(both, 'pa', 0, 0, axis_index_groups=same_core, tiled=True)  1.22 us
  transfers between devices with their start and end apart: 8, of which 5 were waited for; matrix products, arithmetic and copies ran while one was open for 0% of the time, Pallas kernels for 3%

profile of v7, /device:TPU:0, one launch (start us, length us, event | category | flops | bytes accessed | tf_op | source)
XLA Modules:
  0.0 59.9 jit_solution(12000914652922075384)
XLA Ops:
  0.6 0.0 copy-start
  0.6 5.7 %shard_map.67 = (f32[32,8,128]{2,1,0:T(8,128)S(1)}, f32[8,128]{1,0:T(8,128)S(1)}, f32[16,8,256]{2,1,0:T(8,128)S(1)}, bf16[4096,128]{1,0:T(8,128)(2,1)S(1)}, bf16...) custom-call(s32[16]{0:T(128)} %bitcast.14, ...), custom_call_target="tpu_custom_call" | custom-call | flops 2000000000 | bytes 3000000 | tf_op jit(solution)/shard_map/pallas_call | solution.py:263
  6.3 27.2 %all_to_all.10.stat_ref = f32[32,8,128]{2,1,0:T(8,128)S(1)} all-to-all(f32[32,8,128]{2,1,0:T(8,128)S(1)} %get-tuple-element.21), channel_id=1, replica_groups=mesh['pb'=4,'pa'=32] {'pa'}, dimensions={0} | all-to-all | bytes 262144 | tf_op jit(solution)/shard_map/all_to_all | solution.py:286
  33.5 0.0 copy-done
  33.6 2.7 %shard_map.68 = (f32[1,128]{1,0:T(1,128)S(1)}, f32[16,128,128]{2,1,0:T(8,128)S(1)}, f32[16,128,128]{2,1,0:T(8,128)S(1)}, f32[360,128]{1,0:T(8,128)S(1)}, bf16[36...) custom-call(s32[16]{0:T(128)} %bitcast.15, s32[1,128]{1,0:T(1,128)S(1)} %bitcast.12, ...), custom_call_target="tpu_custom_call" | custom-call | flops 5000000000 | bytes 5000000 | tf_op jit(solution)/shard_map/pallas_call | solution.py:289
  36.3 1.6 %collective-permute-start.6 = (f32[16,128,128]{2,1,0:T(8,128)S(1)}, f32[16,128,128]{2,1,0:T(8,128)S(1)}, u32[]{:S(2)}, u32[]{:S(2)}) collective-permute-start(f32[16,128,128]{2,1,0:T(8,128)S(1)} %get-tuple-element.37), channel_id=1, source_target_pairs={{0,1},{1,0},{2,3},{3,2},{4,5},{5,4},{6,7},{7,6},{8,9},{9,8},{10,11... | collective-permute-start | bytes 3145736 | tf_op jit(solution)/shard_map/ppermute | solution.py:314
  37.9 0.0 collective-permute-start
  37.9 0.0 collective-permute-start.1
  37.9 2.0 %collective-permute-start.2 = (bf16[360,128]{1,0:T(8,128)(2,1)S(1)}, bf16[360,128]{1,0:T(8,128)(2,1)S(1)}, u32[]{:S(2)}, u32[]{:S(2)}) collective-permute-start(bf16[360,128]{1,0:T(8,128)(2,1)S(1)} %get-tuple-element.34), channel_id=1, source_target_pairs={{0,32},{32,64},{64,96},{96,0},{1,33},{33,65},{65,97},{97,1},{2,34}... | collective-permute-start | bytes 276488 | tf_op jit(solution)/shard_map/ppermute | solution.py:245
  39.9 0.3 collective-permute-done.6.got_ref
  40.2 0.9 %shard_map.71 = bf16[16,128,128]{2,1,0:T(8,128)(2,1)} custom-call(f32[16,128,128]{2,1,0:T(8,128)S(1)} %get-tuple-element.36.keep_ref, f32[16,128,128]{2,1,0:T(8,128)S(1)} %collective-permute-done.6.got_ref), custom_call_target="tpu_custom_call" | custom-call | flops 10000000000 | tf_op jit(solution)/shard_map/pallas_call | solution.py:315
  41.1 6.2 %all-to-all-start.1 = ((bf16[16,128,128]{2,1,0:T(8,128)(2,1)}), bf16[16,128,128]{2,1,0:T(8,128)(2,1)S(1)}, u32[]{:S(2)}, u32[]{:S(2)}) async-start(bf16[16,128,128]{2,1,0:T(8,128)(2,1)} %shard_map.71), calls=%async_computation.1 | async-start | bytes 1048576 | tf_op jit(solution)/shard_map/all_to_all | solution.py:317
  47.3 0.0 collective-permute-done.a_ref
  47.3 0.0 collective-permute-done.1.b_ref
  47.3 0.0 collective-permute-done.2.c_ref
  47.4 2.2 %collective-permute-start.5 = (bf16[360,128]{1,0:T(8,128)(2,1)S(1)}, bf16[360,128]{1,0:T(8,128)(2,1)S(1)}, u32[]{:S(2)}, u32[]{:S(2)}) collective-permute-start(bf16[360,128]{1,0:T(8,128)(2,1)S(1)} %shard_map.69.own_ref), channel_id=1, source_target_pairs={{0,96},{32,0},{64,32},{96,64},{1,97},{33,1},{65,33},{97,65},{2,98}... | collective-permute-start | bytes 276488 | tf_op jit(solution)/shard_map/ppermute | solution.py:245
  49.6 1.6 %collective-permute-start.4 = (bf16[360,128]{1,0:T(8,128)(2,1)S(1)}, bf16[360,128]{1,0:T(8,128)(2,1)S(1)}, u32[]{:S(2)}, u32[]{:S(2)}) collective-permute-start(bf16[360,128]{1,0:T(8,128)(2,1)S(1)} %shard_map.69.own_ref), channel_id=1, source_target_pairs={{0,64},{32,96},{64,0},{96,32},{1,65},{33,97},{65,1},{97,33},{2,66}... | collective-permute-start | bytes 276488 | tf_op jit(solution)/shard_map/ppermute | solution.py:245
  51.1 1.3 %collective-permute-start.3 = (bf16[360,128]{1,0:T(8,128)(2,1)S(1)}, bf16[360,128]{1,0:T(8,128)(2,1)S(1)}, u32[]{:S(2)}, u32[]{:S(2)}) collective-permute-start(bf16[360,128]{1,0:T(8,128)(2,1)S(1)} %shard_map.69.own_ref), channel_id=1, source_target_pairs={{0,32},{32,64},{64,96},{96,0},{1,33},{33,65},{65,97},{97,1},{2,34}... | collective-permute-start | bytes 276488 | tf_op jit(solution)/shard_map/ppermute | solution.py:245
  52.5 0.2 collective-permute-done.5.c_ref
  52.7 3.3 %collective-permute-done.4.b_ref = bf16[360,128]{1,0:T(8,128)(2,1)S(1)} collective-permute-done((bf16[360,128]{1,0:T(8,128)(2,1)S(1)}, bf16[360,128]{1,0:T(8,128)(2,1)S(1)}, u32[]{:S(2)}, u32[]{:S(2)}) %collective-permute-start.4) | collective-permute-done | bytes 92192 | tf_op jit(solution)/shard_map/ppermute | solution.py:245
  56.0 1.0 %collective-permute-done.3.a_ref = bf16[360,128]{1,0:T(8,128)(2,1)S(1)} collective-permute-done((bf16[360,128]{1,0:T(8,128)(2,1)S(1)}, bf16[360,128]{1,0:T(8,128)(2,1)S(1)}, u32[]{:S(2)}, u32[]{:S(2)}) %collective-permute-start.3) | collective-permute-done | bytes 92192 | tf_op jit(solution)/shard_map/ppermute | solution.py:245
  57.0 1.0 %shard_map.70 = (f32[1440,128]{1,0:T(8,128)}, f32[1,4]{1,0:T(1,128)}) custom-call(f32[1,128]{1,0:T(1,128)S(1)} %get-tuple-element.30.loss_ref, bf16[360,128]{1,0:T(8,128)(2,1)S(1)} %shard_map.69.own_ref, bf16[360,128]{1,0:T(8,128)(2,1)S(1)} %collective-permute-done.3.a_ref, bf16[360,128]{1,0:T(8,128)(2,1)S(1)} %collective-permute-done.4.b_ref, ...), custom_call_target="tpu_custom_call" | custom-call | bytes 1000000 | tf_op jit(solution)/shard_map/pallas_call | solution.py:320
  57.9 1.2 %all-to-all-done.1.terms_ref = bf16[16,128,128]{2,1,0:T(8,128)(2,1)S(1)} async-done(((bf16[16,128,128]{2,1,0:T(8,128)(2,1)}), bf16[16,128,128]{2,1,0:T(8,128)(2,1)S(1)}, u32[]{:S(2)}, u32[]{:S(2)}) %all-to-all-start.1) | async-done | bytes 524320 | tf_op jit(solution)/shard_map/all_to_all | solution.py:317
  59.1 0.8 %shard_map.72 = f32[128,128]{1,0:T(8,128)} custom-call(bf16[16,128,128]{2,1,0:T(8,128)(2,1)S(1)} %all-to-all-done.1.terms_ref), custom_call_target="tpu_custom_call" | custom-call | bytes 1000000 | tf_op jit(solution)/shard_map/pallas_call | solution.py:323
  (1 shorter events, 0.0 us)
Async XLA Ops:
  0.6 32.9 %copy-start = (s32[128]{0:T(128)S(1)}, s32[128]{0:T(128)}, u32[]{:S(2)}) copy-start(s32[128]{0:T(128)} %param.7) | copy-start | bytes 1540
  36.3 3.9 %collective-permute-start.6 = (f32[16,128,128]{2,1,0:T(8,128)S(1)}, f32[16,128,128]{2,1,0:T(8,128)S(1)}, u32[]{:S(2)}, u32[]{:S(2)}) collective-permute-start(f32[16,128,128]{2,1,0:T(8,128)S(1)} %get-tuple-element.37), channel_id=1, source_target_pairs={{0,1},{1,0},{2,3},{3,2},{4,5},{5,4},{6,7},{7,6},{8,9},{9,8},{10,11... | collective-permute-start | bytes 3145736 | tf_op jit(solution)/shard_map/ppermute | solution.py:314
  37.9 9.4 %collective-permute-start = (bf16[360,128]{1,0:T(8,128)(2,1)S(1)}, bf16[360,128]{1,0:T(8,128)(2,1)S(1)}, u32[]{:S(2)}, u32[]{:S(2)}) collective-permute-start(bf16[360,128]{1,0:T(8,128)(2,1)S(1)} %get-tuple-element.32), channel_id=1, source_target_pairs={{0,96},{32,0},{64,32},{96,64},{1,97},{33,1},{65,33},{97,65},{2,98}... | collective-permute-start | bytes 276488 | tf_op jit(solution)/shard_map/ppermute | solution.py:245
  37.9 9.4 %collective-permute-start.1 = (bf16[360,128]{1,0:T(8,128)(2,1)S(1)}, bf16[360,128]{1,0:T(8,128)(2,1)S(1)}, u32[]{:S(2)}, u32[]{:S(2)}) collective-permute-start(bf16[360,128]{1,0:T(8,128)(2,1)S(1)} %get-tuple-element.33), channel_id=1, source_target_pairs={{0,64},{32,96},{64,0},{96,32},{1,65},{33,97},{65,1},{97,33},{2,66}... | collective-permute-start | bytes 276488 | tf_op jit(solution)/shard_map/ppermute | solution.py:245
  37.9 9.4 %collective-permute-start.2 = (bf16[360,128]{1,0:T(8,128)(2,1)S(1)}, bf16[360,128]{1,0:T(8,128)(2,1)S(1)}, u32[]{:S(2)}, u32[]{:S(2)}) collective-permute-start(bf16[360,128]{1,0:T(8,128)(2,1)S(1)} %get-tuple-element.34), channel_id=1, source_target_pairs={{0,32},{32,64},{64,96},{96,0},{1,33},{33,65},{65,97},{97,1},{2,34}... | collective-permute-start | bytes 276488 | tf_op jit(solution)/shard_map/ppermute | solution.py:245
  41.1 18.1 %all-to-all-start.1 = ((bf16[16,128,128]{2,1,0:T(8,128)(2,1)}), bf16[16,128,128]{2,1,0:T(8,128)(2,1)S(1)}, u32[]{:S(2)}, u32[]{:S(2)}) async-start(bf16[16,128,128]{2,1,0:T(8,128)(2,1)} %shard_map.71), calls=%async_computation.1 | async-start | bytes 1048576 | tf_op jit(solution)/shard_map/all_to_all | solution.py:317
  47.4 5.3 %collective-permute-start.5 = (bf16[360,128]{1,0:T(8,128)(2,1)S(1)}, bf16[360,128]{1,0:T(8,128)(2,1)S(1)}, u32[]{:S(2)}, u32[]{:S(2)}) collective-permute-start(bf16[360,128]{1,0:T(8,128)(2,1)S(1)} %shard_map.69.own_ref), channel_id=1, source_target_pairs={{0,96},{32,0},{64,32},{96,64},{1,97},{33,1},{65,33},{97,65},{2,98}... | collective-permute-start | bytes 276488 | tf_op jit(solution)/shard_map/ppermute | solution.py:245
  49.6 6.4 %collective-permute-start.4 = (bf16[360,128]{1,0:T(8,128)(2,1)S(1)}, bf16[360,128]{1,0:T(8,128)(2,1)S(1)}, u32[]{:S(2)}, u32[]{:S(2)}) collective-permute-start(bf16[360,128]{1,0:T(8,128)(2,1)S(1)} %shard_map.69.own_ref), channel_id=1, source_target_pairs={{0,64},{32,96},{64,0},{96,32},{1,65},{33,97},{65,1},{97,33},{2,66}... | collective-permute-start | bytes 276488 | tf_op jit(solution)/shard_map/ppermute | solution.py:245
  51.1 5.8 %collective-permute-start.3 = (bf16[360,128]{1,0:T(8,128)(2,1)S(1)}, bf16[360,128]{1,0:T(8,128)(2,1)S(1)}, u32[]{:S(2)}, u32[]{:S(2)}) collective-permute-start(bf16[360,128]{1,0:T(8,128)(2,1)S(1)} %shard_map.69.own_ref), channel_id=1, source_target_pairs={{0,32},{32,64},{64,96},{96,0},{1,33},{33,65},{65,97},{97,1},{2,34}... | collective-permute-start | bytes 276488 | tf_op jit(solution)/shard_map/ppermute | solution.py:245

commit v8 on v7

--- a/solution.py
+++ b/solution.py
@@ -102,6 +102,26 @@
                 scaled_ref[i] = scaled
                 tot_ref[k] = jnp.sum(scaled.reshape(LP, B, QT), axis=0)
 
+    lane_block = iota((B, blocks * B), 1) // B
+    active = jnp.zeros((B, blocks * B), jnp.int32)
+    for k in range(blocks):
+        active = jnp.where(lane_block == k, mask_s[k], active)
+    active = active > 0
+    def finish():
+        score = pack_means(top_ref[...] + jnp.log(tot_ref[...]))
+        logit = jnp.where(active, score / contrast_temp, very_low)
+        logit_ref[...] = logit
+        positive = (pos_ref[...] == iota(logit.shape, 0) + lax.axis_index("pa") * B) & active
+        local_top = jnp.max(logit, axis=0, keepdims=True)
+        scaled = jnp.where(active, jnp.exp(logit - local_top), 0.0)
+        local_total = jnp.sum(scaled, axis=0, keepdims=True)
+        local_pos = jnp.sum(jnp.where(positive, logit, 0.0), axis=0, keepdims=True)
+        row = iota(logit.shape, 0)
+        send = jnp.where(row == 0, local_top, jnp.where(row == 1, local_total, local_pos))
+        send_ref[...] = jnp.broadcast_to(jnp.where(row < 3, send, 0.0)[None], send_ref.shape)
+
+    finish()
+
     safe = (jnp.min(tot_ref[...]) > safe_low) & (jnp.max(tot_ref[...]) < safe_high)
 
     @pl.when(jnp.logical_not(safe))
@@ -121,22 +141,7 @@
                     tot_ref[k] = jnp.sum(scaled, axis=0)
                     scaled_ref[i] = scaled.reshape(PT, QT)
 
-    lane_block = iota((B, blocks * B), 1) // B
-    active = jnp.zeros((B, blocks * B), jnp.int32)
-    for k in range(blocks):
-        active = jnp.where(lane_block == k, mask_s[k], active)
-    active = active > 0
-    score = pack_means(top_ref[...] + jnp.log(tot_ref[...]))
-    logit = jnp.where(active, score / contrast_temp, very_low)
-    logit_ref[...] = logit
-    positive = (pos_ref[...] == iota(logit.shape, 0) + lax.axis_index("pa") * B) & active
-    local_top = jnp.max(logit, axis=0, keepdims=True)
-    scaled = jnp.where(active, jnp.exp(logit - local_top), 0.0)
-    local_total = jnp.sum(scaled, axis=0, keepdims=True)
-    local_pos = jnp.sum(jnp.where(positive, logit, 0.0), axis=0, keepdims=True)
-    row = iota(logit.shape, 0)
-    send = jnp.where(row == 0, local_top, jnp.where(row == 1, local_total, local_pos))
-    send_ref[...] = jnp.broadcast_to(jnp.where(row < 3, send, 0.0)[None], send_ref.shape)
+        finish()
 
 
 def grads_kernel(

time: 60.3 us -> 60.4 us (level); the launches traced: 59.9 us -> 60.8 us
  Pallas kernels: 11 us -> 26.9 us
  blocking collectives: 27.2 us -> 15.8 us
  starting transfers between devices: 15 us -> 9.43 us
  waiting for transfers between devices: 5.97 us -> 7.9 us
    pallas_call x1, Pallas kernels: 5.67 us -> 17.2 us  [on_device(): call(scores_kernel, (shape((peers, B, rows), f32), packed, wide, shape((r...]
    all_to_all x1, blocking collectives: 27.2 us -> 15.8 us  [on_device(): stats = lax.all_to_all(send, 'pa', 0, 0, tiled=True)]
    pallas_call x1, Pallas kernels: 2.7 us -> 6.98 us  [on_device(): call(grads_kernel, (shape((1, rows), f32), half, half, shape((PT // 4, D)...]
    all_to_all x1, starting transfers between devices: 6.24 us -> 3.57 us  [on_device(): lax.all_to_all(both, 'pa', 0, 0, axis_index_groups=same_core, tiled=True)]
    ppermute x6, waiting for transfers between devices: 4.5 us -> 6.42 us  [turn(): return lax.ppermute(x, 'pb', [(i, (i + s) % 4) for i in range(4)])]
    ppermute x1, starting transfers between devices: 1.61 us -> 0.09 us  [on_device(): got_half = lax.ppermute(give, 'pa', [(i, i ^ 1) for i in range(peers)])]
    ppermute x6, starting transfers between devices: 7.11 us -> 5.77 us  [turn(): return lax.ppermute(x, 'pb', [(i, (i + s) % 4) for i in range(4)])]
  transfers between devices with their start and end apart: 8 -> 8, of which waited for: 5 -> 6; matrix products, arithmetic and copies ran while one was open for 0% -> 0% of each run, Pallas kernels for 3% -> 3%
where the time goes in v8:
time: 60.4 us; the launch traced here: 60.8 us
  Pallas kernels  26.9 us (45%)
  blocking collectives  15.8 us (26%)
  starting transfers between devices  9.43 us (16%)
  waiting for transfers between devices  7.9 us (13%)
  between operations  0.71 us (1%)
    pallas_call x1, Pallas kernels, on_device(): call(scores_kernel, (shape((peers, B, rows), f32), packed, wide, shape((r...  17.2 us
    all_to_all x1, blocking collectives, on_device(): stats = lax.all_to_all(send, 'pa', 0, 0, tiled=True)  15.8 us
    pallas_call x1, Pallas kernels, on_device(): call(grads_kernel, (shape((1, rows), f32), half, half, shape((PT // 4, D)...  6.98 us
    ppermute x6, waiting for transfers between devices, turn(): return lax.ppermute(x, 'pb', [(i, (i + s) % 4) for i in range(4)])  6.42 us
    ppermute x6, starting transfers between devices, turn(): return lax.ppermute(x, 'pb', [(i, (i + s) % 4) for i in range(4)])  5.77 us
    all_to_all x1, starting transfers between devices, on_device(): lax.all_to_all(both, 'pa', 0, 0, axis_index_groups=same_core, tiled=True)  3.57 us
  transfers between devices with their start and end apart: 8, of which 6 were waited for; matrix products, arithmetic and copies ran while one was open for 0% of the time, Pallas kernels for 3%

profile of v8, /device:TPU:0, one launch (start us, length us, event | category | flops | bytes accessed | tf_op | source)
XLA Modules:
  0.0 60.8 jit_solution(12517674994281353263)
XLA Ops:
  0.6 0.0 copy-start
  0.6 17.2 %shard_map.67 = (f32[32,8,128]{2,1,0:T(8,128)S(1)}, f32[8,128]{1,0:T(8,128)S(1)}, f32[16,8,256]{2,1,0:T(8,128)S(1)}, bf16[4096,128]{1,0:T(8,128)(2,1)S(1)}, bf16...) custom-call(s32[16]{0:T(128)} %bitcast.14, ...), custom_call_target="tpu_custom_call" | custom-call | flops 2000000000 | bytes 3000000 | tf_op jit(solution)/shard_map/pallas_call | solution.py:268
  17.8 15.8 %all_to_all.10.stat_ref = f32[32,8,128]{2,1,0:T(8,128)S(1)} all-to-all(f32[32,8,128]{2,1,0:T(8,128)S(1)} %get-tuple-element.21), channel_id=1, replica_groups=mesh['pb'=4,'pa'=32] {'pa'}, dimensions={0} | all-to-all | bytes 262144 | tf_op jit(solution)/shard_map/all_to_all | solution.py:291
  33.7 0.0 copy-done
  33.7 7.0 %shard_map.68 = (f32[1,128]{1,0:T(1,128)S(1)}, f32[16,128,128]{2,1,0:T(8,128)S(1)}, f32[16,128,128]{2,1,0:T(8,128)S(1)}, f32[360,128]{1,0:T(8,128)S(1)}, bf16[36...) custom-call(s32[16]{0:T(128)} %bitcast.15, s32[1,128]{1,0:T(1,128)S(1)} %bitcast.12, ...), custom_call_target="tpu_custom_call" | custom-call | flops 5000000000 | bytes 5000000 | tf_op jit(solution)/shard_map/pallas_call | solution.py:294
  40.7 0.1 collective-permute-start.6
  40.8 0.1 collective-permute-start
  40.9 0.1 collective-permute-start.1
  41.0 1.9 %collective-permute-start.2 = (bf16[360,128]{1,0:T(8,128)(2,1)S(1)}, bf16[360,128]{1,0:T(8,128)(2,1)S(1)}, u32[]{:S(2)}, u32[]{:S(2)}) collective-permute-start(bf16[360,128]{1,0:T(8,128)(2,1)S(1)} %get-tuple-element.34), channel_id=1, source_target_pairs={{0,32},{32,64},{64,96},{96,0},{1,33},{33,65},{65,97},{97,1},{2,34}... | collective-permute-start | bytes 276488 | tf_op jit(solution)/shard_map/ppermute | solution.py:250
  42.9 0.5 collective-permute-done.6.got_ref
  43.4 0.9 %shard_map.71 = bf16[16,128,128]{2,1,0:T(8,128)(2,1)} custom-call(f32[16,128,128]{2,1,0:T(8,128)S(1)} %get-tuple-element.36.keep_ref, f32[16,128,128]{2,1,0:T(8,128)S(1)} %collective-permute-done.6.got_ref), custom_call_target="tpu_custom_call" | custom-call | flops 10000000000 | tf_op jit(solution)/shard_map/pallas_call | solution.py:320
  44.3 3.6 %all-to-all-start.1 = ((bf16[16,128,128]{2,1,0:T(8,128)(2,1)}), bf16[16,128,128]{2,1,0:T(8,128)(2,1)S(1)}, u32[]{:S(2)}, u32[]{:S(2)}) async-start(bf16[16,128,128]{2,1,0:T(8,128)(2,1)} %shard_map.71), calls=%async_computation.1 | async-start | bytes 1048576 | tf_op jit(solution)/shard_map/all_to_all | solution.py:322
  47.9 0.0 collective-permute-done.a_ref
  47.9 0.0 collective-permute-done.1.b_ref
  47.9 1.4 %collective-permute-done.2.c_ref = bf16[360,128]{1,0:T(8,128)(2,1)S(1)} collective-permute-done((bf16[360,128]{1,0:T(8,128)(2,1)S(1)}, bf16[360,128]{1,0:T(8,128)(2,1)S(1)}, u32[]{:S(2)}, u32[]{:S(2)}) %collective-permute-start.2) | collective-permute-done | bytes 92192 | tf_op jit(solution)/shard_map/ppermute | solution.py:250
  49.4 1.3 %collective-permute-start.5 = (bf16[360,128]{1,0:T(8,128)(2,1)S(1)}, bf16[360,128]{1,0:T(8,128)(2,1)S(1)}, u32[]{:S(2)}, u32[]{:S(2)}) collective-permute-start(bf16[360,128]{1,0:T(8,128)(2,1)S(1)} %shard_map.69.own_ref), channel_id=1, source_target_pairs={{0,96},{32,0},{64,32},{96,64},{1,97},{33,1},{65,33},{97,65},{2,98}... | collective-permute-start | bytes 276488 | tf_op jit(solution)/shard_map/ppermute | solution.py:250
  50.6 1.1 %collective-permute-start.4 = (bf16[360,128]{1,0:T(8,128)(2,1)S(1)}, bf16[360,128]{1,0:T(8,128)(2,1)S(1)}, u32[]{:S(2)}, u32[]{:S(2)}) collective-permute-start(bf16[360,128]{1,0:T(8,128)(2,1)S(1)} %shard_map.69.own_ref), channel_id=1, source_target_pairs={{0,64},{32,96},{64,0},{96,32},{1,65},{33,97},{65,1},{97,33},{2,66}... | collective-permute-start | bytes 276488 | tf_op jit(solution)/shard_map/ppermute | solution.py:250
  51.7 1.3 %collective-permute-start.3 = (bf16[360,128]{1,0:T(8,128)(2,1)S(1)}, bf16[360,128]{1,0:T(8,128)(2,1)S(1)}, u32[]{:S(2)}, u32[]{:S(2)}) collective-permute-start(bf16[360,128]{1,0:T(8,128)(2,1)S(1)} %shard_map.69.own_ref), channel_id=1, source_target_pairs={{0,32},{32,64},{64,96},{96,0},{1,33},{33,65},{65,97},{97,1},{2,34}... | collective-permute-start | bytes 276488 | tf_op jit(solution)/shard_map/ppermute | solution.py:250
  53.1 1.9 %collective-permute-done.5.c_ref = bf16[360,128]{1,0:T(8,128)(2,1)S(1)} collective-permute-done((bf16[360,128]{1,0:T(8,128)(2,1)S(1)}, bf16[360,128]{1,0:T(8,128)(2,1)S(1)}, u32[]{:S(2)}, u32[]{:S(2)}) %collective-permute-start.5) | collective-permute-done | bytes 92192 | tf_op jit(solution)/shard_map/ppermute | solution.py:250
  55.0 2.7 %collective-permute-done.4.b_ref = bf16[360,128]{1,0:T(8,128)(2,1)S(1)} collective-permute-done((bf16[360,128]{1,0:T(8,128)(2,1)S(1)}, bf16[360,128]{1,0:T(8,128)(2,1)S(1)}, u32[]{:S(2)}, u32[]{:S(2)}) %collective-permute-start.4) | collective-permute-done | bytes 92192 | tf_op jit(solution)/shard_map/ppermute | solution.py:250
  57.6 0.4 collective-permute-done.3.a_ref
  58.1 1.0 %shard_map.70 = (f32[1440,128]{1,0:T(8,128)}, f32[1,4]{1,0:T(1,128)}) custom-call(f32[1,128]{1,0:T(1,128)S(1)} %get-tuple-element.30.loss_ref, bf16[360,128]{1,0:T(8,128)(2,1)S(1)} %shard_map.69.own_ref, bf16[360,128]{1,0:T(8,128)(2,1)S(1)} %collective-permute-done.3.a_ref, bf16[360,128]{1,0:T(8,128)(2,1)S(1)} %collective-permute-done.4.b_ref, ...), custom_call_target="tpu_custom_call" | custom-call | bytes 1000000 | tf_op jit(solution)/shard_map/pallas_call | solution.py:325
  59.0 0.9 %all-to-all-done.1.terms_ref = bf16[16,128,128]{2,1,0:T(8,128)(2,1)S(1)} async-done(((bf16[16,128,128]{2,1,0:T(8,128)(2,1)}), bf16[16,128,128]{2,1,0:T(8,128)(2,1)S(1)}, u32[]{:S(2)}, u32[]{:S(2)}) %all-to-all-start.1) | async-done | bytes 524320 | tf_op jit(solution)/shard_map/all_to_all | solution.py:322
  60.0 0.8 %shard_map.72 = f32[128,128]{1,0:T(8,128)} custom-call(bf16[16,128,128]{2,1,0:T(8,128)(2,1)S(1)} %all-to-all-done.1.terms_ref), custom_call_target="tpu_custom_call" | custom-call | bytes 1000000 | tf_op jit(solution)/shard_map/pallas_call | solution.py:328
  (1 shorter events, 0.0 us)
Async XLA Ops:
  0.6 33.1 %copy-start = (s32[128]{0:T(128)S(1)}, s32[128]{0:T(128)}, u32[]{:S(2)}) copy-start(s32[128]{0:T(128)} %param.7) | copy-start | bytes 1540
  40.7 2.7 %collective-permute-start.6 = (f32[16,128,128]{2,1,0:T(8,128)S(1)}, f32[16,128,128]{2,1,0:T(8,128)S(1)}, u32[]{:S(2)}, u32[]{:S(2)}) collective-permute-start(f32[16,128,128]{2,1,0:T(8,128)S(1)} %get-tuple-element.37), channel_id=1, source_target_pairs={{0,1},{1,0},{2,3},{3,2},{4,5},{5,4},{6,7},{7,6},{8,9},{9,8},{10,11... | collective-permute-start | bytes 3145736 | tf_op jit(solution)/shard_map/ppermute | solution.py:319
  40.8 7.1 %collective-permute-start = (bf16[360,128]{1,0:T(8,128)(2,1)S(1)}, bf16[360,128]{1,0:T(8,128)(2,1)S(1)}, u32[]{:S(2)}, u32[]{:S(2)}) collective-permute-start(bf16[360,128]{1,0:T(8,128)(2,1)S(1)} %get-tuple-element.32), channel_id=1, source_target_pairs={{0,96},{32,0},{64,32},{96,64},{1,97},{33,1},{65,33},{97,65},{2,98}... | collective-permute-start | bytes 276488 | tf_op jit(solution)/shard_map/ppermute | solution.py:250
  40.9 7.1 %collective-permute-start.1 = (bf16[360,128]{1,0:T(8,128)(2,1)S(1)}, bf16[360,128]{1,0:T(8,128)(2,1)S(1)}, u32[]{:S(2)}, u32[]{:S(2)}) collective-permute-start(bf16[360,128]{1,0:T(8,128)(2,1)S(1)} %get-tuple-element.33), channel_id=1, source_target_pairs={{0,64},{32,96},{64,0},{96,32},{1,65},{33,97},{65,1},{97,33},{2,66}... | collective-permute-start | bytes 276488 | tf_op jit(solution)/shard_map/ppermute | solution.py:250
  41.0 8.4 %collective-permute-start.2 = (bf16[360,128]{1,0:T(8,128)(2,1)S(1)}, bf16[360,128]{1,0:T(8,128)(2,1)S(1)}, u32[]{:S(2)}, u32[]{:S(2)}) collective-permute-start(bf16[360,128]{1,0:T(8,128)(2,1)S(1)} %get-tuple-element.34), channel_id=1, source_target_pairs={{0,32},{32,64},{64,96},{96,0},{1,33},{33,65},{65,97},{97,1},{2,34}... | collective-permute-start | bytes 276488 | tf_op jit(solution)/shard_map/ppermute | solution.py:250
  44.3 15.7 %all-to-all-start.1 = ((bf16[16,128,128]{2,1,0:T(8,128)(2,1)}), bf16[16,128,128]{2,1,0:T(8,128)(2,1)S(1)}, u32[]{:S(2)}, u32[]{:S(2)}) async-start(bf16[16,128,128]{2,1,0:T(8,128)(2,1)} %shard_map.71), calls=%async_computation.1 | async-start | bytes 1048576 | tf_op jit(solution)/shard_map/all_to_all | solution.py:322
  49.4 5.6 %collective-permute-start.5 = (bf16[360,128]{1,0:T(8,128)(2,1)S(1)}, bf16[360,128]{1,0:T(8,128)(2,1)S(1)}, u32[]{:S(2)}, u32[]{:S(2)}) collective-permute-start(bf16[360,128]{1,0:T(8,128)(2,1)S(1)} %shard_map.69.own_ref), channel_id=1, source_target_pairs={{0,96},{32,0},{64,32},{96,64},{1,97},{33,1},{65,33},{97,65},{2,98}... | collective-permute-start | bytes 276488 | tf_op jit(solution)/shard_map/ppermute | solution.py:250
  50.6 7.0 %collective-permute-start.4 = (bf16[360,128]{1,0:T(8,128)(2,1)S(1)}, bf16[360,128]{1,0:T(8,128)(2,1)S(1)}, u32[]{:S(2)}, u32[]{:S(2)}) collective-permute-start(bf16[360,128]{1,0:T(8,128)(2,1)S(1)} %shard_map.69.own_ref), channel_id=1, source_target_pairs={{0,64},{32,96},{64,0},{96,32},{1,65},{33,97},{65,1},{97,33},{2,66}... | collective-permute-start | bytes 276488 | tf_op jit(solution)/shard_map/ppermute | solution.py:250
  51.7 6.3 %collective-permute-start.3 = (bf16[360,128]{1,0:T(8,128)(2,1)S(1)}, bf16[360,128]{1,0:T(8,128)(2,1)S(1)}, u32[]{:S(2)}, u32[]{:S(2)}) collective-permute-start(bf16[360,128]{1,0:T(8,128)(2,1)S(1)} %shard_map.69.own_ref), channel_id=1, source_target_pairs={{0,32},{32,64},{64,96},{96,0},{1,33},{33,65},{65,97},{97,1},{2,34}... | collective-permute-start | bytes 276488 | tf_op jit(solution)/shard_map/ppermute | solution.py:250

commit v9 on v8

--- a/solution.py
+++ b/solution.py
@@ -166,9 +166,13 @@
     prob = jnp.where(active, jnp.exp(logit - glob_top) / glob_total, 0.0)
     coef = (prob - positive.astype(f32)) / (contrast_temp * LQ)
     weight_ref[...] = unpack(coef) / tot_ref[...]
-    gp_ref[...] = jnp.zeros_like(gp_ref)
     fetch.wait()
     count = list_tasks(mask_s, order)
+
+    @pl.when(count <= 0)
+    def _():
+        gp_ref[...] = jnp.zeros_like(gp_ref)
+
     core = lax.rem(lax.axis_index("pa"), 2)
     for group, scaled_ref in enumerate(scaled_refs):
 
@@ -179,7 +183,8 @@
                 dsim = (scaled_ref[i].reshape(LP, B, QT) * weight_ref[k][None]).astype(bf16)
                 dsim_ref[:, i * QT : (i + 1) * QT] = dsim.reshape(PT, QT)
             queries = jnp.concatenate([block_rows(q_ref, k) for k in tasks], axis=0)
-            gp_ref[...] += jnp.dot(dsim_ref[...], queries, preferred_element_type=f32)
+            terms = jnp.dot(dsim_ref[...], queries, preferred_element_type=f32)
+            gp_ref[...] = terms if group == 0 else gp_ref[...] + terms
             turned = jnp.dot(turn_ref[...], dsim_ref[...], preferred_element_type=f32)
             for i, k in enumerate(tasks):
                 first, second = (turned[:, i * QT + j * D : i * QT + (j + 1) * D] for j in range(2))

time: 60.4 us -> 60.9 us (level)
  no operation moved by 1% of the time
where the time goes in v9:
time: 60.9 us
  Pallas kernels  26.8 us (44%)
  blocking collectives  16 us (26%)
  starting transfers between devices  9.49 us (16%)
  waiting for transfers between devices  7.86 us (13%)
  between operations  0.7 us (1%)
    pallas_call x1, Pallas kernels, on_device(): call(scores_kernel, (shape((peers, B, rows), f32), packed, wide, shape((r...  17.2 us
    all_to_all x1, blocking collectives, on_device(): stats = lax.all_to_all(send, 'pa', 0, 0, tiled=True)  16 us
    pallas_call x1, Pallas kernels, on_device(): call(grads_kernel, (shape((1, rows), f32), half, half, shape((PT // 4, D)...  6.96 us
    ppermute x6, waiting for transfers between devices, turn(): return lax.ppermute(x, 'pb', [(i, (i + s) % 4) for i in range(4)])  6.41 us
    ppermute x6, starting transfers between devices, turn(): return lax.ppermute(x, 'pb', [(i, (i + s) % 4) for i in range(4)])  5.73 us
    all_to_all x1, starting transfers between devices, on_device(): lax.all_to_all(both, 'pa', 0, 0, axis_index_groups=same_core, tiled=True)  3.57 us
  transfers between devices with their start and end apart: 8, of which 6 were waited for; matrix products, arithmetic and copies ran while one was open for 0% of the time, Pallas kernels for 3%

profile of v9, /device:TPU:0, one launch (start us, length us, event | category | flops | bytes accessed | tf_op | source)
XLA Modules:
  0.0 60.9 jit_solution(3876867107303285206)
XLA Ops:
  0.6 0.0 copy-start
  0.6 17.2 %shard_map.67 = (f32[32,8,128]{2,1,0:T(8,128)S(1)}, f32[8,128]{1,0:T(8,128)S(1)}, f32[16,8,256]{2,1,0:T(8,128)S(1)}, bf16[4096,128]{1,0:T(8,128)(2,1)S(1)}, bf16...) custom-call(s32[16]{0:T(128)} %bitcast.14, ...), custom_call_target="tpu_custom_call" | custom-call | flops 2000000000 | bytes 3000000 | tf_op jit(solution)/shard_map/pallas_call | solution.py:273
  17.8 16.0 %all_to_all.10.stat_ref = f32[32,8,128]{2,1,0:T(8,128)S(1)} all-to-all(f32[32,8,128]{2,1,0:T(8,128)S(1)} %get-tuple-element.21), channel_id=1, replica_groups=mesh['pb'=4,'pa'=32] {'pa'}, dimensions={0} | all-to-all | bytes 262144 | tf_op jit(solution)/shard_map/all_to_all | solution.py:296
  33.9 0.0 copy-done
  33.9 7.0 %shard_map.68 = (f32[1,128]{1,0:T(1,128)S(1)}, f32[16,128,128]{2,1,0:T(8,128)S(1)}, f32[16,128,128]{2,1,0:T(8,128)S(1)}, f32[360,128]{1,0:T(8,128)S(1)}, bf16[36...) custom-call(s32[16]{0:T(128)} %bitcast.15, s32[1,128]{1,0:T(1,128)S(1)} %bitcast.12, ...), custom_call_target="tpu_custom_call" | custom-call | flops 5000000000 | bytes 5000000 | tf_op jit(solution)/shard_map/pallas_call | solution.py:299
  40.8 0.2 collective-permute-start.6
  41.0 0.0 collective-permute-start
  41.0 0.1 collective-permute-start.1
  41.1 1.9 %collective-permute-start.2 = (bf16[360,128]{1,0:T(8,128)(2,1)S(1)}, bf16[360,128]{1,0:T(8,128)(2,1)S(1)}, u32[]{:S(2)}, u32[]{:S(2)}) collective-permute-start(bf16[360,128]{1,0:T(8,128)(2,1)S(1)} %get-tuple-element.34), channel_id=1, source_target_pairs={{0,32},{32,64},{64,96},{96,0},{1,33},{33,65},{65,97},{97,1},{2,34}... | collective-permute-start | bytes 276488 | tf_op jit(solution)/shard_map/ppermute | solution.py:255
  43.0 0.5 collective-permute-done.6.got_ref
  43.6 0.9 %shard_map.71 = bf16[16,128,128]{2,1,0:T(8,128)(2,1)} custom-call(f32[16,128,128]{2,1,0:T(8,128)S(1)} %get-tuple-element.36.keep_ref, f32[16,128,128]{2,1,0:T(8,128)S(1)} %collective-permute-done.6.got_ref), custom_call_target="tpu_custom_call" | custom-call | flops 10000000000 | tf_op jit(solution)/shard_map/pallas_call | solution.py:325
  44.5 3.6 %all-to-all-start.1 = ((bf16[16,128,128]{2,1,0:T(8,128)(2,1)}), bf16[16,128,128]{2,1,0:T(8,128)(2,1)S(1)}, u32[]{:S(2)}, u32[]{:S(2)}) async-start(bf16[16,128,128]{2,1,0:T(8,128)(2,1)} %shard_map.71), calls=%async_computation.1 | async-start | bytes 1048576 | tf_op jit(solution)/shard_map/all_to_all | solution.py:327
  48.1 0.0 collective-permute-done.a_ref
  48.1 0.0 collective-permute-done.1.b_ref
  48.1 1.4 %collective-permute-done.2.c_ref = bf16[360,128]{1,0:T(8,128)(2,1)S(1)} collective-permute-done((bf16[360,128]{1,0:T(8,128)(2,1)S(1)}, bf16[360,128]{1,0:T(8,128)(2,1)S(1)}, u32[]{:S(2)}, u32[]{:S(2)}) %collective-permute-start.2) | collective-permute-done | bytes 92192 | tf_op jit(solution)/shard_map/ppermute | solution.py:255
  49.5 1.3 %collective-permute-start.5 = (bf16[360,128]{1,0:T(8,128)(2,1)S(1)}, bf16[360,128]{1,0:T(8,128)(2,1)S(1)}, u32[]{:S(2)}, u32[]{:S(2)}) collective-permute-start(bf16[360,128]{1,0:T(8,128)(2,1)S(1)} %shard_map.69.own_ref), channel_id=1, source_target_pairs={{0,96},{32,0},{64,32},{96,64},{1,97},{33,1},{65,33},{97,65},{2,98}... | collective-permute-start | bytes 276488 | tf_op jit(solution)/shard_map/ppermute | solution.py:255
  50.8 1.1 %collective-permute-start.4 = (bf16[360,128]{1,0:T(8,128)(2,1)S(1)}, bf16[360,128]{1,0:T(8,128)(2,1)S(1)}, u32[]{:S(2)}, u32[]{:S(2)}) collective-permute-start(bf16[360,128]{1,0:T(8,128)(2,1)S(1)} %shard_map.69.own_ref), channel_id=1, source_target_pairs={{0,64},{32,96},{64,0},{96,32},{1,65},{33,97},{65,1},{97,33},{2,66}... | collective-permute-start | bytes 276488 | tf_op jit(solution)/shard_map/ppermute | solution.py:255
  51.9 1.3 %collective-permute-start.3 = (bf16[360,128]{1,0:T(8,128)(2,1)S(1)}, bf16[360,128]{1,0:T(8,128)(2,1)S(1)}, u32[]{:S(2)}, u32[]{:S(2)}) collective-permute-start(bf16[360,128]{1,0:T(8,128)(2,1)S(1)} %shard_map.69.own_ref), channel_id=1, source_target_pairs={{0,32},{32,64},{64,96},{96,0},{1,33},{33,65},{65,97},{97,1},{2,34}... | collective-permute-start | bytes 276488 | tf_op jit(solution)/shard_map/ppermute | solution.py:255
  53.2 1.9 %collective-permute-done.5.c_ref = bf16[360,128]{1,0:T(8,128)(2,1)S(1)} collective-permute-done((bf16[360,128]{1,0:T(8,128)(2,1)S(1)}, bf16[360,128]{1,0:T(8,128)(2,1)S(1)}, u32[]{:S(2)}, u32[]{:S(2)}) %collective-permute-start.5) | collective-permute-done | bytes 92192 | tf_op jit(solution)/shard_map/ppermute | solution.py:255
  55.1 2.7 %collective-permute-done.4.b_ref = bf16[360,128]{1,0:T(8,128)(2,1)S(1)} collective-permute-done((bf16[360,128]{1,0:T(8,128)(2,1)S(1)}, bf16[360,128]{1,0:T(8,128)(2,1)S(1)}, u32[]{:S(2)}, u32[]{:S(2)}) %collective-permute-start.4) | collective-permute-done | bytes 92192 | tf_op jit(solution)/shard_map/ppermute | solution.py:255
  57.8 0.5 collective-permute-done.3.a_ref
  58.2 1.0 %shard_map.70 = (f32[1440,128]{1,0:T(8,128)}, f32[1,4]{1,0:T(1,128)}) custom-call(f32[1,128]{1,0:T(1,128)S(1)} %get-tuple-element.30.loss_ref, bf16[360,128]{1,0:T(8,128)(2,1)S(1)} %shard_map.69.own_ref, bf16[360,128]{1,0:T(8,128)(2,1)S(1)} %collective-permute-done.3.a_ref, bf16[360,128]{1,0:T(8,128)(2,1)S(1)} %collective-permute-done.4.b_ref, ...), custom_call_target="tpu_custom_call" | custom-call | bytes 1000000 | tf_op jit(solution)/shard_map/pallas_call | solution.py:330
  59.2 0.9 %all-to-all-done.1.terms_ref = bf16[16,128,128]{2,1,0:T(8,128)(2,1)S(1)} async-done(((bf16[16,128,128]{2,1,0:T(8,128)(2,1)}), bf16[16,128,128]{2,1,0:T(8,128)(2,1)S(1)}, u32[]{:S(2)}, u32[]{:S(2)}) %all-to-all-start.1) | async-done | bytes 524320 | tf_op jit(solution)/shard_map/all_to_all | solution.py:327
  60.1 0.8 %shard_map.72 = f32[128,128]{1,0:T(8,128)} custom-call(bf16[16,128,128]{2,1,0:T(8,128)(2,1)S(1)} %all-to-all-done.1.terms_ref), custom_call_target="tpu_custom_call" | custom-call | bytes 1000000 | tf_op jit(solution)/shard_map/pallas_call | solution.py:333
  (1 shorter events, 0.0 us)
Async XLA Ops:
  0.6 33.2 %copy-start = (s32[128]{0:T(128)S(1)}, s32[128]{0:T(128)}, u32[]{:S(2)}) copy-start(s32[128]{0:T(128)} %param.7) | copy-start | bytes 1540
  40.8 2.7 %collective-permute-start.6 = (f32[16,128,128]{2,1,0:T(8,128)S(1)}, f32[16,128,128]{2,1,0:T(8,128)S(1)}, u32[]{:S(2)}, u32[]{:S(2)}) collective-permute-start(f32[16,128,128]{2,1,0:T(8,128)S(1)} %get-tuple-element.37), channel_id=1, source_target_pairs={{0,1},{1,0},{2,3},{3,2},{4,5},{5,4},{6,7},{7,6},{8,9},{9,8},{10,11... | collective-permute-start | bytes 3145736 | tf_op jit(solution)/shard_map/ppermute | solution.py:324
  41.0 7.0 %collective-permute-start = (bf16[360,128]{1,0:T(8,128)(2,1)S(1)}, bf16[360,128]{1,0:T(8,128)(2,1)S(1)}, u32[]{:S(2)}, u32[]{:S(2)}) collective-permute-start(bf16[360,128]{1,0:T(8,128)(2,1)S(1)} %get-tuple-element.32), channel_id=1, source_target_pairs={{0,96},{32,0},{64,32},{96,64},{1,97},{33,1},{65,33},{97,65},{2,98}... | collective-permute-start | bytes 276488 | tf_op jit(solution)/shard_map/ppermute | solution.py:255
  41.0 7.0 %collective-permute-start.1 = (bf16[360,128]{1,0:T(8,128)(2,1)S(1)}, bf16[360,128]{1,0:T(8,128)(2,1)S(1)}, u32[]{:S(2)}, u32[]{:S(2)}) collective-permute-start(bf16[360,128]{1,0:T(8,128)(2,1)S(1)} %get-tuple-element.33), channel_id=1, source_target_pairs={{0,64},{32,96},{64,0},{96,32},{1,65},{33,97},{65,1},{97,33},{2,66}... | collective-permute-start | bytes 276488 | tf_op jit(solution)/shard_map/ppermute | solution.py:255
  41.1 8.4 %collective-permute-start.2 = (bf16[360,128]{1,0:T(8,128)(2,1)S(1)}, bf16[360,128]{1,0:T(8,128)(2,1)S(1)}, u32[]{:S(2)}, u32[]{:S(2)}) collective-permute-start(bf16[360,128]{1,0:T(8,128)(2,1)S(1)} %get-tuple-element.34), channel_id=1, source_target_pairs={{0,32},{32,64},{64,96},{96,0},{1,33},{33,65},{65,97},{97,1},{2,34}... | collective-permute-start | bytes 276488 | tf_op jit(solution)/shard_map/ppermute | solution.py:255
  44.5 15.7 %all-to-all-start.1 = ((bf16[16,128,128]{2,1,0:T(8,128)(2,1)}), bf16[16,128,128]{2,1,0:T(8,128)(2,1)S(1)}, u32[]{:S(2)}, u32[]{:S(2)}) async-start(bf16[16,128,128]{2,1,0:T(8,128)(2,1)} %shard_map.71), calls=%async_computation.1 | async-start | bytes 1048576 | tf_op jit(solution)/shard_map/all_to_all | solution.py:327
  49.5 5.6 %collective-permute-start.5 = (bf16[360,128]{1,0:T(8,128)(2,1)S(1)}, bf16[360,128]{1,0:T(8,128)(2,1)S(1)}, u32[]{:S(2)}, u32[]{:S(2)}) collective-permute-start(bf16[360,128]{1,0:T(8,128)(2,1)S(1)} %shard_map.69.own_ref), channel_id=1, source_target_pairs={{0,96},{32,0},{64,32},{96,64},{1,97},{33,1},{65,33},{97,65},{2,98}... | collective-permute-start | bytes 276488 | tf_op jit(solution)/shard_map/ppermute | solution.py:255
  50.8 7.0 %collective-permute-start.4 = (bf16[360,128]{1,0:T(8,128)(2,1)S(1)}, bf16[360,128]{1,0:T(8,128)(2,1)S(1)}, u32[]{:S(2)}, u32[]{:S(2)}) collective-permute-start(bf16[360,128]{1,0:T(8,128)(2,1)S(1)} %shard_map.69.own_ref), channel_id=1, source_target_pairs={{0,64},{32,96},{64,0},{96,32},{1,65},{33,97},{65,1},{97,33},{2,66}... | collective-permute-start | bytes 276488 | tf_op jit(solution)/shard_map/ppermute | solution.py:255
  51.9 6.3 %collective-permute-start.3 = (bf16[360,128]{1,0:T(8,128)(2,1)S(1)}, bf16[360,128]{1,0:T(8,128)(2,1)S(1)}, u32[]{:S(2)}, u32[]{:S(2)}) collective-permute-start(bf16[360,128]{1,0:T(8,128)(2,1)S(1)} %shard_map.69.own_ref), channel_id=1, source_target_pairs={{0,32},{32,64},{64,96},{96,0},{1,33},{33,65},{65,97},{97,1},{2,34}... | collective-permute-start | bytes 276488 | tf_op jit(solution)/shard_map/ppermute | solution.py:255
